TPU v7x, 32 devices: a whole 2x2x4 slice. The times are simulated.
32 devices in a mesh: section: 4 (over x, core), dp: 8 (over z, y).
Axes of the slice: x: 2, y: 2, z: 4, core: 2. Of those that a mesh axis runs over, the one named last changes fastest.
Arguments:
- h_forward: bfloat16 [4, 8, 128, 3584], P('section', 'dp'), may hold values from -6 to 6
- h_reverse: bfloat16 [4, 8, 128, 3584], P('section', 'dp'), may hold values from -6 to 6
- weights: bfloat16 [4, 3584, 256], P('section', 'dp'), may hold values from -0.09375 to 0.09375
- gains: bfloat16 [4, 256], P('section'), may hold values from 0.25 to 1.75
Outputs:
- grad_forward: bfloat16 [4, 8, 128, 3584], P('section', 'dp')
- grad_reverse: bfloat16 [4, 8, 128, 3584], P('section', 'dp')
- grad_weights: float32 [4, 3584, 256], P('section', 'dp')
- grad_gains: float32 [4, 256], P('section')
All inputs are finite; a program needn't handle non-finite values.
Results may differ from a plain program's by a relative error of at most 0.01.
Values may be sent and summed in bfloat16 or wider, within the bound.
No kernel may reach another device: no remote copies, remote signals or barrier semaphores. Data moves between devices by JAX's collectives and lax.ppermute only.
A program may use at most 64 MiB of HBM per device.

v0:
```python
import jax
import jax.numpy as jnp
from jax import lax
from jax.sharding import PartitionSpec as P

EPS = 1e-06


def from_partner(value, axis, apart):
    mask = 2**apart
    pairs = [(source, source ^ mask) for source in range(lax.axis_size(axis))]
    return lax.ppermute(value, axis, pairs)


def passed_along(value, axis, by):
    devices = lax.axis_size(axis)
    return lax.ppermute(value, axis, [(i, (i + by) % devices) for i in range(devices)])


def group_forward(x, w, g):
    c = jnp.dot(x, w, preferred_element_type=jnp.float32)
    inv = lax.rsqrt(jnp.mean(c * c, axis=-1, keepdims=True) + EPS)
    normed = (c * inv * g.astype(jnp.float32)).astype(jnp.bfloat16)
    scale = 3.0 / c.shape[-1]
    scores = jnp.dot(normed, normed.T, preferred_element_type=jnp.float32) * scale
    count = x.shape[0]
    rows = lax.broadcasted_iota(jnp.int32, (count, count), 0)
    cols = lax.broadcasted_iota(jnp.int32, (count, count), 1)
    scores = jnp.where(cols <= rows, scores, -1e30)
    top = jnp.max(scores, axis=-1, keepdims=True)
    expo = jnp.exp(scores - top)
    probs = expo / jnp.sum(expo, axis=-1, keepdims=True)
    probs_b = probs.astype(jnp.bfloat16)
    mixed = jnp.dot(probs_b, x, preferred_element_type=jnp.float32)
    out = (x.astype(jnp.float32) + mixed).astype(jnp.bfloat16)
    return (out, (c, inv, normed, probs, probs_b))


def group_backward(x, w, g, saved, grad_out):
    c, inv, normed, probs, probs_b = saved
    scale = 3.0 / c.shape[-1]
    dx = grad_out.astype(jnp.float32) + jnp.dot(
        probs_b.T, grad_out, preferred_element_type=jnp.float32
    )
    dprobs = jnp.dot(grad_out, x.T, preferred_element_type=jnp.float32)
    dscores = probs * (dprobs - jnp.sum(dprobs * probs, axis=-1, keepdims=True))
    dscores_b = (dscores * scale).astype(jnp.bfloat16)
    dnormed = jnp.dot(dscores_b, normed, preferred_element_type=jnp.float32) + jnp.dot(
        dscores_b.T, normed, preferred_element_type=jnp.float32
    )
    dgain = jnp.sum(dnormed * c * inv, axis=0)
    dhat = dnormed * g.astype(jnp.float32)
    dc = inv * dhat - c * (inv * inv * inv) * jnp.mean(dhat * c, axis=-1, keepdims=True)
    dc_b = dc.astype(jnp.bfloat16)
    dx = dx + jnp.dot(dc_b, w.T, preferred_element_type=jnp.float32)
    dw = jnp.dot(x.T, dc_b, preferred_element_type=jnp.float32)
    return (dx, dw, dgain)


def twin_copy(pair):
    for bit in range(lax.axis_size("section").bit_length() - 1):
        pair = from_partner((pair[0], pair[1]), "section", bit)
    return (pair[0], pair[1])


def grad_twin(pair):
    for bit in range(lax.axis_size("section").bit_length() - 1):
        pair = (
            from_partner(pair[0].astype(jnp.bfloat16), "section", bit).astype(jnp.float32),
            from_partner(pair[1].astype(jnp.bfloat16), "section", bit).astype(jnp.float32),
        )
    return (pair[0], pair[1])


def neighbour(values, offset):
    return passed_along(values, "section", offset)


def on_device(h_forward, h_reverse, weights, gains):
    shard = weights[0]
    gain = gains[0]
    twin_shard, twin_gain = twin_copy((shard, gain))
    own, twin = (
        lax.all_gather(shard, "dp", axis=0, tiled=True),
        lax.all_gather(twin_shard, "dp", axis=0, tiled=True),
    )
    x_fwd = h_forward[0, 0]
    x_rev = h_reverse[0, 0]
    u_fwd, saved_f1 = group_forward(x_fwd, own, gain)
    u_rev, saved_r1 = group_forward(x_rev, twin, twin_gain)
    in_fwd = neighbour(u_fwd, 1)
    in_rev = neighbour(u_rev, -1)
    v_fwd, saved_f2 = group_forward(in_fwd, own, gain)
    v_rev, saved_r2 = group_forward(in_rev, twin, twin_gain)
    din_fwd, dw_f2, dg_f2 = group_backward(in_fwd, own, gain, saved_f2, v_fwd)
    din_rev, dw_r2, dg_r2 = group_backward(in_rev, twin, twin_gain, saved_r2, v_rev)
    back_fwd = neighbour(din_fwd.astype(jnp.bfloat16), -1)
    back_rev = neighbour(din_rev.astype(jnp.bfloat16), 1)
    dh_fwd, dw_f1, dg_f1 = group_backward(x_fwd, own, gain, saved_f1, back_fwd)
    dh_rev, dw_r1, dg_r1 = group_backward(x_rev, twin, twin_gain, saved_r1, back_rev)
    share_fwd, share_rev = (
        lax.psum_scatter(
            (dw_f1 + dw_f2).astype(jnp.bfloat16), "dp", scatter_dimension=0, tiled=True
        ).astype(jnp.float32),
        lax.psum_scatter(
            (dw_r1 + dw_r2).astype(jnp.bfloat16), "dp", scatter_dimension=0, tiled=True
        ).astype(jnp.float32),
    )
    gsum_fwd, gsum_rev = lax.psum((dg_f1 + dg_f2, dg_r1 + dg_r2), "dp")
    mirror_w, mirror_g = grad_twin((share_rev, gsum_rev))
    grad_weights = (share_fwd + mirror_w)[None]
    grad_gains = (gsum_fwd + mirror_g)[None]
    return (
        dh_fwd.astype(jnp.bfloat16)[None, None],
        dh_rev.astype(jnp.bfloat16)[None, None],
        grad_weights,
        grad_gains,
    )


def solution(mesh):
    in_specs = (
        P("section", "dp", None, None),
        P("section", "dp", None, None),
        P("section", "dp", None),
        P("section", None),
    )
    out_specs = (
        P("section", "dp", None, None),
        P("section", "dp", None, None),
        P("section", "dp", None),
        P("section", None),
    )
    return jax.shard_map(
        on_device, mesh=mesh, in_specs=in_specs, out_specs=out_specs, check_vma=False
    )
```

profile of v0, /device:TPU:0, one launch (start us, length us, event | category | flops | bytes accessed | tf_op | source)
XLA Modules:
  0.0 288.2 jit_solution(1580039817160999895)
XLA Ops:
  7.2 0.7 all-gather.6.cloned.1.call-update
  8.0 0.5 collective-permute-start.2
  8.5 1.3 collective-permute-done.2
  9.8 2.9 collective-permute-start.3
  12.7 5.9 %collective-permute-done.3 = bf16[448,256]{1,0:T(8,128)(2,1)S(1)} collective-permute-done((bf16[448,256]{1,0:T(8,128)(2,1)S(1)}, bf16[448,256]{1,0:T(8,128)(2,1)S(1)}, u32[]{:S(2)}, u32[]{:S(2)}) %collective-permute-start.3) | collective-permute-done | bytes 229408 | tf_op jit(solution)/shard_map/ppermute | solution.py:12
  18.6 0.7 copy-done.12
  19.3 0.7 reduce
  20.1 1.1 collective-permute-done.4
  21.2 1.7 collective-permute-start.5
  22.9 1.8 collective-permute-done.5
  24.7 34.4 %all-gather.6.cloned.1.call-done = bf16[1,3584,256]{2,1,0:T(8,128)(2,1)} async-done(((bf16[1,448,256]{2,1,0:T(8,128)(2,1)}), bf16[1,3584,256]{2,1,0:T(8,128)(2,1)}) %all-gather.6.cloned.1.call-update) | async-done | bytes 1835024 | tf_op jit(solution)/shard_map/all_gather | solution.py:84
  59.2 2.3 multiply_reduce_fusion.11
  61.8 1.4 fusion.2
  63.1 44.1 %all-gather.4.cloned.1.call-done = bf16[3584,256]{1,0:T(8,128)(2,1)} async-done(((bf16[448,256]{1,0:T(8,128)(2,1)}), bf16[3584,256]{1,0:T(8,128)(2,1)}) %all-gather.4.cloned.1.call-update) | async-done | bytes 1835024 | tf_op jit(solution)/shard_map/all_gather | solution.py:85
  107.2 2.3 multiply_reduce_fusion.7
  109.9 0.4 fusion.3
  110.4 0.5 multiply_reduce_fusion.10
  111.3 0.4 add_convert_fusion.3
  111.7 0.4 multiply_reduce_fusion.15
  112.2 9.2 %collective-permute-done.6 = bf16[128,3584]{1,0:T(8,128)(2,1)S(1)} collective-permute-done((bf16[128,3584]{1,0:T(8,128)(2,1)S(1)}, bf16[128,3584]{1,0:T(8,128)(2,1)S(1)}, u32[]{:S(2)}, u32[]{:S(2)}) %collective-permute-start.6) | collective-permute-done | bytes 917536 | tf_op jit(solution)/shard_map/ppermute | solution.py:17
  121.3 0.5 multiply_reduce_fusion.6
  122.2 0.4 add_convert_fusion
  123.0 0.4 multiply_reduce_fusion.13
  124.1 0.7 fusion.4
  124.9 1.8 collective-permute-start.7
  127.3 10.5 %collective-permute-done.7 = bf16[128,3584]{1,0:T(8,128)(2,1)S(1)} collective-permute-done((bf16[128,3584]{1,0:T(8,128)(2,1)S(1)}, bf16[128,3584]{1,0:T(8,128)(2,1)S(1)}, u32[]{:S(2)}, u32[]{:S(2)}) %collective-permute-start.7) | collective-permute-done | bytes 917536 | tf_op jit(solution)/shard_map/ppermute | solution.py:17
  139.0 0.7 convolution_bitcast_fusion
  139.7 1.9 fusion.1
  141.6 3.8 %copy.18 = bf16[3584,256]{1,0:T(8,128)(2,1)} copy(bf16[3584,256]{0,1:T(8,128)(2,1)} %fusion.1) | data formatting | bytes 3670016
  145.5 0.7 fusion.9
  146.2 0.4 copy-done.9
  147.1 10.9 %collective-permute-done.1 = bf16[128,3584]{1,0:T(8,128)(2,1)S(1)} collective-permute-done((bf16[128,3584]{1,0:T(8,128)(2,1)S(1)}, bf16[128,3584]{1,0:T(8,128)(2,1)S(1)}, u32[]{:S(2)}, u32[]{:S(2)}) %collective-permute-start.1) | collective-permute-done | bytes 917536 | tf_op jit(solution)/shard_map/ppermute | solution.py:17
  159.2 0.7 convolution_bitcast_fusion.1
  159.8 2.0 fusion
  161.8 3.8 %copy.16 = bf16[3584,256]{1,0:T(8,128)(2,1)} copy(bf16[3584,256]{0,1:T(8,128)(2,1)} %fusion) | data formatting | bytes 3670016
  165.7 0.7 fusion.7
  166.4 0.5 copy-done.11
  166.9 1.3 fusion.19
  168.2 20.6 %all-reduce = (f32[256]{0:T(256)S(1)}, bf16[256]{0:T(256)(128)(2,1)S(1)}) all-reduce(f32[256]{0:T(256)S(1)} %add.141, f32[256]{0:T(256)S(1)} %add.142), channel_id=1, replica_groups=mesh['section'=4,'dp'=8] {'dp'}, use_global_device_ids=true, to_apply=%region_24.25 | all-reduce | flops 512 | bytes 3584 | tf_op jit(solution)/shard_map/psum | solution.py:109
  188.8 21.9 %reduce-scatter.9.cloned.1.call-done = bf16[448,256]{1,0:T(8,128)(2,1)} async-done(((bf16[3584,256]{1,0:T(8,128)(2,1)}), bf16[448,256]{1,0:T(8,128)(2,1)}) %reduce-scatter.9.cloned.1.call-update) | async-done | bytes 229392
  210.7 1.1 copy.19
  212.2 1.5 collective-permute-start.11
  213.8 1.0 collective-permute-start.9
  214.8 1.7 fusion.6
  216.5 0.6 convert_add_fusion
  217.1 62.4 %reduce-scatter.7.cloned.1.call-done = bf16[448,256]{1,0:T(8,128)(2,1)} async-done(((bf16[3584,256]{1,0:T(8,128)(2,1)}), bf16[448,256]{1,0:T(8,128)(2,1)}) %reduce-scatter.7.cloned.1.call-update) | async-done | bytes 229392
  279.5 1.1 copy.17
  280.7 1.0 copy.13
  (83 shorter events, 6.7 us)
Async XLA Ops:
  7.2 54.6 %copy-start.4 = (bf16[1,1,128,3584]{3,2,1,0:T(8,128)(2,1)S(1)}, bf16[1,1,128,3584]{3,2,1,0:T(8,128)(2,1)}, u32[]{:S(2)}) copy-start(bf16[1,1,128,3584]{3,2,1,0:T(8,128)(2,1)} %param.4) | copy-start | bytes 2752516
  7.2 52.0 %all-gather.6.cloned.1.call-start = ((), (), s32[]{:S(2)}) async-start(), calls=%async_computation.3 | async-start | bytes 2064384 | tf_op jit(solution)/shard_map/all_gather | solution.py:84
  7.9 99.3 %all-gather.4.cloned.1.call-start = ((), (), s32[]{:S(2)}) async-start(), calls=%async_computation.2 | async-start | bytes 2064384 | tf_op jit(solution)/shard_map/all_gather | solution.py:85
  8.0 1.8 collective-permute-start.2
  9.8 8.8 %collective-permute-start.3 = (bf16[448,256]{1,0:T(8,128)(2,1)S(1)}, bf16[448,256]{1,0:T(8,128)(2,1)S(1)}, u32[]{:S(2)}, u32[]{:S(2)}) collective-permute-start(bf16[448,256]{1,0:T(8,128)(2,1)S(1)} %collective-permute-done.2), channel_id=1, source_target_pairs={{0,16},{8,24},{16,0},{24,8},{1,17},{9,25},{17,1},{25,9},{2,18},{10... | collective-permute-start | bytes 688136 | tf_op jit(solution)/shard_map/ppermute | solution.py:12
  18.6 0.7 copy-start.12
  19.3 191.4 %reduce-scatter.9.cloned.1.call-start = ((), (), s32[]{:S(2)}) async-start(), calls=%async_computation.5 | async-start | bytes 2064384
  20.0 1.2 collective-permute-start.4
  21.2 3.5 %collective-permute-start.5 = (bf16[256]{0:T(256)(128)(2,1)S(1)}, bf16[256]{0:T(256)(128)(2,1)S(1)}, u32[]{:S(2)}, u32[]{:S(2)}) collective-permute-start(bf16[256]{0:T(256)(128)(2,1)S(1)} %collective-permute-done.4), channel_id=1, source_target_pairs={{0,16},{8,24},{16,0},{24,8},{1,17},{9,25},{17,1},{25,9},{2,18},{10... | collective-permute-start | bytes 1544 | tf_op jit(solution)/shard_map/ppermute | solution.py:12
  63.1 47.3 %copy-start = (bf16[1,3584,256]{2,1,0:T(8,128)(2,1)S(1)}, bf16[1,3584,256]{2,1,0:T(8,128)(2,1)}, u32[]{:S(2)}) copy-start(bf16[1,3584,256]{2,1,0:T(8,128)(2,1)} %all-gather.6.cloned.1.call-done) | copy-start | bytes 5505028
  63.1 47.3 %collective-permute-start = (bf16[128,3584]{1,0:T(8,128)(2,1)}, bf16[128,3584]{1,0:T(8,128)(2,1)S(1)}, u32[]{:S(2)}, u32[]{:S(2)}) collective-permute-start(bf16[128,3584]{1,0:T(8,128)(2,1)} %fusion.2), channel_id=1, source_target_pairs={{0,8},{8,16},{16,24},{24,0},{1,9},{9,17},{17,25},{25,1},{2,10},{10... | collective-permute-start | bytes 2752520 | tf_op jit(solution)/shard_map/ppermute | solution.py:17
  107.2 2.7 copy-start.3
  110.4 11.0 %collective-permute-start.6 = (bf16[128,3584]{1,0:T(8,128)(2,1)S(1)}, bf16[128,3584]{1,0:T(8,128)(2,1)S(1)}, u32[]{:S(2)}, u32[]{:S(2)}) collective-permute-start(bf16[128,3584]{1,0:T(8,128)(2,1)S(1)} %fusion.3), channel_id=1, source_target_pairs={{0,24},{8,0},{16,8},{24,16},{1,25},{9,1},{17,9},{25,17},{2,26},{10... | collective-permute-start | bytes 2752520 | tf_op jit(solution)/shard_map/ppermute | solution.py:17
  111.3 10.1 %copy-start.1 = (bf16[3584,256]{1,0:T(8,128)(2,1)S(1)}, bf16[3584,256]{1,0:T(8,128)(2,1)}, u32[]{:S(2)}) copy-start(bf16[3584,256]{1,0:T(8,128)(2,1)} %all-gather.4.cloned.1.call-done) | copy-start | bytes 5505028
  111.7 10.1 %copy-start.8 = (bf16[128,3584]{1,0:T(8,128)(2,1)}, bf16[128,3584]{1,0:T(8,128)(2,1)S(1)}, u32[]{:S(2)}) copy-start(bf16[128,3584]{1,0:T(8,128)(2,1)S(1)} %add_convert_fusion.3) | copy-start | bytes 2752516
  124.9 13.0 %collective-permute-start.7 = (bf16[128,3584]{1,0:T(8,128)(2,1)S(1)}, bf16[128,3584]{1,0:T(8,128)(2,1)S(1)}, u32[]{:S(2)}, u32[]{:S(2)}) collective-permute-start(bf16[128,3584]{1,0:T(8,128)(2,1)S(1)} %fusion.4), channel_id=1, source_target_pairs={{0,8},{8,16},{16,24},{24,0},{1,9},{9,17},{17,25},{25,1},{2,10},{10... | collective-permute-start | bytes 2752520 | tf_op jit(solution)/shard_map/ppermute | solution.py:17
  137.9 1.0 copy-start.6
  145.4 134.1 %reduce-scatter.7.cloned.1.call-start = ((), (), s32[]{:S(2)}) async-start(), calls=%async_computation.4 | async-start | bytes 2064384
  145.5 1.2 copy-start.9
  146.7 11.4 %copy-start.5 = (bf16[1,1,128,3584]{3,2,1,0:T(8,128)(2,1)S(1)}, bf16[1,1,128,3584]{3,2,1,0:T(8,128)(2,1)}, u32[]{:S(2)}) copy-start(bf16[1,1,128,3584]{3,2,1,0:T(8,128)(2,1)} %param.4) | copy-start | bytes 2752516
  147.1 11.0 %collective-permute-start.1 = (bf16[128,3584]{1,0:T(8,128)(2,1)S(1)}, bf16[128,3584]{1,0:T(8,128)(2,1)S(1)}, u32[]{:S(2)}, u32[]{:S(2)}) collective-permute-start(bf16[128,3584]{1,0:T(8,128)(2,1)S(1)} %add_convert_fusion.2), channel_id=1, source_target_pairs={{0,24},{8,0},{16,8},{24,16},{1,25},{9,1},{17,9},{25,17},{2,26},{10... | collective-permute-start | bytes 2752520 | tf_op jit(solution)/shard_map/ppermute | solution.py:17
  158.0 1.0 copy-start.10
  165.7 1.2 copy-start.11
  166.9 45.0 %copy-start.7 = (bf16[128,3584]{1,0:T(8,128)(2,1)S(1)}, bf16[128,3584]{1,0:T(8,128)(2,1)}, u32[]{:S(2)}) copy-start(bf16[128,3584]{1,0:T(8,128)(2,1)} %copy-done.6) | copy-start | bytes 2752516
  168.2 46.7 %copy-start.2 = (bf16[3584,256]{1,0:T(8,128)(2,1)S(1)}, bf16[3584,256]{1,0:T(8,128)(2,1)}, u32[]{:S(2)}) copy-start(bf16[3584,256]{1,0:T(8,128)(2,1)} %all-gather.4.cloned.1.call-done) | copy-start | bytes 5505028
  188.8 23.5 %collective-permute-start.10 = (bf16[256]{0:T(256)(128)(2,1)S(1)}, bf16[256]{0:T(256)(128)(2,1)S(1)}, u32[]{:S(2)}, u32[]{:S(2)}) collective-permute-start(bf16[256]{0:T(256)(128)(2,1)S(1)} %get-tuple-element.21), channel_id=1, source_target_pairs={{0,8},{8,0},{16,24},{24,16},{1,9},{9,1},{17,25},{25,17},{2,10},{10... | collective-permute-start | bytes 1544 | tf_op jit(solution)/shard_map/ppermute | solution.py:12
  211.8 2.0 collective-permute-start.8
  212.2 4.3 %collective-permute-start.11 = (bf16[256]{0:T(256)(128)(2,1)S(1)}, bf16[256]{0:T(256)(128)(2,1)S(1)}, u32[]{:S(2)}, u32[]{:S(2)}) collective-permute-start(bf16[256]{0:T(256)(128)(2,1)S(1)} %collective-permute-done.10), channel_id=1, source_target_pairs={{0,16},{8,24},{16,0},{24,8},{1,17},{9,25},{17,1},{25,9},{2,18},{10... | collective-permute-start | bytes 1544 | tf_op jit(solution)/shard_map/ppermute | solution.py:12
  213.8 66.8 %collective-permute-start.9 = (bf16[448,256]{0,1:T(8,128)(2,1)S(1)}, bf16[448,256]{0,1:T(8,128)(2,1)S(1)}, u32[]{:S(2)}, u32[]{:S(2)}) collective-permute-start(bf16[448,256]{0,1:T(8,128)(2,1)S(1)} %collective-permute-done.8), channel_id=1, source_target_pairs={{0,16},{8,24},{16,0},{24,8},{1,17},{9,25},{17,1},{25,9},{2,18},{10... | collective-permute-start | bytes 688136 | tf_op jit(solution)/shard_map/ppermute | solution.py:12
Sparse Core Ops, SparseCore 0:
  10.2 48.9 all-gather.5
  61.9 45.2 all-gather.3
  145.6 65.0 reduce-scatter.8
  214.4 65.0 reduce-scatter.6
where the time goes:
time: 289 us; the launch traced here: 288 us
  waiting for transfers between devices  204 us (71%)
  matrix products  24.7 us (9%)
  blocking collectives  20.6 us (7%)
  between operations  14.1 us (5%)
  local copies, waits for them, and re-layouts  12.3 us (4%)
  starting transfers between devices  9.96 us (3%)
    unnamed x6, waiting for transfers between devices  85 us
    all_gather x1, waiting for transfers between devices, on_device(): lax.all_gather(twin_shard, 'dp', axis=0, tiled=True)  44.1 us
    all_gather x1, waiting for transfers between devices, on_device(): lax.all_gather(shard, 'dp', axis=0, tiled=True)  34.4 us
    ppermute x4, waiting for transfers between devices, passed_along(): lax.ppermute(value, axis, [(i, (i + by) % devices) for i in range(devices)])  30.6 us
    psum x1, blocking collectives, on_device(): gsum_fwd, gsum_rev = lax.psum((dg_f1 + dg_f2, dg_r1 + dg_r2), 'dp')  20.6 us
    unnamed x31, local copies, waits for them, and re-layouts  12.3 us
    ppermute x8, waiting for transfers between devices, from_partner(): return lax.ppermute(value, axis, pairs)  10.1 us
    ppermute x8, starting transfers between devices, from_partner(): return lax.ppermute(value, axis, pairs)  7.89 us
  transfers between devices with their start and end apart: 16, of which 11 were waited for; matrix products, arithmetic and copies ran while one was open for 9% of the time, Pallas kernels for 0%

commit v1 on v0

--- a/solution.py
+++ b/solution.py
@@ -1,9 +1,278 @@
+import functools
+
 import jax
 import jax.numpy as jnp
 from jax import lax
+from jax.experimental import pallas as pl
+from jax.experimental.pallas import tpu as pltpu
 from jax.sharding import PartitionSpec as P
 
 EPS = 1e-06
+AXES = ("section", "dp")
+BF16 = jnp.bfloat16
+F32 = jnp.float32
+CHUNK = 512
+VMEM_LIMIT = 40 * 1024 * 1024
+
+
+def matmul(a, b):
+    return jnp.dot(a, b, preferred_element_type=F32)
+
+
+def matmul_nt(a, b):
+    return lax.dot_general(a, b, (((1,), (1,)), ((), ())), preferred_element_type=F32)
+
+
+def matmul_tn(a, b):
+    return lax.dot_general(a, b, (((0,), (0,)), ((), ())), preferred_element_type=F32)
+
+
+def latent_norm(c, g):
+    inv = lax.rsqrt(jnp.mean(c * c, axis=-1, keepdims=True) + EPS)
+    return inv, (c * inv * g.astype(F32)).astype(BF16)
+
+
+def attention(normed, width):
+    scores = matmul_nt(normed, normed) * (3.0 / width)
+    rows = lax.broadcasted_iota(jnp.int32, scores.shape, 0)
+    cols = lax.broadcasted_iota(jnp.int32, scores.shape, 1)
+    scores = jnp.where(cols <= rows, scores, -1e30)
+    expo = jnp.exp(scores - jnp.max(scores, axis=-1, keepdims=True))
+    return expo / jnp.sum(expo, axis=-1, keepdims=True)
+
+
+def column_chunks(width):
+    return [slice(at, at + CHUNK) for at in range(0, width, CHUNK)]
+
+
+def mix_into(out_ref, x_ref, probs_b):
+    for cols in column_chunks(x_ref.shape[-1]):
+        x = x_ref[:, cols]
+        out_ref[:, cols] = (x.astype(F32) + matmul(probs_b, x)).astype(BF16)
+
+
+def score_grad(dy_ref, x_ref):
+    total = None
+    for cols in column_chunks(x_ref.shape[-1]):
+        part = matmul_nt(dy_ref[:, cols], x_ref[:, cols])
+        total = part if total is None else total + part
+    return total
+
+
+def latent_grad(dprobs, probs, c, inv, normed, g):
+    scale = 3.0 / c.shape[-1]
+    dscores = probs * (dprobs - jnp.sum(dprobs * probs, axis=-1, keepdims=True))
+    dscores_b = (dscores * scale).astype(BF16)
+    dnormed = matmul(dscores_b, normed) + matmul_tn(dscores_b, normed)
+    dgain = jnp.sum(dnormed * c * inv, axis=0, keepdims=True)
+    dhat = dnormed * g.astype(F32)
+    dc = inv * dhat - c * (inv * inv * inv) * jnp.mean(dhat * c, axis=-1, keepdims=True)
+    return dc.astype(BF16), dgain
+
+
+def input_grad(out_ref, dy_ref, probs_b, dc_b, w_ref):
+    for cols in column_chunks(dy_ref.shape[-1]):
+        dy = dy_ref[:, cols]
+        dx = dy.astype(F32) + matmul_tn(probs_b, dy) + matmul_nt(dc_b, w_ref[cols, :])
+        out_ref[:, cols] = dx.astype(BF16)
+
+
+def ring_place(value):
+    return value ^ (value >> 1)
+
+
+def shard_row(dy, steps, rows):
+    dp = lax.axis_index("dp")
+    place = (ring_place(dp >> 1) + steps) & 3
+    return pl.multiple_of((ring_place(place) * 2 + ((dp & 1) ^ dy)) * rows, 16)
+
+
+def copies(pairs, sems):
+    return [pltpu.make_async_copy(a, b, sems.at[i]) for i, (a, b) in enumerate(pairs)]
+
+
+def first_kernel(*refs):
+    pieces, (gain_ref, hf_ref, hr_ref, u_ref, w_ref, c_ref, p_ref, sems) = refs[:16], refs[16:]
+    rows = pieces[0].shape[0]
+    pairs = []
+    for dx in range(2):
+        for dy in range(2):
+            for k in range(4):
+                at = shard_row(dy, 4 - k, rows)
+                pairs.append((pieces[len(pairs)], w_ref.at[dx, pl.ds(at, rows), :]))
+    moves = copies(pairs, sems)
+    for move in moves:
+        move.start()
+    odd = lax.axis_index("section") & 1
+    for slot, x_ref in enumerate((hf_ref, hr_ref)):
+        for move in moves[8 * slot : 8 * slot + 8]:
+            move.wait()
+        g = gain_ref[slot : slot + 1, :]
+        c = matmul(x_ref[...], w_ref[slot])
+        _, normed = latent_norm(c, g)
+        probs = attention(normed, c.shape[-1])
+        c_ref[slot] = c
+        p_ref[slot] = probs
+        mix_into(u_ref.at[slot ^ odd], x_ref, probs.astype(BF16))
+
+
+def second_kernel(gain_ref, x_ref, w_ref, e_ref, dc_ref, dg_ref, v_ref):
+    even = 1 - (lax.axis_index("section") & 1)
+    for slot in range(2):
+        g = gain_ref[slot : slot + 1, :]
+        x = x_ref.at[slot]
+        c = matmul(x[...], w_ref[slot])
+        inv, normed = latent_norm(c, g)
+        probs = attention(normed, c.shape[-1])
+        probs_b = probs.astype(BF16)
+        mix_into(v_ref, x, probs_b)
+        dc_b, dgain = latent_grad(score_grad(v_ref, x), probs, c, inv, normed, g)
+        dc_ref[slot] = dc_b
+        dg_ref[slot : slot + 1, :] = dgain
+        input_grad(e_ref.at[slot ^ even], v_ref, probs_b, dc_b, w_ref.at[slot])
+
+
+def third_kernel(*refs):
+    ins, outs = refs[:11], refs[11:]
+    gain_ref, hf_ref, hr_ref, w_ref, c_ref, p_ref, cot_ref, x2_ref, dc2_ref, dg2_ref, _ = ins
+    gf_ref, gr_ref, dg_ref = outs[:3]
+    pieces, (dw_ref, sems) = outs[3:19], outs[19:]
+    rows = pieces[0].shape[0]
+    pairs = []
+    for dx in range(2):
+        for dy in range(2):
+            for k in range(4):
+                at = shard_row(dy, k, rows)
+                pairs.append((dw_ref.at[dx, pl.ds(at, rows), :], pieces[len(pairs)]))
+    moves = copies(pairs, sems)
+    for slot, x_ref, out_ref in ((1, hr_ref, gr_ref), (0, hf_ref, gf_ref)):
+        g = gain_ref[slot : slot + 1, :]
+        c = c_ref[slot]
+        probs = p_ref[slot]
+        inv, normed = latent_norm(c, g)
+        cot = cot_ref.at[slot]
+        dc_b, dgain = latent_grad(score_grad(cot, x_ref), probs, c, inv, normed, g)
+        dg_ref[slot : slot + 1, :] = dgain + dg2_ref[slot : slot + 1, :]
+        for cols in column_chunks(x_ref.shape[-1]):
+            dw = matmul_tn(x_ref[:, cols], dc_b) + matmul_tn(x2_ref[slot, :, cols], dc2_ref[slot])
+            dw_ref[slot, cols, :] = dw.astype(BF16)
+        for move in moves[8 * slot : 8 * slot + 8]:
+            move.start()
+        input_grad(out_ref, cot, probs.astype(BF16), dc_b, w_ref.at[slot])
+    for move in moves:
+        move.wait()
+
+
+def kernel_call(body, n_any, n_vmem, outs, out_any, scratch, flops):
+    anywhere, local = pl.BlockSpec(memory_space=pl.ANY), pl.BlockSpec(memory_space=pltpu.VMEM)
+    return pl.pallas_call(
+        body,
+        out_shape=outs,
+        in_specs=[anywhere] * n_any + [local] * n_vmem,
+        out_specs=[local] * (len(outs) - out_any) + [anywhere] * out_any,
+        scratch_shapes=scratch,
+        compiler_params=pltpu.CompilerParams(vmem_limit_bytes=VMEM_LIMIT),
+        cost_estimate=pl.CostEstimate(flops=flops, bytes_accessed=8 << 20, transcendentals=0),
+    )
+
+
+def moves_between():
+    def pairs(change):
+        found = []
+        for i in range(32):
+            s, d = divmod(i, 8)
+            to_s, to_d = change(s, d)
+            found.append((i, to_s * 8 + to_d))
+        return found
+
+    following = {0: 1, 1: 3, 3: 2, 2: 0}
+    changes = (
+        lambda s, d: (s ^ 1, d),
+        lambda s, d: (s ^ 2, d),
+        lambda s, d: (s, d ^ 1),
+        lambda s, d: (s, following[d >> 1] * 2 + (d & 1)),
+        lambda s, d: (s, d ^ 2),
+        lambda s, d: (s, d ^ 4),
+    )
+    return [functools.partial(lambda v, p: lax.ppermute(v, AXES, p), p=pairs(c)) for c in changes]
+
+
+def after(value, *others):
+    return lax.optimization_barrier((value, *others))[0]
+
+
+def gather(shard, over_x, over_y, along_z):
+    own, x, y, xy = [shard] + [None] * 3, [None] * 4, [None] * 4, [None] * 4
+    x[0], y[0], own[1] = over_x(own[0]), over_y(own[0]), along_z(own[0])
+    own[1] = after(own[1], x[0], y[0])
+    xy[0], y[1], own[2] = over_x(y[0]), over_y(own[1]), along_z(own[1])
+    x[1], y[2], own[3] = over_x(own[1]), over_y(own[2]), along_z(own[2])
+    own[3] = after(own[3], xy[0], y[1])
+    x[3], y[3], xy[1] = over_x(own[3]), over_y(own[3]), along_z(xy[0])
+    x[2] = over_x(after(own[2], x[1]))
+    xy[3], xy[2] = over_y(x[3]), along_z(xy[1])
+    return own + y + x + xy
+
+
+def add(*values):
+    return sum(v.astype(F32) for v in values)
+
+
+def scatter(parts, over_x, over_y, along_z):
+    own, y, x, xy = parts[:4], parts[4:8], parts[8:12], parts[12:]
+
+    def total(*values):
+        return add(*values).astype(BF16)
+
+    e1 = total(xy[1], along_z(xy[2]))
+    c3 = total(x[3], over_y(xy[3]))
+    s3 = total(own[3], over_x(c3), over_y(y[3]))
+    e0 = total(xy[0], along_z(e1))
+    s2 = total(own[2], over_x(x[2]), over_y(y[2]), along_z(s3))
+    b0 = total(y[0], over_x(e0))
+    s1 = total(own[1], over_x(x[1]), over_y(y[1]), along_z(s2))
+    return add(own[0], over_x(x[0]), over_y(b0), along_z(s1))
+
+
+def on_chip_relay(h_forward, h_reverse, weights, gains):
+    other_core, over_x, over_y, along_z, z_near, z_far = moves_between()
+    tokens, width = h_forward.shape[2:]
+    rows, latent = weights.shape[1:]
+    shard, gain = weights[0], gains
+    x_fwd, x_rev = h_forward[0, 0], other_core(h_reverse[0, 0])
+    both_gains = jnp.concatenate([gain, over_x(gain)], axis=0)
+    shards = gather(shard, over_x, over_y, along_z)
+    pair = jax.ShapeDtypeStruct((2, tokens, width), BF16)
+    whole = jax.ShapeDtypeStruct((2, width, latent), BF16)
+    saved_c = jax.ShapeDtypeStruct((2, tokens, latent), F32)
+    saved_p = jax.ShapeDtypeStruct((2, tokens, tokens), F32)
+    dgains = jax.ShapeDtypeStruct((2, latent), F32)
+    dcs = jax.ShapeDtypeStruct((2, tokens, latent), BF16)
+    one = jax.ShapeDtypeStruct((tokens, width), BF16)
+    product = 2 * tokens * width * latent
+    u, w, c1, p1 = kernel_call(
+        first_kernel, 16, 3, [pair, whole, saved_c, saved_p], 0,
+        [pltpu.SemaphoreType.DMA((16,))], 3 * product,
+    )(*shards, both_gains, x_fwd, x_rev)
+    x2 = other_core(u)
+    e, dc2, dg2 = kernel_call(
+        second_kernel, 0, 3, [pair, dcs, dgains], 0,
+        [pltpu.VMEM((tokens, width), BF16)], 7 * product,
+    )(both_gains, x2, w)
+    cot = other_core(e)
+    piece = jax.ShapeDtypeStruct((rows, latent), BF16)
+    out = kernel_call(
+        third_kernel, 0, 11, [one, one, dgains] + [piece] * 16, 16,
+        [pltpu.VMEM((2, width, latent), BF16), pltpu.SemaphoreType.DMA((16,))], 8 * product,
+    )(both_gains, x_fwd, x_rev, w, c1, p1, cot, x2, dc2, dg2, both_gains)
+    grad_fwd, grad_rev, dgain = out[:3]
+    grad_rev = other_core(grad_rev)
+    grad_weights = scatter(out[3:], over_x, over_y, along_z)
+    dgain = dgain[:1] + over_x(dgain[1:])
+    dgain = dgain + over_y(dgain)
+    dgain = dgain + z_near(dgain)
+    dgain = dgain + z_far(dgain)
+    return grad_fwd[None, None], grad_rev[None, None], grad_weights[None], dgain
 
 
 def from_partner(value, axis, apart):
@@ -76,7 +345,7 @@
     return passed_along(values, "section", offset)
 
 
-def on_device(h_forward, h_reverse, weights, gains):
+def sections_apart(h_forward, h_reverse, weights, gains):
     shard = weights[0]
     gain = gains[0]
     twin_shard, twin_gain = twin_copy((shard, gain))
@@ -131,6 +400,8 @@
         P("section", "dp", None),
         P("section", None),
     )
+    on_chip = (mesh.shape["section"], mesh.shape["dp"]) == (4, 8)
+    on_device = on_chip_relay if on_chip else sections_apart
     return jax.shard_map(
         on_device, mesh=mesh, in_specs=in_specs, out_specs=out_specs, check_vma=False
     )

time: 289 us -> 162 us (0.56)
  waiting for transfers between devices: 204 us -> 76.5 us
  starting transfers between devices: 9.96 us -> 51.3 us
  Pallas kernels: 0 us -> 27.4 us
  matrix products: 24.7 us -> 0 us
  blocking collectives: 20.6 us -> 0 us
  between operations: 14.1 us -> 0.75 us
  local copies, waits for them, and re-layouts: 12.3 us -> 3.05 us
    unnamed x6 -> x0, waiting for transfers between devices: 85 us -> none
    all_gather x2 -> x0, waiting for transfers between devices: 78.5 us -> none  [the longest x1 44.1 us: on_device(): lax.all_gather(twin_shard, 'dp', axis=0, tiled=True)]
    ppermute x12 -> x39, starting transfers between devices: 9.8 us -> 51.3 us  [moves_between(): lax.ppermute(v, AXES, p)]
    ppermute x12 -> x39, waiting for transfers between devices: 40.8 us -> 76.5 us  [moves_between(): lax.ppermute(v, AXES, p)]
    pallas_call x0 -> x3, Pallas kernels: none -> 27.4 us  [the longest x1 12.6 us: on_chip_relay(): kernel_call(third_kernel, 0, 11, [one, one, dgains] + [piece] * 16, 16, [...]
    dot_general x36 -> x0, matrix products: 24.7 us -> none  [the longest x4 5.6 us: group_forward(): c = jnp.dot(x, w, preferred_element_type=jnp.float32)]
    psum x1 -> x0, blocking collectives: 20.6 us -> none  [on_device(): gsum_fwd, gsum_rev = lax.psum((dg_f1 + dg_f2, dg_r1 + dg_r2), 'dp')]
    unnamed x31 -> x7, local copies, waits for them, and re-layouts: 12.3 us -> 3.04 us
  transfers between devices with their start and end apart: 16 -> 39, of which waited for: 11 -> 25; matrix products, arithmetic and copies ran while one was open for 9% -> 1% of each run, Pallas kernels for 0% -> 0%
where the time goes in v1:
time: 162 us
  waiting for transfers between devices  76.5 us (47%)
  starting transfers between devices  51.3 us (32%)
  Pallas kernels  27.4 us (17%)
  local copies, waits for them, and re-layouts  3.05 us (2%)
  other arithmetic  2.73 us (2%)
    ppermute x39, waiting for transfers between devices, moves_between(): lax.ppermute(v, AXES, p)  76.5 us
    ppermute x39, starting transfers between devices, moves_between(): lax.ppermute(v, AXES, p)  51.3 us
    pallas_call x1, Pallas kernels, on_chip_relay(): kernel_call(third_kernel, 0, 11, [one, one, dgains] + [piece] * 16, 16, [...  12.6 us
    pallas_call x1, Pallas kernels, on_chip_relay(): kernel_call(first_kernel, 16, 3, [pair, whole, saved_c, saved_p], 0, [plt...  8.59 us
    pallas_call x1, Pallas kernels, on_chip_relay(): kernel_call(second_kernel, 0, 3, [pair, dcs, dgains], 0, [pltpu.VMEM((tok...  6.28 us
  transfers between devices with their start and end apart: 39, of which 25 were waited for; matrix products, arithmetic and copies ran while one was open for 1% of the time, Pallas kernels for 0%

profile of v1, /device:TPU:0, one launch (start us, length us, event | category | flops | bytes accessed | tf_op | source)
XLA Modules:
  0.0 161.7 jit_solution(195161883672720852)
XLA Ops:
  0.6 3.0 %collective-permute-start.4 = (bf16[448,256]{1,0:T(8,128)(2,1)}, bf16[448,256]{1,0:T(8,128)(2,1)S(1)}, u32[]{:S(2)}, u32[]{:S(2)}) collective-permute-start(bf16[448,256]{1,0:T(8,128)(2,1)} %bitcast.9), channel_id=1, source_target_pairs={{0,1},{1,0},{2,3},{3,2},{4,5},{5,4},{6,7},{7,6},{8,9},{9,8},{10,11... | collective-permute-start | bytes 688136 | tf_op jit(solution)/shard_map/ppermute | solution.py:197
  3.7 1.5 collective-permute-start.3
  5.2 1.6 collective-permute-start.2
  6.7 2.7 %collective-permute-done.4.refs_4_ = bf16[448,256]{1,0:T(8,128)(2,1)S(1)} collective-permute-done((bf16[448,256]{1,0:T(8,128)(2,1)}, bf16[448,256]{1,0:T(8,128)(2,1)S(1)}, u32[]{:S(2)}, u32[]{:S(2)}) %collective-permute-start.4) | collective-permute-done | bytes 229408 | tf_op jit(solution)/shard_map/ppermute | solution.py:197
  9.5 1.5 collective-permute-done.3.refs_8_
  10.9 2.1 %collective-permute-done.2.refs_1_ = bf16[448,256]{1,0:T(8,128)(2,1)S(1)} collective-permute-done((bf16[448,256]{1,0:T(8,128)(2,1)}, bf16[448,256]{1,0:T(8,128)(2,1)S(1)}, u32[]{:S(2)}, u32[]{:S(2)}) %collective-permute-start.2) | collective-permute-done | bytes 229408 | tf_op jit(solution)/shard_map/ppermute | solution.py:197
  14.5 1.5 collective-permute-start.7
  16.5 3.5 %collective-permute-done.5.refs_2_ = bf16[448,256]{1,0:T(8,128)(2,1)S(1)} collective-permute-done((bf16[448,256]{1,0:T(8,128)(2,1)S(1)}, bf16[448,256]{1,0:T(8,128)(2,1)S(1)}, u32[]{:S(2)}, u32[]{:S(2)}) %collective-permute-start.5) | collective-permute-done | bytes 229408 | tf_op jit(solution)/shard_map/ppermute | solution.py:197
  20.8 1.6 collective-permute-done.11.refs_9_
  22.9 4.4 %collective-permute-done.7.refs_12_ = bf16[448,256]{1,0:T(8,128)(2,1)S(1)} collective-permute-done((bf16[448,256]{1,0:T(8,128)(2,1)S(1)}, bf16[448,256]{1,0:T(8,128)(2,1)S(1)}, u32[]{:S(2)}, u32[]{:S(2)}) %collective-permute-start.7) | collective-permute-done | bytes 229408 | tf_op jit(solution)/shard_map/ppermute | solution.py:197
  27.3 3.3 %collective-permute-start.14 = (bf16[448,256]{1,0:T(8,128)(2,1)S(1)}, bf16[448,256]{1,0:T(8,128)(2,1)S(1)}, u32[]{:S(2)}, u32[]{:S(2)}) collective-permute-start(bf16[448,256]{1,0:T(8,128)(2,1)S(1)} %collective-permute-done.7.refs_12_), channel_id=1, source_target_pairs={{0,2},{1,3},{2,6},{3,7},{4,0},{5,1},{6,4},{7,5},{8,10},{9,11},{10,... | collective-permute-start | bytes 688136 | tf_op jit(solution)/shard_map/ppermute | solution.py:197
  31.1 1.5 collective-permute-start
  32.6 4.6 %collective-permute-done = bf16[1,256]{1,0:T(2,128)(2,1)S(1)} collective-permute-done((bf16[1,256]{1,0:T(2,128)(2,1)}, bf16[1,256]{1,0:T(2,128)(2,1)S(1)}, u32[]{:S(2)}, u32[]{:S(2)}) %collective-permute-start) | collective-permute-done | bytes 544 | tf_op jit(solution)/shard_map/ppermute | solution.py:197
  37.7 2.9 %collective-permute-start.15 = (bf16[448,256]{1,0:T(8,128)(2,1)S(1)}, bf16[448,256]{1,0:T(8,128)(2,1)S(1)}, u32[]{:S(2)}, u32[]{:S(2)}) collective-permute-start(bf16[448,256]{1,0:T(8,128)(2,1)S(1)} %collective-permute-done.14.refs_13_), channel_id=1, source_target_pairs={{0,2},{1,3},{2,6},{3,7},{4,0},{5,1},{6,4},{7,5},{8,10},{9,11},{10,... | collective-permute-start | bytes 688136 | tf_op jit(solution)/shard_map/ppermute | solution.py:197
  40.6 1.5 collective-permute-start.10
  45.0 4.1 %collective-permute-done.10.refs_7_ = bf16[448,256]{1,0:T(8,128)(2,1)S(1)} collective-permute-done((bf16[448,256]{1,0:T(8,128)(2,1)S(1)}, bf16[448,256]{1,0:T(8,128)(2,1)S(1)}, u32[]{:S(2)}, u32[]{:S(2)}) %collective-permute-start.10) | collective-permute-done | bytes 229408 | tf_op jit(solution)/shard_map/ppermute | solution.py:197
  49.1 3.9 %collective-permute-done.16.refs_15_ = bf16[448,256]{1,0:T(8,128)(2,1)S(1)} collective-permute-done((bf16[448,256]{1,0:T(8,128)(2,1)S(1)}, bf16[448,256]{1,0:T(8,128)(2,1)S(1)}, u32[]{:S(2)}, u32[]{:S(2)}) %collective-permute-start.16) | collective-permute-done | bytes 229408 | tf_op jit(solution)/shard_map/ppermute | solution.py:197
  53.0 1.2 copy-done
  54.2 0.9 copy-done.2
  55.1 8.6 %shard_map.75 = (bf16[2,128,3584]{2,1,0:T(8,128)(2,1)S(1)}, bf16[2,3584,256]{2,1,0:T(8,128)(2,1)S(1)}, f32[2,128,256]{2,1,0:T(8,128)S(1)}, f32[2,128,128]{2,1,0:T(8,128)S(1)}) custom-call(bf16[448,256]{1,0:T(8,128)(2,1)S(1)} %bitcast.12, bf16[448,256]{1,0:T(8,128)(2,1)S(1)} %collective-permute-done.2.refs_1_, ...), custom_call_target="tpu_custom_call" | custom-call | flops 704643072 | bytes 8388608 | tf_op jit(solution)/shard_map/pallas_call | solution.py:253
  63.8 3.8 %collective-permute-done.17.x_ref.refs_7_ = bf16[2,128,3584]{2,1,0:T(8,128)(2,1)S(1)} collective-permute-done((bf16[2,128,3584]{2,1,0:T(8,128)(2,1)S(1)}, bf16[2,128,3584]{2,1,0:T(8,128)(2,1)S(1)}, u32[]{:S(2)}, u32[]{:S(2)}) %collective-permute-start.17) | collective-permute-done | bytes 1835040 | tf_op jit(solution)/shard_map/ppermute | solution.py:197
  67.6 6.3 %shard_map.76 = (bf16[2,128,3584]{2,1,0:T(8,128)(2,1)S(1)}, bf16[2,128,256]{2,1,0:T(8,128)(2,1)S(1)}, f32[2,256]{1,0:T(2,128)S(1)}) custom-call(bf16[2,256]{1,0:T(2,128)(2,1)S(1)} %pad_maximum_fusion.refs_16_.gain_ref.refs_0_.refs_10_, bf16[2,128,3584]{2,1,0:T(8,128)(2,1)S(1)} %collective-permute-done.17.x_ref.refs_7_, ...), custom_call_target="tpu_custom_call" | custom-call | flops 1644167168 | bytes 8388608 | tf_op jit(solution)/shard_map/pallas_call | solution.py:258
  74.1 3.6 %collective-permute-done.18.refs_6_ = bf16[2,128,3584]{2,1,0:T(8,128)(2,1)S(1)} collective-permute-done((bf16[2,128,3584]{2,1,0:T(8,128)(2,1)S(1)}, bf16[2,128,3584]{2,1,0:T(8,128)(2,1)S(1)}, u32[]{:S(2)}, u32[]{:S(2)}) %collective-permute-start.18) | collective-permute-done | bytes 1835040 | tf_op jit(solution)/shard_map/ppermute | solution.py:197
  77.7 12.6 %shard_map.77 = (bf16[128,3584]{1,0:T(8,128)(2,1)}, bf16[128,3584]{1,0:T(8,128)(2,1)S(1)}, f32[2,256]{1,0:T(2,128)S(1)}, bf16[448,256]{1,0:T(8,128)(2,1)S(1)}, b...) custom-call(bf16[2,256]{1,0:T(2,128)(2,1)S(1)} %pad_maximum_fusion.r, ...), custom_call_target="tpu_custom_call" | custom-call | flops 1879048192 | bytes 8388608 | tf_op jit(solution)/shard_map/pallas_call | solution.py:264
  91.5 4.0 %collective-permute-start.21 = (bf16[448,256]{1,0:T(8,128)(2,1)S(1)}, bf16[448,256]{1,0:T(8,128)(2,1)S(1)}, u32[]{:S(2)}, u32[]{:S(2)}) collective-permute-start(bf16[448,256]{1,0:T(8,128)(2,1)S(1)} %get-tuple-element.50), channel_id=1, source_target_pairs={{0,2},{1,3},{2,6},{3,7},{4,0},{5,1},{6,4},{7,5},{8,10},{9,11},{10,... | collective-permute-start | bytes 688136 | tf_op jit(solution)/shard_map/ppermute | solution.py:197
  95.4 1.5 collective-permute-start.25
  98.0 1.0 collective-permute-start.31
  99.1 1.0 collective-permute-done.21
  100.1 1.5 collective-permute-start.30
  101.6 3.2 %collective-permute-done.31 = bf16[448,256]{1,0:T(8,128)(2,1)S(1)} collective-permute-done((bf16[448,256]{1,0:T(8,128)(2,1)S(1)}, bf16[448,256]{1,0:T(8,128)(2,1)S(1)}, u32[]{:S(2)}, u32[]{:S(2)}) %collective-permute-start.31) | collective-permute-done | bytes 229408 | tf_op jit(solution)/shard_map/ppermute | solution.py:197
  105.4 7.6 %collective-permute-done.30 = bf16[448,256]{1,0:T(8,128)(2,1)S(1)} collective-permute-done((bf16[448,256]{1,0:T(8,128)(2,1)S(1)}, bf16[448,256]{1,0:T(8,128)(2,1)S(1)}, u32[]{:S(2)}, u32[]{:S(2)}) %collective-permute-start.30) | collective-permute-done | bytes 229408 | tf_op jit(solution)/shard_map/ppermute | solution.py:197
  113.1 3.9 %collective-permute-start.22 = (bf16[448,256]{1,0:T(8,128)(2,1)S(1)}, bf16[448,256]{1,0:T(8,128)(2,1)S(1)}, u32[]{:S(2)}, u32[]{:S(2)}) collective-permute-start(bf16[448,256]{1,0:T(8,128)(2,1)S(1)} %add_convert_fusion.6), channel_id=1, source_target_pairs={{0,2},{1,3},{2,6},{3,7},{4,0},{5,1},{6,4},{7,5},{8,10},{9,11},{10,... | collective-permute-start | bytes 688136 | tf_op jit(solution)/shard_map/ppermute | solution.py:197
  117.1 3.9 %collective-permute-done.22 = bf16[448,256]{1,0:T(8,128)(2,1)S(1)} collective-permute-done((bf16[448,256]{1,0:T(8,128)(2,1)S(1)}, bf16[448,256]{1,0:T(8,128)(2,1)S(1)}, u32[]{:S(2)}, u32[]{:S(2)}) %collective-permute-start.22) | collective-permute-done | bytes 229408 | tf_op jit(solution)/shard_map/ppermute | solution.py:197
  121.1 2.5 %collective-permute-start.32 = (bf16[448,256]{1,0:T(8,128)(2,1)S(1)}, bf16[448,256]{1,0:T(8,128)(2,1)S(1)}, u32[]{:S(2)}, u32[]{:S(2)}) collective-permute-start(bf16[448,256]{1,0:T(8,128)(2,1)S(1)} %add_convert_fusion.2), channel_id=1, source_target_pairs={{0,2},{1,3},{2,6},{3,7},{4,0},{5,1},{6,4},{7,5},{8,10},{9,11},{10,... | collective-permute-start | bytes 688136 | tf_op jit(solution)/shard_map/ppermute | solution.py:197
  123.6 1.6 collective-permute-start.26
  125.2 2.8 %collective-permute-done.32 = bf16[448,256]{1,0:T(8,128)(2,1)S(1)} collective-permute-done((bf16[448,256]{1,0:T(8,128)(2,1)S(1)}, bf16[448,256]{1,0:T(8,128)(2,1)S(1)}, u32[]{:S(2)}, u32[]{:S(2)}) %collective-permute-start.32) | collective-permute-done | bytes 229408 | tf_op jit(solution)/shard_map/ppermute | solution.py:197
  128.6 5.4 %collective-permute-done.23 = bf16[448,256]{1,0:T(8,128)(2,1)S(1)} collective-permute-done((bf16[448,256]{1,0:T(8,128)(2,1)S(1)}, bf16[448,256]{1,0:T(8,128)(2,1)S(1)}, u32[]{:S(2)}, u32[]{:S(2)}) %collective-permute-start.23) | collective-permute-done | bytes 229408 | tf_op jit(solution)/shard_map/ppermute | solution.py:197
  134.0 1.6 collective-permute-start.33
  135.7 1.6 collective-permute-start.24
  137.2 4.5 %collective-permute-done.33 = bf16[448,256]{1,0:T(8,128)(2,1)S(1)} collective-permute-done((bf16[448,256]{1,0:T(8,128)(2,1)S(1)}, bf16[448,256]{1,0:T(8,128)(2,1)S(1)}, u32[]{:S(2)}, u32[]{:S(2)}) %collective-permute-start.33) | collective-permute-done | bytes 229408 | tf_op jit(solution)/shard_map/ppermute | solution.py:197
  141.9 2.1 %collective-permute-start.34 = (bf16[448,256]{1,0:T(8,128)(2,1)S(1)}, bf16[448,256]{1,0:T(8,128)(2,1)S(1)}, u32[]{:S(2)}, u32[]{:S(2)}) collective-permute-start(bf16[448,256]{1,0:T(8,128)(2,1)S(1)} %add_convert_fusion), channel_id=1, source_target_pairs={{0,2},{1,3},{2,6},{3,7},{4,0},{5,1},{6,4},{7,5},{8,10},{9,11},{10,... | collective-permute-start | bytes 688136 | tf_op jit(solution)/shard_map/ppermute | solution.py:197
  144.5 3.0 %collective-permute-done.35 = f32[1,256]{1,0:T(1,128)S(1)} collective-permute-done((f32[1,256]{1,0:T(1,128)S(1)}, f32[1,256]{1,0:T(1,128)S(1)}, u32[]{:S(2)}, u32[]{:S(2)}) %collective-permute-start.35) | collective-permute-done | bytes 1056 | tf_op jit(solution)/shard_map/ppermute | solution.py:197
  147.6 1.7 %collective-permute-start.36 = (f32[1,256]{1,0:T(1,128)S(1)}, f32[1,256]{1,0:T(1,128)S(1)}, u32[]{:S(2)}, u32[]{:S(2)}) collective-permute-start(f32[1,256]{1,0:T(1,128)S(1)} %slice_add_fusion), channel_id=1, source_target_pairs={{0,1},{1,0},{2,3},{3,2},{4,5},{5,4},{6,7},{7,6},{8,9},{9,8},{10,11... | collective-permute-start | bytes 3080 | tf_op jit(solution)/shard_map/ppermute | solution.py:197
  149.3 1.8 %collective-permute-done.36 = f32[1,256]{1,0:T(1,128)S(1)} collective-permute-done((f32[1,256]{1,0:T(1,128)S(1)}, f32[1,256]{1,0:T(1,128)S(1)}, u32[]{:S(2)}, u32[]{:S(2)}) %collective-permute-start.36) | collective-permute-done | bytes 1056 | tf_op jit(solution)/shard_map/ppermute | solution.py:197
  151.1 2.2 %collective-permute-start.37 = (f32[1,256]{1,0:T(1,128)S(1)}, f32[1,256]{1,0:T(1,128)S(1)}, u32[]{:S(2)}, u32[]{:S(2)}) collective-permute-start(f32[1,256]{1,0:T(1,128)S(1)} %add.73), channel_id=1, source_target_pairs={{0,2},{1,3},{2,0},{3,1},{4,6},{5,7},{6,4},{7,5},{8,10},{9,11},{10,... | collective-permute-start | bytes 3080 | tf_op jit(solution)/shard_map/ppermute | solution.py:197
  153.3 1.5 collective-permute-done.37
  154.9 1.0 collective-permute-start.38
  155.9 3.4 %collective-permute-done.38 = f32[1,256]{1,0:T(1,128)S(1)} collective-permute-done((f32[1,256]{1,0:T(1,128)S(1)}, f32[1,256]{1,0:T(1,128)S(1)}, u32[]{:S(2)}, u32[]{:S(2)}) %collective-permute-start.38) | collective-permute-done | bytes 1056 | tf_op jit(solution)/shard_map/ppermute | solution.py:197
  (54 shorter events, 14.4 us)
Async XLA Ops:
  0.6 8.8 %collective-permute-start.4 = (bf16[448,256]{1,0:T(8,128)(2,1)}, bf16[448,256]{1,0:T(8,128)(2,1)S(1)}, u32[]{:S(2)}, u32[]{:S(2)}) collective-permute-start(bf16[448,256]{1,0:T(8,128)(2,1)} %bitcast.9), channel_id=1, source_target_pairs={{0,1},{1,0},{2,3},{3,2},{4,5},{5,4},{6,7},{7,6},{8,9},{9,8},{10,11... | collective-permute-start | bytes 688136 | tf_op jit(solution)/shard_map/ppermute | solution.py:197
  3.7 7.3 %collective-permute-start.3 = (bf16[448,256]{1,0:T(8,128)(2,1)}, bf16[448,256]{1,0:T(8,128)(2,1)S(1)}, u32[]{:S(2)}, u32[]{:S(2)}) collective-permute-start(bf16[448,256]{1,0:T(8,128)(2,1)} %bitcast.10), channel_id=1, source_target_pairs={{0,16},{1,17},{2,18},{3,19},{4,20},{5,21},{6,22},{7,23},{8,24},{9,... | collective-permute-start | bytes 688136 | tf_op jit(solution)/shard_map/ppermute | solution.py:197
  5.2 7.9 %collective-permute-start.2 = (bf16[448,256]{1,0:T(8,128)(2,1)}, bf16[448,256]{1,0:T(8,128)(2,1)S(1)}, u32[]{:S(2)}, u32[]{:S(2)}) collective-permute-start(bf16[448,256]{1,0:T(8,128)(2,1)} %bitcast.11), channel_id=1, source_target_pairs={{0,2},{1,3},{2,6},{3,7},{4,0},{5,1},{6,4},{7,5},{8,10},{9,11},{10,... | collective-permute-start | bytes 688136 | tf_op jit(solution)/shard_map/ppermute | solution.py:197
  13.1 6.9 %collective-permute-start.5 = (bf16[448,256]{1,0:T(8,128)(2,1)S(1)}, bf16[448,256]{1,0:T(8,128)(2,1)S(1)}, u32[]{:S(2)}, u32[]{:S(2)}) collective-permute-start(bf16[448,256]{1,0:T(8,128)(2,1)S(1)} %collective-permute-done.2.refs_1_), channel_id=1, source_target_pairs={{0,2},{1,3},{2,6},{3,7},{4,0},{5,1},{6,4},{7,5},{8,10},{9,11},{10,... | collective-permute-start | bytes 688136 | tf_op jit(solution)/shard_map/ppermute | solution.py:197
  13.9 35.2 %collective-permute-start.1 = (bf16[128,3584]{1,0:T(8,128)(2,1)}, bf16[128,3584]{1,0:T(8,128)(2,1)S(1)}, u32[]{:S(2)}, u32[]{:S(2)}) collective-permute-start(bf16[128,3584]{1,0:T(8,128)(2,1)} %bitcast.14), channel_id=1, source_target_pairs={{0,8},{1,9},{2,10},{3,11},{4,12},{5,13},{6,14},{7,15},{8,0},{9,1},... | collective-permute-start | bytes 2752520 | tf_op jit(solution)/shard_map/ppermute | solution.py:197
  13.9 8.4 %collective-permute-start.11 = (bf16[448,256]{1,0:T(8,128)(2,1)S(1)}, bf16[448,256]{1,0:T(8,128)(2,1)S(1)}, u32[]{:S(2)}, u32[]{:S(2)}) collective-permute-start(bf16[448,256]{1,0:T(8,128)(2,1)S(1)} %collective-permute-done.2.refs_1_), channel_id=1, source_target_pairs={{0,16},{1,17},{2,18},{3,19},{4,20},{5,21},{6,22},{7,23},{8,24},{9,... | collective-permute-start | bytes 688136 | tf_op jit(solution)/shard_map/ppermute | solution.py:197
  14.5 12.8 %collective-permute-start.7 = (bf16[448,256]{1,0:T(8,128)(2,1)S(1)}, bf16[448,256]{1,0:T(8,128)(2,1)S(1)}, u32[]{:S(2)}, u32[]{:S(2)}) collective-permute-start(bf16[448,256]{1,0:T(8,128)(2,1)S(1)} %collective-permute-done.4.refs_4_), channel_id=1, source_target_pairs={{0,16},{1,17},{2,18},{3,19},{4,20},{5,21},{6,22},{7,23},{8,24},{9,... | collective-permute-start | bytes 688136 | tf_op jit(solution)/shard_map/ppermute | solution.py:197
  16.0 14.6 %collective-permute-start.8 = (bf16[448,256]{1,0:T(8,128)(2,1)S(1)}, bf16[448,256]{1,0:T(8,128)(2,1)S(1)}, u32[]{:S(2)}, u32[]{:S(2)}) collective-permute-start(bf16[448,256]{1,0:T(8,128)(2,1)S(1)} %collective-permute-done.2.refs_1_), channel_id=1, source_target_pairs={{0,1},{1,0},{2,3},{3,2},{4,5},{5,4},{6,7},{7,6},{8,9},{9,8},{10,11... | collective-permute-start | bytes 688136 | tf_op jit(solution)/shard_map/ppermute | solution.py:197
  20.0 10.6 %collective-permute-start.6 = (bf16[448,256]{1,0:T(8,128)(2,1)S(1)}, bf16[448,256]{1,0:T(8,128)(2,1)S(1)}, u32[]{:S(2)}, u32[]{:S(2)}) collective-permute-start(bf16[448,256]{1,0:T(8,128)(2,1)S(1)} %collective-permute-done.5.refs_2_), channel_id=1, source_target_pairs={{0,2},{1,3},{2,6},{3,7},{4,0},{5,1},{6,4},{7,5},{8,10},{9,11},{10,... | collective-permute-start | bytes 688136 | tf_op jit(solution)/shard_map/ppermute | solution.py:197
  22.3 18.2 %collective-permute-start.12 = (bf16[448,256]{1,0:T(8,128)(2,1)S(1)}, bf16[448,256]{1,0:T(8,128)(2,1)S(1)}, u32[]{:S(2)}, u32[]{:S(2)}) collective-permute-start(bf16[448,256]{1,0:T(8,128)(2,1)S(1)} %collective-permute-done.5.refs_2_), channel_id=1, source_target_pairs={{0,16},{1,17},{2,18},{3,19},{4,20},{5,21},{6,22},{7,23},{8,24},{9,... | collective-permute-start | bytes 688136 | tf_op jit(solution)/shard_map/ppermute | solution.py:197
  27.3 10.4 %collective-permute-start.14 = (bf16[448,256]{1,0:T(8,128)(2,1)S(1)}, bf16[448,256]{1,0:T(8,128)(2,1)S(1)}, u32[]{:S(2)}, u32[]{:S(2)}) collective-permute-start(bf16[448,256]{1,0:T(8,128)(2,1)S(1)} %collective-permute-done.7.refs_12_), channel_id=1, source_target_pairs={{0,2},{1,3},{2,6},{3,7},{4,0},{5,1},{6,4},{7,5},{8,10},{9,11},{10,... | collective-permute-start | bytes 688136 | tf_op jit(solution)/shard_map/ppermute | solution.py:197
  30.5 11.5 %collective-permute-start.13 = (bf16[448,256]{1,0:T(8,128)(2,1)S(1)}, bf16[448,256]{1,0:T(8,128)(2,1)S(1)}, u32[]{:S(2)}, u32[]{:S(2)}) collective-permute-start(bf16[448,256]{1,0:T(8,128)(2,1)S(1)} %collective-permute-done.6.refs_3_), channel_id=1, source_target_pairs={{0,16},{1,17},{2,18},{3,19},{4,20},{5,21},{6,22},{7,23},{8,24},{9,... | collective-permute-start | bytes 688136 | tf_op jit(solution)/shard_map/ppermute | solution.py:197
  31.1 6.1 %collective-permute-start = (bf16[1,256]{1,0:T(2,128)(2,1)}, bf16[1,256]{1,0:T(2,128)(2,1)S(1)}, u32[]{:S(2)}, u32[]{:S(2)}) collective-permute-start(bf16[1,256]{1,0:T(2,128)(2,1)} %param.7), channel_id=1, source_target_pairs={{0,16},{1,17},{2,18},{3,19},{4,20},{5,21},{6,22},{7,23},{8,24},{9,... | collective-permute-start | bytes 1544 | tf_op jit(solution)/shard_map/ppermute | solution.py:197
  37.2 6.9 %collective-permute-start.9 = (bf16[448,256]{1,0:T(8,128)(2,1)S(1)}, bf16[448,256]{1,0:T(8,128)(2,1)S(1)}, u32[]{:S(2)}, u32[]{:S(2)}) collective-permute-start(bf16[448,256]{1,0:T(8,128)(2,1)S(1)} %collective-permute-done.5.refs_2_), channel_id=1, source_target_pairs={{0,1},{1,0},{2,3},{3,2},{4,5},{5,4},{6,7},{7,6},{8,9},{9,8},{10,11... | collective-permute-start | bytes 688136 | tf_op jit(solution)/shard_map/ppermute | solution.py:197
  37.7 7.3 %collective-permute-start.15 = (bf16[448,256]{1,0:T(8,128)(2,1)S(1)}, bf16[448,256]{1,0:T(8,128)(2,1)S(1)}, u32[]{:S(2)}, u32[]{:S(2)}) collective-permute-start(bf16[448,256]{1,0:T(8,128)(2,1)S(1)} %collective-permute-done.14.refs_13_), channel_id=1, source_target_pairs={{0,2},{1,3},{2,6},{3,7},{4,0},{5,1},{6,4},{7,5},{8,10},{9,11},{10,... | collective-permute-start | bytes 688136 | tf_op jit(solution)/shard_map/ppermute | solution.py:197
  40.6 8.6 %collective-permute-start.10 = (bf16[448,256]{1,0:T(8,128)(2,1)S(1)}, bf16[448,256]{1,0:T(8,128)(2,1)S(1)}, u32[]{:S(2)}, u32[]{:S(2)}) collective-permute-start(bf16[448,256]{1,0:T(8,128)(2,1)S(1)} %collective-permute-done.6.refs_3_), channel_id=1, source_target_pairs={{0,1},{1,0},{2,3},{3,2},{4,5},{5,4},{6,7},{7,6},{8,9},{9,8},{10,11... | collective-permute-start | bytes 688136 | tf_op jit(solution)/shard_map/ppermute | solution.py:197
  42.1 10.9 %collective-permute-start.16 = (bf16[448,256]{1,0:T(8,128)(2,1)S(1)}, bf16[448,256]{1,0:T(8,128)(2,1)S(1)}, u32[]{:S(2)}, u32[]{:S(2)}) collective-permute-start(bf16[448,256]{1,0:T(8,128)(2,1)S(1)} %collective-permute-done.13.refs_11_), channel_id=1, source_target_pairs={{0,1},{1,0},{2,3},{3,2},{4,5},{5,4},{6,7},{7,6},{8,9},{9,8},{10,11... | collective-permute-start | bytes 688136 | tf_op jit(solution)/shard_map/ppermute | solution.py:197
  53.0 1.2 copy-start
  54.2 0.9 copy-start.2
  63.7 3.9 %collective-permute-start.17 = (bf16[2,128,3584]{2,1,0:T(8,128)(2,1)S(1)}, bf16[2,128,3584]{2,1,0:T(8,128)(2,1)S(1)}, u32[]{:S(2)}, u32[]{:S(2)}) collective-permute-start(bf16[2,128,3584]{2,1,0:T(8,128)(2,1)S(1)} %get-tuple-element.39), channel_id=1, source_target_pairs={{0,8},{1,9},{2,10},{3,11},{4,12},{5,13},{6,14},{7,15},{8,0},{9,1},... | collective-permute-start | bytes 5505032 | tf_op jit(solution)/shard_map/ppermute | solution.py:197
  67.6 10.1 %copy-start.1 = (bf16[1,1,128,3584]{3,2,1,0:T(8,128)(2,1)S(1)}, bf16[1,1,128,3584]{3,2,1,0:T(8,128)(2,1)}, u32[]{:S(2)}) copy-start(bf16[1,1,128,3584]{3,2,1,0:T(8,128)(2,1)} %param.4) | copy-start | bytes 2752516
  73.9 3.9 %collective-permute-start.18 = (bf16[2,128,3584]{2,1,0:T(8,128)(2,1)S(1)}, bf16[2,128,3584]{2,1,0:T(8,128)(2,1)S(1)}, u32[]{:S(2)}, u32[]{:S(2)}) collective-permute-start(bf16[2,128,3584]{2,1,0:T(8,128)(2,1)S(1)} %get-tuple-element.40), channel_id=1, source_target_pairs={{0,8},{1,9},{2,10},{3,11},{4,12},{5,13},{6,14},{7,15},{8,0},{9,1},... | collective-permute-start | bytes 5505032 | tf_op jit(solution)/shard_map/ppermute | solution.py:197
  90.3 7.7 %collective-permute-start.29 = (bf16[448,256]{1,0:T(8,128)(2,1)S(1)}, bf16[448,256]{1,0:T(8,128)(2,1)S(1)}, u32[]{:S(2)}, u32[]{:S(2)}) collective-permute-start(bf16[448,256]{1,0:T(8,128)(2,1)S(1)} %get-tuple-element.59), channel_id=1, source_target_pairs={{0,1},{1,0},{2,3},{3,2},{4,5},{5,4},{6,7},{7,6},{8,9},{9,8},{10,11... | collective-permute-start | bytes 688136 | tf_op jit(solution)/shard_map/ppermute | solution.py:197
  91.0 69.0 %collective-permute-start.20 = (bf16[448,256]{1,0:T(8,128)(2,1)S(1)}, bf16[448,256]{1,0:T(8,128)(2,1)S(1)}, u32[]{:S(2)}, u32[]{:S(2)}) collective-permute-start(bf16[448,256]{1,0:T(8,128)(2,1)S(1)} %get-tuple-element.46), channel_id=1, source_target_pairs={{0,16},{1,17},{2,18},{3,19},{4,20},{5,21},{6,22},{7,23},{8,24},{9,... | collective-permute-start | bytes 688136 | tf_op jit(solution)/shard_map/ppermute | solution.py:197
  91.5 8.6 %collective-permute-start.21 = (bf16[448,256]{1,0:T(8,128)(2,1)S(1)}, bf16[448,256]{1,0:T(8,128)(2,1)S(1)}, u32[]{:S(2)}, u32[]{:S(2)}) collective-permute-start(bf16[448,256]{1,0:T(8,128)(2,1)S(1)} %get-tuple-element.50), channel_id=1, source_target_pairs={{0,2},{1,3},{2,6},{3,7},{4,0},{5,1},{6,4},{7,5},{8,10},{9,11},{10,... | collective-permute-start | bytes 688136 | tf_op jit(solution)/shard_map/ppermute | solution.py:197
  95.4 40.2 %collective-permute-start.25 = (bf16[448,256]{1,0:T(8,128)(2,1)S(1)}, bf16[448,256]{1,0:T(8,128)(2,1)S(1)}, u32[]{:S(2)}, u32[]{:S(2)}) collective-permute-start(bf16[448,256]{1,0:T(8,128)(2,1)S(1)} %get-tuple-element.52), channel_id=1, source_target_pairs={{0,16},{1,17},{2,18},{3,19},{4,20},{5,21},{6,22},{7,23},{8,24},{9,... | collective-permute-start | bytes 688136 | tf_op jit(solution)/shard_map/ppermute | solution.py:197
  96.9 26.7 %collective-permute-start.27 = (bf16[448,256]{1,0:T(8,128)(2,1)S(1)}, bf16[448,256]{1,0:T(8,128)(2,1)S(1)}, u32[]{:S(2)}, u32[]{:S(2)}) collective-permute-start(bf16[448,256]{1,0:T(8,128)(2,1)S(1)} %get-tuple-element.55), channel_id=1, source_target_pairs={{0,16},{1,17},{2,18},{3,19},{4,20},{5,21},{6,22},{7,23},{8,24},{9,... | collective-permute-start | bytes 688136 | tf_op jit(solution)/shard_map/ppermute | solution.py:197
  98.0 6.8 %collective-permute-start.31 = (bf16[448,256]{1,0:T(8,128)(2,1)S(1)}, bf16[448,256]{1,0:T(8,128)(2,1)S(1)}, u32[]{:S(2)}, u32[]{:S(2)}) collective-permute-start(bf16[448,256]{1,0:T(8,128)(2,1)S(1)} %get-tuple-element.60), channel_id=1, source_target_pairs={{0,1},{1,0},{2,3},{3,2},{4,5},{5,4},{6,7},{7,6},{8,9},{9,8},{10,11... | collective-permute-start | bytes 688136 | tf_op jit(solution)/shard_map/ppermute | solution.py:197
  100.1 13.0 %collective-permute-start.30 = (bf16[448,256]{1,0:T(8,128)(2,1)S(1)}, bf16[448,256]{1,0:T(8,128)(2,1)S(1)}, u32[]{:S(2)}, u32[]{:S(2)}) collective-permute-start(bf16[448,256]{1,0:T(8,128)(2,1)S(1)} %add_convert_fusion.3), channel_id=1, source_target_pairs={{0,16},{1,17},{2,18},{3,19},{4,20},{5,21},{6,22},{7,23},{8,24},{9,... | collective-permute-start | bytes 688136 | tf_op jit(solution)/shard_map/ppermute | solution.py:197
  104.8 20.3 %collective-permute-start.28 = (bf16[448,256]{1,0:T(8,128)(2,1)S(1)}, bf16[448,256]{1,0:T(8,128)(2,1)S(1)}, u32[]{:S(2)}, u32[]{:S(2)}) collective-permute-start(bf16[448,256]{1,0:T(8,128)(2,1)S(1)} %get-tuple-element.56), channel_id=1, source_target_pairs={{0,1},{1,0},{2,3},{3,2},{4,5},{5,4},{6,7},{7,6},{8,9},{9,8},{10,11... | collective-permute-start | bytes 688136 | tf_op jit(solution)/shard_map/ppermute | solution.py:197
  113.1 8.0 %collective-permute-start.22 = (bf16[448,256]{1,0:T(8,128)(2,1)S(1)}, bf16[448,256]{1,0:T(8,128)(2,1)S(1)}, u32[]{:S(2)}, u32[]{:S(2)}) collective-permute-start(bf16[448,256]{1,0:T(8,128)(2,1)S(1)} %add_convert_fusion.6), channel_id=1, source_target_pairs={{0,2},{1,3},{2,6},{3,7},{4,0},{5,1},{6,4},{7,5},{8,10},{9,11},{10,... | collective-permute-start | bytes 688136 | tf_op jit(solution)/shard_map/ppermute | solution.py:197
  121.1 6.9 %collective-permute-start.32 = (bf16[448,256]{1,0:T(8,128)(2,1)S(1)}, bf16[448,256]{1,0:T(8,128)(2,1)S(1)}, u32[]{:S(2)}, u32[]{:S(2)}) collective-permute-start(bf16[448,256]{1,0:T(8,128)(2,1)S(1)} %add_convert_fusion.2), channel_id=1, source_target_pairs={{0,2},{1,3},{2,6},{3,7},{4,0},{5,1},{6,4},{7,5},{8,10},{9,11},{10,... | collective-permute-start | bytes 688136 | tf_op jit(solution)/shard_map/ppermute | solution.py:197
  123.6 13.6 %collective-permute-start.26 = (bf16[448,256]{1,0:T(8,128)(2,1)S(1)}, bf16[448,256]{1,0:T(8,128)(2,1)S(1)}, u32[]{:S(2)}, u32[]{:S(2)}) collective-permute-start(bf16[448,256]{1,0:T(8,128)(2,1)S(1)} %get-tuple-element.53), channel_id=1, source_target_pairs={{0,1},{1,0},{2,3},{3,2},{4,5},{5,4},{6,7},{7,6},{8,9},{9,8},{10,11... | collective-permute-start | bytes 688136 | tf_op jit(solution)/shard_map/ppermute | solution.py:197
  125.2 34.7 %collective-permute-start.19 = (bf16[128,3584]{1,0:T(8,128)(2,1)S(1)}, bf16[128,3584]{1,0:T(8,128)(2,1)S(1)}, u32[]{:S(2)}, u32[]{:S(2)}) collective-permute-start(bf16[128,3584]{1,0:T(8,128)(2,1)S(1)} %get-tuple-element.44), channel_id=1, source_target_pairs={{0,8},{1,9},{2,10},{3,11},{4,12},{5,13},{6,14},{7,15},{8,0},{9,1},... | collective-permute-start | bytes 2752520 | tf_op jit(solution)/shard_map/ppermute | solution.py:197
  128.0 6.0 %collective-permute-start.23 = (bf16[448,256]{1,0:T(8,128)(2,1)S(1)}, bf16[448,256]{1,0:T(8,128)(2,1)S(1)}, u32[]{:S(2)}, u32[]{:S(2)}) collective-permute-start(bf16[448,256]{1,0:T(8,128)(2,1)S(1)} %add_convert_fusion.5), channel_id=1, source_target_pairs={{0,16},{1,17},{2,18},{3,19},{4,20},{5,21},{6,22},{7,23},{8,24},{9,... | collective-permute-start | bytes 688136 | tf_op jit(solution)/shard_map/ppermute | solution.py:197
  134.0 7.8 %collective-permute-start.33 = (bf16[448,256]{1,0:T(8,128)(2,1)S(1)}, bf16[448,256]{1,0:T(8,128)(2,1)S(1)}, u32[]{:S(2)}, u32[]{:S(2)}) collective-permute-start(bf16[448,256]{1,0:T(8,128)(2,1)S(1)} %add_convert_fusion.1), channel_id=1, source_target_pairs={{0,2},{1,3},{2,6},{3,7},{4,0},{5,1},{6,4},{7,5},{8,10},{9,11},{10,... | collective-permute-start | bytes 688136 | tf_op jit(solution)/shard_map/ppermute | solution.py:197
  135.7 24.3 %collective-permute-start.24 = (bf16[448,256]{1,0:T(8,128)(2,1)S(1)}, bf16[448,256]{1,0:T(8,128)(2,1)S(1)}, u32[]{:S(2)}, u32[]{:S(2)}) collective-permute-start(bf16[448,256]{1,0:T(8,128)(2,1)S(1)} %add_convert_fusion.4), channel_id=1, source_target_pairs={{0,1},{1,0},{2,3},{3,2},{4,5},{5,4},{6,7},{7,6},{8,9},{9,8},{10,11... | collective-permute-start | bytes 688136 | tf_op jit(solution)/shard_map/ppermute | solution.py:197
  141.9 18.0 %collective-permute-start.34 = (bf16[448,256]{1,0:T(8,128)(2,1)S(1)}, bf16[448,256]{1,0:T(8,128)(2,1)S(1)}, u32[]{:S(2)}, u32[]{:S(2)}) collective-permute-start(bf16[448,256]{1,0:T(8,128)(2,1)S(1)} %add_convert_fusion), channel_id=1, source_target_pairs={{0,2},{1,3},{2,6},{3,7},{4,0},{5,1},{6,4},{7,5},{8,10},{9,11},{10,... | collective-permute-start | bytes 688136 | tf_op jit(solution)/shard_map/ppermute | solution.py:197
  144.0 3.6 %collective-permute-start.35 = (f32[1,256]{1,0:T(1,128)S(1)}, f32[1,256]{1,0:T(1,128)S(1)}, u32[]{:S(2)}, u32[]{:S(2)}) collective-permute-start(f32[1,256]{1,0:T(1,128)S(1)} %slice.7), channel_id=1, source_target_pairs={{0,16},{1,17},{2,18},{3,19},{4,20},{5,21},{6,22},{7,23},{8,24},{9,... | collective-permute-start | bytes 3080 | tf_op jit(solution)/shard_map/ppermute | solution.py:197
  147.6 3.6 %collective-permute-start.36 = (f32[1,256]{1,0:T(1,128)S(1)}, f32[1,256]{1,0:T(1,128)S(1)}, u32[]{:S(2)}, u32[]{:S(2)}) collective-permute-start(f32[1,256]{1,0:T(1,128)S(1)} %slice_add_fusion), channel_id=1, source_target_pairs={{0,1},{1,0},{2,3},{3,2},{4,5},{5,4},{6,7},{7,6},{8,9},{9,8},{10,11... | collective-permute-start | bytes 3080 | tf_op jit(solution)/shard_map/ppermute | solution.py:197
  151.1 3.7 %collective-permute-start.37 = (f32[1,256]{1,0:T(1,128)S(1)}, f32[1,256]{1,0:T(1,128)S(1)}, u32[]{:S(2)}, u32[]{:S(2)}) collective-permute-start(f32[1,256]{1,0:T(1,128)S(1)} %add.73), channel_id=1, source_target_pairs={{0,2},{1,3},{2,0},{3,1},{4,6},{5,7},{6,4},{7,5},{8,10},{9,11},{10,... | collective-permute-start | bytes 3080 | tf_op jit(solution)/shard_map/ppermute | solution.py:197
  154.9 4.5 %collective-permute-start.38 = (f32[1,256]{1,0:T(1,128)S(1)}, f32[1,256]{1,0:T(1,128)S(1)}, u32[]{:S(2)}, u32[]{:S(2)}) collective-permute-start(f32[1,256]{1,0:T(1,128)S(1)} %add.74), channel_id=1, source_target_pairs={{0,4},{1,5},{2,6},{3,7},{4,0},{5,1},{6,2},{7,3},{8,12},{9,13},{10,... | collective-permute-start | bytes 3080 | tf_op jit(solution)/shard_map/ppermute | solution.py:197

commit v2 on v0

--- a/solution.py
+++ b/solution.py
@@ -1,9 +1,283 @@
+import functools
+
 import jax
 import jax.numpy as jnp
 from jax import lax
+from jax.experimental import pallas as pl
+from jax.experimental.pallas import tpu as pltpu
 from jax.sharding import PartitionSpec as P
 
 EPS = 1e-06
+AXES = ("section", "dp")
+BF16 = jnp.bfloat16
+F32 = jnp.float32
+CHUNK = 512
+VMEM_LIMIT = 40 * 1024 * 1024
+
+
+def matmul(a, b):
+    return jnp.dot(a, b, preferred_element_type=F32)
+
+
+def matmul_nt(a, b):
+    return lax.dot_general(a, b, (((1,), (1,)), ((), ())), preferred_element_type=F32)
+
+
+def matmul_tn(a, b):
+    return lax.dot_general(a, b, (((0,), (0,)), ((), ())), preferred_element_type=F32)
+
+
+def latent_norm(c, g):
+    inv = lax.rsqrt(jnp.mean(c * c, axis=-1, keepdims=True) + EPS)
+    return inv, (c * inv * g.astype(F32)).astype(BF16)
+
+
+def attention(normed, width):
+    scores = matmul_nt(normed, normed) * (3.0 / width)
+    rows = lax.broadcasted_iota(jnp.int32, scores.shape, 0)
+    cols = lax.broadcasted_iota(jnp.int32, scores.shape, 1)
+    scores = jnp.where(cols <= rows, scores, -1e30)
+    expo = jnp.exp(scores - jnp.max(scores, axis=-1, keepdims=True))
+    return expo / jnp.sum(expo, axis=-1, keepdims=True)
+
+
+def column_chunks(width):
+    return [slice(at, at + CHUNK) for at in range(0, width, CHUNK)]
+
+
+def mix_into(out_ref, x_ref, probs_b):
+    for cols in column_chunks(x_ref.shape[-1]):
+        x = x_ref[:, cols]
+        out_ref[:, cols] = (x.astype(F32) + matmul(probs_b, x)).astype(BF16)
+
+
+def score_grad(dy_ref, x_ref):
+    total = None
+    for cols in column_chunks(x_ref.shape[-1]):
+        part = matmul_nt(dy_ref[:, cols], x_ref[:, cols])
+        total = part if total is None else total + part
+    return total
+
+
+def latent_grad(dprobs, probs, c, inv, normed, g):
+    scale = 3.0 / c.shape[-1]
+    dscores = probs * (dprobs - jnp.sum(dprobs * probs, axis=-1, keepdims=True))
+    dscores_b = (dscores * scale).astype(BF16)
+    dnormed = matmul(dscores_b, normed) + matmul_tn(dscores_b, normed)
+    dgain = jnp.sum(dnormed * c * inv, axis=0, keepdims=True)
+    dhat = dnormed * g.astype(F32)
+    dc = inv * dhat - c * (inv * inv * inv) * jnp.mean(dhat * c, axis=-1, keepdims=True)
+    return dc.astype(BF16), dgain
+
+
+def input_grad(out_ref, dy_ref, probs_b, dc_b, w_ref):
+    for cols in column_chunks(dy_ref.shape[-1]):
+        dy = dy_ref[:, cols]
+        dx = dy.astype(F32) + matmul_tn(probs_b, dy) + matmul_nt(dc_b, w_ref[cols, :])
+        out_ref[:, cols] = dx.astype(BF16)
+
+
+def ring_place(value):
+    return value ^ (value >> 1)
+
+
+def shard_row(dy, steps, rows):
+    dp = lax.axis_index("dp")
+    place = (ring_place(dp >> 1) + steps) & 3
+    return pl.multiple_of((ring_place(place) * 2 + ((dp & 1) ^ dy)) * rows, 16)
+
+
+def slot_of(chain):
+    return chain ^ 1 ^ (lax.axis_index("section") & 1)
+
+
+def first_block(slot, *refs):
+    pieces, (gain_ref, x_ref, u_ref, w_ref, c_ref, p_ref) = refs[:8], refs[8:]
+    rows = pieces[0].shape[0]
+    for at, piece in enumerate(pieces):
+        w_ref[pl.ds(shard_row(at // 4, 4 - at % 4, rows), rows), :] = piece[...]
+    c = matmul(x_ref[...], w_ref[...])
+    _, normed = latent_norm(c, gain_ref[slot : slot + 1, :])
+    probs = attention(normed, c.shape[-1])
+    c_ref[...] = c
+    p_ref[...] = probs
+    mix_into(u_ref, x_ref, probs.astype(BF16))
+
+
+def second_block(chain, gain_ref, x_ref, w0_ref, w1_ref, e_ref, dc_ref, dg_ref, v_ref, c_ref):
+    slot = slot_of(chain)
+    g = jnp.where(slot == 0, gain_ref[0:1, :].astype(F32), gain_ref[1:2, :].astype(F32))
+    for at, w_ref in enumerate((w0_ref, w1_ref)):
+
+        @pl.when(slot == at)
+        def _(w_ref=w_ref):
+            c_ref[...] = matmul(x_ref[...], w_ref[...])
+
+    c = c_ref[...]
+    inv, normed = latent_norm(c, g)
+    probs = attention(normed, c.shape[-1])
+    probs_b = probs.astype(BF16)
+    mix_into(v_ref, x_ref, probs_b)
+    dc_b, dgain = latent_grad(score_grad(v_ref, x_ref), probs, c, inv, normed, g)
+    dc_ref[...] = dc_b
+    dg_ref[...] = dgain
+    for at, w_ref in enumerate((w0_ref, w1_ref)):
+
+        @pl.when(slot == at)
+        def _(w_ref=w_ref):
+            input_grad(e_ref, v_ref, probs_b, dc_b, w_ref)
+
+
+def first_weight_grad(slot, *refs):
+    gain_ref, x_ref, c_ref, p_ref, cot_ref, x2a_ref, x2b_ref, dc2a_ref, dc2b_ref, dg2a_ref, dg2b_ref = refs[:11]
+    dc_ref, dg_ref = refs[11:13]
+    pieces, (dw_ref, dcs_ref) = refs[13:21], refs[21:]
+    tokens, rows = x_ref.shape[0], pieces[0].shape[0]
+    g = gain_ref[slot : slot + 1, :]
+    c, probs = c_ref[...], p_ref[...]
+    inv, normed = latent_norm(c, g)
+    dc_b, dgain = latent_grad(score_grad(cot_ref, x_ref), probs, c, inv, normed, g)
+    dc_ref[...] = dc_b
+    dcs_ref[:tokens, :] = dc_b
+    for chain, x2_ref, dc2_ref, dg2_ref in ((0, x2a_ref, dc2a_ref, dg2a_ref), (1, x2b_ref, dc2b_ref, dg2b_ref)):
+
+        @pl.when(slot_of(chain) == slot)
+        def _(x2_ref=x2_ref, dc2_ref=dc2_ref, dg2_ref=dg2_ref):
+            dg_ref[...] = dgain + dg2_ref[...]
+            dcs_ref[tokens:, :] = dc2_ref[...]
+            for cols in column_chunks(x_ref.shape[-1]):
+                x = jnp.concatenate([x_ref[:, cols], x2_ref[:, cols]], axis=0)
+                dw_ref[cols, :] = matmul_tn(x, dcs_ref[...]).astype(BF16)
+
+    for at, piece in enumerate(pieces):
+        piece[...] = dw_ref[pl.ds(shard_row(at // 4, at % 4, rows), rows), :]
+
+
+def first_input_grad(cot_ref, p_ref, dc_ref, w_ref, out_ref):
+    input_grad(out_ref, cot_ref, p_ref[...].astype(BF16), dc_ref[...], w_ref)
+
+
+def kernel_call(body, args, outs, scratch=(), flops=0):
+    local = pl.BlockSpec(memory_space=pltpu.VMEM)
+    return pl.pallas_call(
+        body,
+        out_shape=outs,
+        in_specs=[local] * len(args),
+        out_specs=[local] * len(outs),
+        scratch_shapes=scratch,
+        compiler_params=pltpu.CompilerParams(vmem_limit_bytes=VMEM_LIMIT),
+        cost_estimate=pl.CostEstimate(flops=flops, bytes_accessed=4 << 20, transcendentals=0),
+    )(*args)
+
+
+def moves_between():
+    def pairs(change):
+        found = []
+        for i in range(32):
+            s, d = divmod(i, 8)
+            to_s, to_d = change(s, d)
+            found.append((i, to_s * 8 + to_d))
+        return found
+
+    following = {0: 1, 1: 3, 3: 2, 2: 0}
+    changes = (
+        lambda s, d: (s ^ 1, d),
+        lambda s, d: (s ^ 2, d),
+        lambda s, d: (s, d ^ 1),
+        lambda s, d: (s, following[d >> 1] * 2 + (d & 1)),
+        lambda s, d: (s, d ^ 2),
+        lambda s, d: (s, d ^ 4),
+    )
+    return [functools.partial(lambda v, p: lax.ppermute(v, AXES, p), p=pairs(c)) for c in changes]
+
+
+def after(value, *others):
+    return lax.optimization_barrier((value, *others))[0]
+
+
+def gather(shard, over_x, over_y, along_z):
+    own, x, y, xy = [shard] + [None] * 3, [None] * 4, [None] * 4, [None] * 4
+    x[0], y[0], own[1] = over_x(own[0]), over_y(own[0]), along_z(own[0])
+    own[1] = after(own[1], x[0], y[0])
+    xy[0], y[1], own[2] = over_x(y[0]), over_y(own[1]), along_z(own[1])
+    x[1], y[2], own[3] = over_x(own[1]), over_y(own[2]), along_z(own[2])
+    own[3] = after(own[3], xy[0], y[1])
+    x[3], y[3], xy[1] = over_x(own[3]), over_y(own[3]), along_z(xy[0])
+    x[2] = over_x(after(own[2], x[1]))
+    xy[3], xy[2] = over_y(x[3]), along_z(xy[1])
+    return own + y, x + xy
+
+
+def add(*values):
+    return sum(v.astype(F32) for v in values)
+
+
+def scatter(slot0, slot1, dgain, over_x, over_y, along_z):
+    own, y, x, xy = slot0[:4], slot0[4:], slot1[:4], slot1[4:]
+
+    def total(*values):
+        return add(*values).astype(BF16)
+
+    xy2, xy3, x2 = along_z(xy[2]), over_y(xy[3]), over_x(x[2])
+    c3, e1 = total(x[3], xy3), total(xy[1], xy2)
+    c3, e1, y3 = lax.optimization_barrier((c3, e1, y[3]))
+    y3, c3, e1 = over_y(y3), over_x(c3), along_z(e1)
+    s3, e0 = total(own[3], c3, y3), total(xy[0], e1)
+    y2, s3, x1 = over_y(after(y[2], xy3, x2)), along_z(s3), over_x(after(x[1], x2))
+    s2 = total(own[2], x2, y2, s3)
+    e0, y1, s2 = over_x(e0), over_y(after(y[1], y3)), along_z(s2)
+    s1, b0 = total(own[1], x1, y1, s2), total(y[0], e0)
+    s1 = after(s1, dgain)
+    return add(own[0], over_x(after(x[0], c3)), over_y(b0), along_z(s1))
+
+
+def on_chip_relay(h_forward, h_reverse, weights, gains):
+    other_core, over_x, over_y, along_z, z_near, z_far = moves_between()
+    tokens, width = h_forward.shape[2:]
+    rows, latent = weights.shape[1:]
+    x_fwd, x_rev = h_forward[0, 0], other_core(h_reverse[0, 0])
+    both_gains = jnp.concatenate([gains, over_x(gains)], axis=0)
+    shards = gather(weights[0], over_x, over_y, along_z)
+
+    one = jax.ShapeDtypeStruct((tokens, width), BF16)
+    matrix = jax.ShapeDtypeStruct((width, latent), BF16)
+    saved_c = jax.ShapeDtypeStruct((tokens, latent), F32)
+    saved_p = jax.ShapeDtypeStruct((tokens, tokens), F32)
+    dgains = jax.ShapeDtypeStruct((1, latent), F32)
+    dcs = jax.ShapeDtypeStruct((tokens, latent), BF16)
+    piece = jax.ShapeDtypeStruct((rows, latent), BF16)
+    product = 2 * tokens * width * latent
+
+    x1, x2, w, c1, p1 = (x_fwd, x_rev), [None] * 2, [None] * 2, [None] * 2, [None] * 2
+    for slot in range(2):
+        u, w[slot], c1[slot], p1[slot] = kernel_call(
+            functools.partial(first_block, slot), (*shards[slot], both_gains, x1[slot]),
+            [one, matrix, saved_c, saved_p], flops=2 * product,
+        )
+        x2[slot] = other_core(u)
+    cot, dc2, dg2 = [None] * 2, [None] * 2, [None] * 2
+    for chain in range(2):
+        e, dc2[chain], dg2[chain] = kernel_call(
+            functools.partial(second_block, chain), (both_gains, x2[chain], *w), [one, dcs, dgains],
+            [pltpu.VMEM((tokens, width), BF16), pltpu.VMEM((tokens, latent), F32)], 4 * product,
+        )
+        cot[chain] = other_core(e)
+    parts, dgain, grads = [None] * 2, [None] * 2, [None] * 2
+    dc1 = [None] * 2
+    for slot in range(2):
+        dc1[slot], dgain[slot], *parts[slot] = kernel_call(
+            functools.partial(first_weight_grad, slot),
+            (both_gains, x1[slot], c1[slot], p1[slot], cot[slot], *x2, *dc2, *dg2), [dcs, dgains] + [piece] * 8,
+            [pltpu.VMEM((width, latent), BF16), pltpu.VMEM((2 * tokens, latent), BF16)], 4 * product,
+        )
+    for slot in range(2):
+        (grads[slot],) = kernel_call(first_input_grad, (cot[slot], p1[slot], dc1[slot], w[slot]), [one], flops=2 * product)
+    dgain = dgain[0] + over_x(dgain[1])
+    dgain = dgain + over_y(dgain)
+    dgain = dgain + z_near(dgain)
+    dgain = dgain + z_far(dgain)
+    grad_weights = scatter(*parts, dgain, over_x, over_y, along_z)
+    return grads[0][None, None], other_core(grads[1])[None, None], grad_weights[None], dgain
 
 
 def from_partner(value, axis, apart):
@@ -76,7 +350,7 @@
     return passed_along(values, "section", offset)
 
 
-def on_device(h_forward, h_reverse, weights, gains):
+def sections_apart(h_forward, h_reverse, weights, gains):
     shard = weights[0]
     gain = gains[0]
     twin_shard, twin_gain = twin_copy((shard, gain))
@@ -131,6 +405,8 @@
         P("section", "dp", None),
         P("section", None),
     )
+    on_chip = (mesh.shape["section"], mesh.shape["dp"]) == (4, 8)
+    on_device = on_chip_relay if on_chip else sections_apart
     return jax.shard_map(
         on_device, mesh=mesh, in_specs=in_specs, out_specs=out_specs, check_vma=False
     )

time: 289 us -> 123 us (0.43)
  waiting for transfers between devices: 204 us -> 59.9 us
  starting transfers between devices: 9.96 us -> 42.5 us
  matrix products: 24.7 us -> 0 us
  blocking collectives: 20.6 us -> 0 us
  Pallas kernels: 0 us -> 16 us
  between operations: 14.1 us -> 0.81 us
  local copies, waits for them, and re-layouts: 12.3 us -> 0.93 us
    unnamed x6 -> x0, waiting for transfers between devices: 85 us -> none
    all_gather x2 -> x0, waiting for transfers between devices: 78.5 us -> none  [the longest x1 44.1 us: on_device(): lax.all_gather(twin_shard, 'dp', axis=0, tiled=True)]
    ppermute x12 -> x41, starting transfers between devices: 9.8 us -> 42.5 us  [moves_between(): lax.ppermute(v, AXES, p)]
    dot_general x36 -> x0, matrix products: 24.7 us -> none  [the longest x4 5.6 us: group_forward(): c = jnp.dot(x, w, preferred_element_type=jnp.float32)]
    psum x1 -> x0, blocking collectives: 20.6 us -> none  [on_device(): gsum_fwd, gsum_rev = lax.psum((dg_f1 + dg_f2, dg_r1 + dg_r2), 'dp')]
    ppermute x12 -> x41, waiting for transfers between devices: 40.8 us -> 59.9 us  [moves_between(): lax.ppermute(v, AXES, p)]
    pallas_call x0 -> x8, Pallas kernels: none -> 16 us  [kernel_call(): pl.pallas_call(body, out_shape=outs, in_specs=[local] * len(args), out_sp...]
    unnamed x31 -> x5, local copies, waits for them, and re-layouts: 12.3 us -> 0.93 us
  transfers between devices with their start and end apart: 16 -> 41, of which waited for: 11 -> 25; matrix products, arithmetic and copies ran while one was open for 9% -> 1% of each run, Pallas kernels for 0% -> 13%
where the time goes in v2:
time: 123 us
  waiting for transfers between devices  59.9 us (49%)
  starting transfers between devices  42.5 us (35%)
  Pallas kernels  16 us (13%)
  other arithmetic  2.73 us (2%)
    ppermute x41, waiting for transfers between devices, moves_between(): lax.ppermute(v, AXES, p)  59.9 us
    ppermute x41, starting transfers between devices, moves_between(): lax.ppermute(v, AXES, p)  42.5 us
    pallas_call x8, Pallas kernels, kernel_call(): pl.pallas_call(body, out_shape=outs, in_specs=[local] * len(args), out_sp...  16 us
  transfers between devices with their start and end apart: 41, of which 25 were waited for; matrix products, arithmetic and copies ran while one was open for 1% of the time, Pallas kernels for 13%

profile of v2, /device:TPU:0, one launch (start us, length us, event | category | flops | bytes accessed | tf_op | source)
XLA Modules:
  0.0 122.9 jit_solution(14763451520986253190)
XLA Ops:
  0.7 3.0 %collective-permute-start.3 = (bf16[448,256]{1,0:T(8,128)(2,1)}, bf16[448,256]{1,0:T(8,128)(2,1)S(1)}, u32[]{:S(2)}, u32[]{:S(2)}) collective-permute-start(bf16[448,256]{1,0:T(8,128)(2,1)} %bitcast.9), channel_id=1, source_target_pairs={{0,1},{1,0},{2,3},{3,2},{4,5},{5,4},{6,7},{7,6},{8,9},{9,8},{10,11... | collective-permute-start | bytes 688136 | tf_op jit(solution)/shard_map/ppermute | solution.py:191
  3.7 1.5 %collective-permute-start.2 = (bf16[448,256]{1,0:T(8,128)(2,1)}, bf16[448,256]{1,0:T(8,128)(2,1)S(1)}, u32[]{:S(2)}, u32[]{:S(2)}) collective-permute-start(bf16[448,256]{1,0:T(8,128)(2,1)} %bitcast.10), channel_id=1, source_target_pairs={{0,16},{1,17},{2,18},{3,19},{4,20},{5,21},{6,22},{7,23},{8,24},{9,... | collective-permute-start | bytes 688136 | tf_op jit(solution)/shard_map/ppermute | solution.py:191
  5.2 1.6 %collective-permute-start.1 = (bf16[448,256]{1,0:T(8,128)(2,1)}, bf16[448,256]{1,0:T(8,128)(2,1)S(1)}, u32[]{:S(2)}, u32[]{:S(2)}) collective-permute-start(bf16[448,256]{1,0:T(8,128)(2,1)} %bitcast.11), channel_id=1, source_target_pairs={{0,2},{1,3},{2,6},{3,7},{4,0},{5,1},{6,4},{7,5},{8,10},{9,11},{10,... | collective-permute-start | bytes 688136 | tf_op jit(solution)/shard_map/ppermute | solution.py:191
  6.8 2.7 %collective-permute-done.3.refs_4_ = bf16[448,256]{1,0:T(8,128)(2,1)S(1)} collective-permute-done((bf16[448,256]{1,0:T(8,128)(2,1)}, bf16[448,256]{1,0:T(8,128)(2,1)S(1)}, u32[]{:S(2)}, u32[]{:S(2)}) %collective-permute-start.3) | collective-permute-done | bytes 229408 | tf_op jit(solution)/shard_map/ppermute | solution.py:191
  9.5 1.5 %collective-permute-done.2.refs_0_ = bf16[448,256]{1,0:T(8,128)(2,1)S(1)} collective-permute-done((bf16[448,256]{1,0:T(8,128)(2,1)}, bf16[448,256]{1,0:T(8,128)(2,1)S(1)}, u32[]{:S(2)}, u32[]{:S(2)}) %collective-permute-start.2) | collective-permute-done | bytes 229408 | tf_op jit(solution)/shard_map/ppermute | solution.py:191
  11.0 2.1 %collective-permute-done.1.refs_1_ = bf16[448,256]{1,0:T(8,128)(2,1)S(1)} collective-permute-done((bf16[448,256]{1,0:T(8,128)(2,1)}, bf16[448,256]{1,0:T(8,128)(2,1)S(1)}, u32[]{:S(2)}, u32[]{:S(2)}) %collective-permute-start.1) | collective-permute-done | bytes 229408 | tf_op jit(solution)/shard_map/ppermute | solution.py:191
  15.0 5.0 %collective-permute-done.4.refs_2_ = bf16[448,256]{1,0:T(8,128)(2,1)S(1)} collective-permute-done((bf16[448,256]{1,0:T(8,128)(2,1)S(1)}, bf16[448,256]{1,0:T(8,128)(2,1)S(1)}, u32[]{:S(2)}, u32[]{:S(2)}) %collective-permute-start.4) | collective-permute-done | bytes 229408 | tf_op jit(solution)/shard_map/ppermute | solution.py:191
  21.3 1.1 collective-permute-done.6.refs_4_
  22.4 3.3 %collective-permute-start.14 = (bf16[448,256]{1,0:T(8,128)(2,1)S(1)}, bf16[448,256]{1,0:T(8,128)(2,1)S(1)}, u32[]{:S(2)}, u32[]{:S(2)}) collective-permute-start(bf16[448,256]{1,0:T(8,128)(2,1)S(1)} %collective-permute-done.6.refs_4_), channel_id=1, source_target_pairs={{0,2},{1,3},{2,6},{3,7},{4,0},{5,1},{6,4},{7,5},{8,10},{9,11},{10,... | collective-permute-start | bytes 688136 | tf_op jit(solution)/shard_map/ppermute | solution.py:191
  25.6 3.1 %collective-permute-done.5.refs_3_ = bf16[448,256]{1,0:T(8,128)(2,1)S(1)} collective-permute-done((bf16[448,256]{1,0:T(8,128)(2,1)S(1)}, bf16[448,256]{1,0:T(8,128)(2,1)S(1)}, u32[]{:S(2)}, u32[]{:S(2)}) %collective-permute-start.5) | collective-permute-done | bytes 229408 | tf_op jit(solution)/shard_map/ppermute | solution.py:191
  29.2 1.5 %collective-permute-start.12 = (bf16[448,256]{1,0:T(8,128)(2,1)S(1)}, bf16[448,256]{1,0:T(8,128)(2,1)S(1)}, u32[]{:S(2)}, u32[]{:S(2)}) collective-permute-start(bf16[448,256]{1,0:T(8,128)(2,1)S(1)} %collective-permute-done.4.refs_2_), channel_id=1, source_target_pairs={{0,16},{1,17},{2,18},{3,19},{4,20},{5,21},{6,22},{7,23},{8,24},{9,... | collective-permute-start | bytes 688136 | tf_op jit(solution)/shard_map/ppermute | solution.py:191
  30.7 1.1 collective-permute-done.14.refs_5_
  32.7 2.0 %collective-permute-done.13.refs_3_ = bf16[448,256]{1,0:T(8,128)(2,1)S(1)} collective-permute-done((bf16[448,256]{1,0:T(8,128)(2,1)S(1)}, bf16[448,256]{1,0:T(8,128)(2,1)S(1)}, u32[]{:S(2)}, u32[]{:S(2)}) %collective-permute-start.13) | collective-permute-done | bytes 229408 | tf_op jit(solution)/shard_map/ppermute | solution.py:191
  36.0 3.0 %collective-permute-done = bf16[1,256]{1,0:T(2,128)(2,1)S(1)} collective-permute-done((bf16[1,256]{1,0:T(2,128)(2,1)}, bf16[1,256]{1,0:T(2,128)(2,1)S(1)}, u32[]{:S(2)}, u32[]{:S(2)}) %collective-permute-start) | collective-permute-done | bytes 544 | tf_op jit(solution)/shard_map/ppermute | solution.py:191
  39.7 1.5 %collective-permute-start.8 = (bf16[448,256]{1,0:T(8,128)(2,1)S(1)}, bf16[448,256]{1,0:T(8,128)(2,1)S(1)}, u32[]{:S(2)}, u32[]{:S(2)}) collective-permute-start(bf16[448,256]{1,0:T(8,128)(2,1)S(1)} %collective-permute-done.4.refs_2_), channel_id=1, source_target_pairs={{0,1},{1,0},{2,3},{3,2},{4,5},{5,4},{6,7},{7,6},{8,9},{9,8},{10,11... | collective-permute-start | bytes 688136 | tf_op jit(solution)/shard_map/ppermute | solution.py:191
  41.7 1.5 %collective-permute-done.16.refs_7_ = bf16[448,256]{1,0:T(8,128)(2,1)S(1)} collective-permute-done((bf16[448,256]{1,0:T(8,128)(2,1)S(1)}, bf16[448,256]{1,0:T(8,128)(2,1)S(1)}, u32[]{:S(2)}, u32[]{:S(2)}) %collective-permute-start.16) | collective-permute-done | bytes 229408 | tf_op jit(solution)/shard_map/ppermute | solution.py:191
  43.2 1.7 %shard_map.76 = (bf16[128,3584]{1,0:T(8,128)(2,1)S(1)}, bf16[3584,256]{1,0:T(8,128)(2,1)S(1)}, f32[128,256]{1,0:T(8,128)S(1)}, f32[128,128]{1,0:T(8,128)S(1)}) custom-call(bf16[448,256]{1,0:T(8,128)(2,1)S(1)} %collective-permute-done.2.refs_0_, bf16[448,256]{1,0:T(8,128)(2,1)S(1)} %collective-permute-done.11.refs_1_, ...), custom_call_target="tpu_custom_call" | custom-call | flops 469762048 | bytes 4194304 | tf_op jit(solution)/shard_map/pallas_call | solution.py:162
  45.0 1.9 %collective-permute-done.8.refs_6_ = bf16[448,256]{1,0:T(8,128)(2,1)S(1)} collective-permute-done((bf16[448,256]{1,0:T(8,128)(2,1)S(1)}, bf16[448,256]{1,0:T(8,128)(2,1)S(1)}, u32[]{:S(2)}, u32[]{:S(2)}) %collective-permute-start.8) | collective-permute-done | bytes 229408 | tf_op jit(solution)/shard_map/ppermute | solution.py:191
  47.0 2.5 %collective-permute-done.9.refs_7_ = bf16[448,256]{1,0:T(8,128)(2,1)S(1)} collective-permute-done((bf16[448,256]{1,0:T(8,128)(2,1)S(1)}, bf16[448,256]{1,0:T(8,128)(2,1)S(1)}, u32[]{:S(2)}, u32[]{:S(2)}) %collective-permute-start.9) | collective-permute-done | bytes 229408 | tf_op jit(solution)/shard_map/ppermute | solution.py:191
  49.4 1.7 %shard_map.75 = (bf16[128,3584]{1,0:T(8,128)(2,1)S(1)}, bf16[3584,256]{1,0:T(8,128)(2,1)S(1)}, f32[128,256]{1,0:T(8,128)S(1)}, f32[128,128]{1,0:T(8,128)S(1)}) custom-call(bf16[448,256]{1,0:T(8,128)(2,1)S(1)} %bitcast.12, bf16[448,256]{1,0:T(8,128)(2,1)S(1)} %collective-permute-done.1.refs_1_, bf16[448,256]{1,0:T(8,128)(2,1)S(1)} %collective-permute-done.4.refs_2_, ...), custom_call_target="tpu_custom_call" | custom-call | flops 469762048 | bytes 4194304 | tf_op jit(solution)/shard_map/pallas_call | solution.py:162
  51.2 3.1 %shard_map.78 = (bf16[128,3584]{1,0:T(8,128)(2,1)S(1)}, bf16[128,256]{1,0:T(8,128)(2,1)S(1)}, f32[1,256]{1,0:T(1,128)S(1)}) custom-call(bf16[2,256]{1,0:T(2,128)(2,1)S(1)} %pad_maximum_fusion.refs_8_.gain_ref.refs_0_, bf16[128,3584]{1,0:T(8,128)(2,1)S(1)} %collective-permute-done.19.x_ref.refs_6_, bf16[3584,256]{1,0:T(8,128)(2,1)S(1)} %get-tuple-element.52.w0_ref.w_ref, ...), custom_call_target="tpu_custom_call" | custom-call | flops 939524096 | bytes 4194304 | tf_op jit(solution)/shard_map/pallas_call | solution.py:162
  54.8 3.0 %shard_map.77 = (bf16[128,3584]{1,0:T(8,128)(2,1)S(1)}, bf16[128,256]{1,0:T(8,128)(2,1)S(1)}, f32[1,256]{1,0:T(1,128)S(1)}) custom-call(bf16[2,256]{1,0:T(2,128)(2,1)S(1)} %pad_maximum_fusion.refs_8_.gain_ref.refs_0_, bf16[128,3584]{1,0:T(8,128)(2,1)S(1)} %collective-permute-done.10.x_ref.refs_5_, bf16[3584,256]{1,0:T(8,128)(2,1)S(1)} %get-tuple-element.52.w0_ref.w_ref, ...), custom_call_target="tpu_custom_call" | custom-call | flops 939524096 | bytes 4194304 | tf_op jit(solution)/shard_map/pallas_call | solution.py:162
  58.0 1.6 %shard_map.81 = (bf16[128,256]{1,0:T(8,128)(2,1)S(1)}, f32[1,256]{1,0:T(1,128)S(1)}, bf16[448,256]{1,0:T(8,128)(2,1)S(1)}, bf16[448,256]{1,0:T(8,128)(2,1)S(1)},...) custom-call(bf16[2,256]{1,0:T(2,128)(2,1)S(1)} %pad_maximum_fusion.r, ...), custom_call_target="tpu_custom_call" | custom-call | flops 939524096 | bytes 4194304 | tf_op jit(solution)/shard_map/pallas_call | solution.py:162
  59.6 2.9 %collective-permute-start.23 = (bf16[448,256]{1,0:T(8,128)(2,1)S(1)}, bf16[448,256]{1,0:T(8,128)(2,1)S(1)}, u32[]{:S(2)}, u32[]{:S(2)}) collective-permute-start(bf16[448,256]{1,0:T(8,128)(2,1)S(1)} %get-tuple-element.73), channel_id=1, source_target_pairs={{0,2},{1,3},{2,6},{3,7},{4,0},{5,1},{6,4},{7,5},{8,10},{9,11},{10,... | collective-permute-start | bytes 688136 | tf_op jit(solution)/shard_map/ppermute | solution.py:191
  62.6 1.8 %shard_map.79 = (bf16[128,256]{1,0:T(8,128)(2,1)S(1)}, f32[1,256]{1,0:T(1,128)S(1)}, bf16[448,256]{1,0:T(8,128)(2,1)S(1)}, bf16[448,256]{1,0:T(8,128)(2,1)S(1)},...) custom-call(bf16[2,256]{1,0:T(2,128)(2,1)S(1)} %pad_maximum_fusion.r, ...), custom_call_target="tpu_custom_call" | custom-call | flops 939524096 | bytes 4194304 | tf_op jit(solution)/shard_map/pallas_call | solution.py:162
  64.4 1.6 %collective-permute-start.22 = (bf16[448,256]{1,0:T(8,128)(2,1)S(1)}, bf16[448,256]{1,0:T(8,128)(2,1)S(1)}, u32[]{:S(2)}, u32[]{:S(2)}) collective-permute-start(bf16[448,256]{1,0:T(8,128)(2,1)S(1)} %get-tuple-element.71), channel_id=1, source_target_pairs={{0,1},{1,0},{2,3},{3,2},{4,5},{5,4},{6,7},{7,6},{8,9},{9,8},{10,11... | collective-permute-start | bytes 688136 | tf_op jit(solution)/shard_map/ppermute | solution.py:191
  66.5 2.1 %collective-permute-done.23 = bf16[448,256]{1,0:T(8,128)(2,1)S(1)} collective-permute-done((bf16[448,256]{1,0:T(8,128)(2,1)S(1)}, bf16[448,256]{1,0:T(8,128)(2,1)S(1)}, u32[]{:S(2)}, u32[]{:S(2)}) %collective-permute-start.23) | collective-permute-done | bytes 229408 | tf_op jit(solution)/shard_map/ppermute | solution.py:191
  68.6 3.5 %collective-permute-done.22 = bf16[448,256]{1,0:T(8,128)(2,1)S(1)} collective-permute-done((bf16[448,256]{1,0:T(8,128)(2,1)S(1)}, bf16[448,256]{1,0:T(8,128)(2,1)S(1)}, u32[]{:S(2)}, u32[]{:S(2)}) %collective-permute-start.22) | collective-permute-done | bytes 229408 | tf_op jit(solution)/shard_map/ppermute | solution.py:191
  72.9 1.5 %collective-permute-start.31 = (bf16[448,256]{1,0:T(8,128)(2,1)S(1)}, bf16[448,256]{1,0:T(8,128)(2,1)S(1)}, u32[]{:S(2)}, u32[]{:S(2)}) collective-permute-start(bf16[448,256]{1,0:T(8,128)(2,1)S(1)} %get-tuple-element.85), channel_id=1, source_target_pairs={{0,1},{1,0},{2,3},{3,2},{4,5},{5,4},{6,7},{7,6},{8,9},{9,8},{10,11... | collective-permute-start | bytes 688136 | tf_op jit(solution)/shard_map/ppermute | solution.py:191
  74.4 1.5 %collective-permute-start.36 = (f32[1,256]{1,0:T(1,128)S(1)}, f32[1,256]{1,0:T(1,128)S(1)}, u32[]{:S(2)}, u32[]{:S(2)}) collective-permute-start(f32[1,256]{1,0:T(1,128)S(1)} %get-tuple-element.92), channel_id=1, source_target_pairs={{0,16},{1,17},{2,18},{3,19},{4,20},{5,21},{6,22},{7,23},{8,24},{9,... | collective-permute-start | bytes 3080 | tf_op jit(solution)/shard_map/ppermute | solution.py:191
  75.9 3.4 %collective-permute-done.36 = f32[1,256]{1,0:T(1,128)S(1)} collective-permute-done((f32[1,256]{1,0:T(1,128)S(1)}, f32[1,256]{1,0:T(1,128)S(1)}, u32[]{:S(2)}, u32[]{:S(2)}) %collective-permute-start.36) | collective-permute-done | bytes 1056 | tf_op jit(solution)/shard_map/ppermute | solution.py:191
  79.3 1.5 %collective-permute-start.37 = (f32[1,256]{1,0:T(1,128)S(1)}, f32[1,256]{1,0:T(1,128)S(1)}, u32[]{:S(2)}, u32[]{:S(2)}) collective-permute-start(f32[1,256]{1,0:T(1,128)S(1)} %add.71), channel_id=1, source_target_pairs={{0,1},{1,0},{2,3},{3,2},{4,5},{5,4},{6,7},{7,6},{8,9},{9,8},{10,11... | collective-permute-start | bytes 3080 | tf_op jit(solution)/shard_map/ppermute | solution.py:191
  80.8 2.0 %collective-permute-done.37 = f32[1,256]{1,0:T(1,128)S(1)} collective-permute-done((f32[1,256]{1,0:T(1,128)S(1)}, f32[1,256]{1,0:T(1,128)S(1)}, u32[]{:S(2)}, u32[]{:S(2)}) %collective-permute-start.37) | collective-permute-done | bytes 1056 | tf_op jit(solution)/shard_map/ppermute | solution.py:191
  83.4 3.0 %collective-permute-done.38 = f32[1,256]{1,0:T(1,128)S(1)} collective-permute-done((f32[1,256]{1,0:T(1,128)S(1)}, f32[1,256]{1,0:T(1,128)S(1)}, u32[]{:S(2)}, u32[]{:S(2)}) %collective-permute-start.38) | collective-permute-done | bytes 1056 | tf_op jit(solution)/shard_map/ppermute | solution.py:191
  87.6 3.3 %collective-permute-done.39 = f32[1,256]{1,0:T(1,128)S(1)} collective-permute-done((f32[1,256]{1,0:T(1,128)S(1)}, f32[1,256]{1,0:T(1,128)S(1)}, u32[]{:S(2)}, u32[]{:S(2)}) %collective-permute-start.39) | collective-permute-done | bytes 1056 | tf_op jit(solution)/shard_map/ppermute | solution.py:191
  92.6 1.5 %collective-permute-start.33 = (bf16[448,256]{1,0:T(8,128)(2,1)S(1)}, bf16[448,256]{1,0:T(8,128)(2,1)S(1)}, u32[]{:S(2)}, u32[]{:S(2)}) collective-permute-start(bf16[448,256]{1,0:T(8,128)(2,1)S(1)} %get-tuple-element.89), channel_id=1, source_target_pairs={{0,1},{1,0},{2,3},{3,2},{4,5},{5,4},{6,7},{7,6},{8,9},{9,8},{10,11... | collective-permute-start | bytes 688136 | tf_op jit(solution)/shard_map/ppermute | solution.py:191
  94.1 1.5 %collective-permute-start.25 = (bf16[448,256]{1,0:T(8,128)(2,1)S(1)}, bf16[448,256]{1,0:T(8,128)(2,1)S(1)}, u32[]{:S(2)}, u32[]{:S(2)}) collective-permute-start(bf16[448,256]{1,0:T(8,128)(2,1)S(1)} %get-tuple-element.76), channel_id=1, source_target_pairs={{0,16},{1,17},{2,18},{3,19},{4,20},{5,21},{6,22},{7,23},{8,24},{9,... | collective-permute-start | bytes 688136 | tf_op jit(solution)/shard_map/ppermute | solution.py:191
  95.7 2.7 %collective-permute-done.26 = bf16[448,256]{1,0:T(8,128)(2,1)S(1)} collective-permute-done((bf16[448,256]{1,0:T(8,128)(2,1)S(1)}, bf16[448,256]{1,0:T(8,128)(2,1)S(1)}, u32[]{:S(2)}, u32[]{:S(2)}) %collective-permute-start.26) | collective-permute-done | bytes 229408 | tf_op jit(solution)/shard_map/ppermute | solution.py:191
  98.6 1.5 %collective-permute-start.27 = (bf16[448,256]{1,0:T(8,128)(2,1)S(1)}, bf16[448,256]{1,0:T(8,128)(2,1)S(1)}, u32[]{:S(2)}, u32[]{:S(2)}) collective-permute-start(bf16[448,256]{1,0:T(8,128)(2,1)S(1)} %add_convert_fusion.4), channel_id=1, source_target_pairs={{0,16},{1,17},{2,18},{3,19},{4,20},{5,21},{6,22},{7,23},{8,24},{9,... | collective-permute-start | bytes 688136 | tf_op jit(solution)/shard_map/ppermute | solution.py:191
  100.1 5.2 %collective-permute-done.34 = bf16[448,256]{1,0:T(8,128)(2,1)S(1)} collective-permute-done((bf16[448,256]{1,0:T(8,128)(2,1)S(1)}, bf16[448,256]{1,0:T(8,128)(2,1)S(1)}, u32[]{:S(2)}, u32[]{:S(2)}) %collective-permute-start.34) | collective-permute-done | bytes 229408 | tf_op jit(solution)/shard_map/ppermute | solution.py:191
  105.3 1.5 %collective-permute-start.32 = (bf16[448,256]{1,0:T(8,128)(2,1)S(1)}, bf16[448,256]{1,0:T(8,128)(2,1)S(1)}, u32[]{:S(2)}, u32[]{:S(2)}) collective-permute-start(bf16[448,256]{1,0:T(8,128)(2,1)S(1)} %get-tuple-element.86), channel_id=1, source_target_pairs={{0,1},{1,0},{2,3},{3,2},{4,5},{5,4},{6,7},{7,6},{8,9},{9,8},{10,11... | collective-permute-start | bytes 688136 | tf_op jit(solution)/shard_map/ppermute | solution.py:191
  107.1 2.1 %collective-permute-start.35 = (bf16[448,256]{1,0:T(8,128)(2,1)S(1)}, bf16[448,256]{1,0:T(8,128)(2,1)S(1)}, u32[]{:S(2)}, u32[]{:S(2)}) collective-permute-start(bf16[448,256]{1,0:T(8,128)(2,1)S(1)} %add_convert_fusion.1), channel_id=1, source_target_pairs={{0,2},{1,3},{2,6},{3,7},{4,0},{5,1},{6,4},{7,5},{8,10},{9,11},{10,... | collective-permute-start | bytes 688136 | tf_op jit(solution)/shard_map/ppermute | solution.py:191
  109.3 1.6 %collective-permute-start.28 = (bf16[448,256]{1,0:T(8,128)(2,1)S(1)}, bf16[448,256]{1,0:T(8,128)(2,1)S(1)}, u32[]{:S(2)}, u32[]{:S(2)}) collective-permute-start(bf16[448,256]{1,0:T(8,128)(2,1)S(1)} %add_convert_fusion.3), channel_id=1, source_target_pairs={{0,1},{1,0},{2,3},{3,2},{4,5},{5,4},{6,7},{7,6},{8,9},{9,8},{10,11... | collective-permute-start | bytes 688136 | tf_op jit(solution)/shard_map/ppermute | solution.py:191
  110.8 2.1 %collective-permute-done.32 = bf16[448,256]{1,0:T(8,128)(2,1)S(1)} collective-permute-done((bf16[448,256]{1,0:T(8,128)(2,1)S(1)}, bf16[448,256]{1,0:T(8,128)(2,1)S(1)}, u32[]{:S(2)}, u32[]{:S(2)}) %collective-permute-start.32) | collective-permute-done | bytes 229408 | tf_op jit(solution)/shard_map/ppermute | solution.py:191
  112.9 1.1 collective-permute-done.35
  114.1 1.3 %collective-permute-start.40 = (bf16[448,256]{1,0:T(8,128)(2,1)S(1)}, bf16[448,256]{1,0:T(8,128)(2,1)S(1)}, u32[]{:S(2)}, u32[]{:S(2)}) collective-permute-start(bf16[448,256]{1,0:T(8,128)(2,1)S(1)} %add_convert_fusion), channel_id=1, source_target_pairs={{0,2},{1,3},{2,6},{3,7},{4,0},{5,1},{6,4},{7,5},{8,10},{9,11},{10,... | collective-permute-start | bytes 688136 | tf_op jit(solution)/shard_map/ppermute | solution.py:191
  115.4 2.0 %shard_map.80 = bf16[128,3584]{1,0:T(8,128)(2,1)} custom-call(bf16[128,3584]{1,0:T(8,128)(2,1)S(1)} %collective-permute-done.18.refs_4_.cot_ref, f32[128,128]{1,0:T(8,128)S(1)} %get-tuple-element.56.refs_3_.p_ref, bf16[128,256]{1,0:T(8,128)(2,1)S(1)} %get-tuple-element.63.dc_ref, bf16[3584,256]{1,0:T(8,128)(2,1)S(1)} %get-tuple-element.52.w0_ref.w_ref), custom_call_target="tpu_custom_call" | custom-call | flops 469762048 | bytes 4194304 | tf_op jit(solution)/shard_map/pallas_call | solution.py:162
  117.4 3.7 %collective-permute-done.40 = bf16[448,256]{1,0:T(8,128)(2,1)S(1)} collective-permute-done((bf16[448,256]{1,0:T(8,128)(2,1)S(1)}, bf16[448,256]{1,0:T(8,128)(2,1)S(1)}, u32[]{:S(2)}, u32[]{:S(2)}) %collective-permute-start.40) | collective-permute-done | bytes 229408 | tf_op jit(solution)/shard_map/ppermute | solution.py:191
  (60 shorter events, 15.1 us)
Async XLA Ops:
  0.6 48.8 %copy-start.1 = (bf16[1,448,256]{2,1,0:T(8,128)(2,1)S(1)}, bf16[1,448,256]{2,1,0:T(8,128)(2,1)}, u32[]{:S(2)}) copy-start(bf16[1,448,256]{2,1,0:T(8,128)(2,1)} %param.6) | copy-start | bytes 688132
  0.6 48.8 %copy-start = (bf16[1,1,128,3584]{3,2,1,0:T(8,128)(2,1)S(1)}, bf16[1,1,128,3584]{3,2,1,0:T(8,128)(2,1)}, u32[]{:S(2)}) copy-start(bf16[1,1,128,3584]{3,2,1,0:T(8,128)(2,1)} %param.4) | copy-start | bytes 2752516
  0.7 8.8 %collective-permute-start.3 = (bf16[448,256]{1,0:T(8,128)(2,1)}, bf16[448,256]{1,0:T(8,128)(2,1)S(1)}, u32[]{:S(2)}, u32[]{:S(2)}) collective-permute-start(bf16[448,256]{1,0:T(8,128)(2,1)} %bitcast.9), channel_id=1, source_target_pairs={{0,1},{1,0},{2,3},{3,2},{4,5},{5,4},{6,7},{7,6},{8,9},{9,8},{10,11... | collective-permute-start | bytes 688136 | tf_op jit(solution)/shard_map/ppermute | solution.py:191
  3.7 7.3 %collective-permute-start.2 = (bf16[448,256]{1,0:T(8,128)(2,1)}, bf16[448,256]{1,0:T(8,128)(2,1)S(1)}, u32[]{:S(2)}, u32[]{:S(2)}) collective-permute-start(bf16[448,256]{1,0:T(8,128)(2,1)} %bitcast.10), channel_id=1, source_target_pairs={{0,16},{1,17},{2,18},{3,19},{4,20},{5,21},{6,22},{7,23},{8,24},{9,... | collective-permute-start | bytes 688136 | tf_op jit(solution)/shard_map/ppermute | solution.py:191
  5.2 7.9 %collective-permute-start.1 = (bf16[448,256]{1,0:T(8,128)(2,1)}, bf16[448,256]{1,0:T(8,128)(2,1)S(1)}, u32[]{:S(2)}, u32[]{:S(2)}) collective-permute-start(bf16[448,256]{1,0:T(8,128)(2,1)} %bitcast.11), channel_id=1, source_target_pairs={{0,2},{1,3},{2,6},{3,7},{4,0},{5,1},{6,4},{7,5},{8,10},{9,11},{10,... | collective-permute-start | bytes 688136 | tf_op jit(solution)/shard_map/ppermute | solution.py:191
  13.1 6.9 %collective-permute-start.4 = (bf16[448,256]{1,0:T(8,128)(2,1)S(1)}, bf16[448,256]{1,0:T(8,128)(2,1)S(1)}, u32[]{:S(2)}, u32[]{:S(2)}) collective-permute-start(bf16[448,256]{1,0:T(8,128)(2,1)S(1)} %collective-permute-done.1.refs_1_), channel_id=1, source_target_pairs={{0,2},{1,3},{2,6},{3,7},{4,0},{5,1},{6,4},{7,5},{8,10},{9,11},{10,... | collective-permute-start | bytes 688136 | tf_op jit(solution)/shard_map/ppermute | solution.py:191
  14.0 27.8 %collective-permute-start.17 = (bf16[128,3584]{1,0:T(8,128)(2,1)}, bf16[128,3584]{1,0:T(8,128)(2,1)S(1)}, u32[]{:S(2)}, u32[]{:S(2)}) collective-permute-start(bf16[128,3584]{1,0:T(8,128)(2,1)} %bitcast.15), channel_id=1, source_target_pairs={{0,8},{1,9},{2,10},{3,11},{4,12},{5,13},{6,14},{7,15},{8,0},{9,1},... | collective-permute-start | bytes 2752520 | tf_op jit(solution)/shard_map/ppermute | solution.py:191
  14.0 8.4 %collective-permute-start.6 = (bf16[448,256]{1,0:T(8,128)(2,1)S(1)}, bf16[448,256]{1,0:T(8,128)(2,1)S(1)}, u32[]{:S(2)}, u32[]{:S(2)}) collective-permute-start(bf16[448,256]{1,0:T(8,128)(2,1)S(1)} %collective-permute-done.3.refs_4_), channel_id=1, source_target_pairs={{0,16},{1,17},{2,18},{3,19},{4,20},{5,21},{6,22},{7,23},{8,24},{9,... | collective-permute-start | bytes 688136 | tf_op jit(solution)/shard_map/ppermute | solution.py:191
  14.5 11.1 %collective-permute-start.7 = (bf16[448,256]{1,0:T(8,128)(2,1)S(1)}, bf16[448,256]{1,0:T(8,128)(2,1)S(1)}, u32[]{:S(2)}, u32[]{:S(2)}) collective-permute-start(bf16[448,256]{1,0:T(8,128)(2,1)S(1)} %collective-permute-done.1.refs_1_), channel_id=1, source_target_pairs={{0,1},{1,0},{2,3},{3,2},{4,5},{5,4},{6,7},{7,6},{8,9},{9,8},{10,11... | collective-permute-start | bytes 688136 | tf_op jit(solution)/shard_map/ppermute | solution.py:191
  20.0 8.7 %collective-permute-start.5 = (bf16[448,256]{1,0:T(8,128)(2,1)S(1)}, bf16[448,256]{1,0:T(8,128)(2,1)S(1)}, u32[]{:S(2)}, u32[]{:S(2)}) collective-permute-start(bf16[448,256]{1,0:T(8,128)(2,1)S(1)} %collective-permute-done.4.refs_2_), channel_id=1, source_target_pairs={{0,2},{1,3},{2,6},{3,7},{4,0},{5,1},{6,4},{7,5},{8,10},{9,11},{10,... | collective-permute-start | bytes 688136 | tf_op jit(solution)/shard_map/ppermute | solution.py:191
  20.8 8.5 %collective-permute-start.11 = (bf16[448,256]{1,0:T(8,128)(2,1)S(1)}, bf16[448,256]{1,0:T(8,128)(2,1)S(1)}, u32[]{:S(2)}, u32[]{:S(2)}) collective-permute-start(bf16[448,256]{1,0:T(8,128)(2,1)S(1)} %collective-permute-done.1.refs_1_), channel_id=1, source_target_pairs={{0,16},{1,17},{2,18},{3,19},{4,20},{5,21},{6,22},{7,23},{8,24},{9,... | collective-permute-start | bytes 688136 | tf_op jit(solution)/shard_map/ppermute | solution.py:191
  22.4 9.5 %collective-permute-start.14 = (bf16[448,256]{1,0:T(8,128)(2,1)S(1)}, bf16[448,256]{1,0:T(8,128)(2,1)S(1)}, u32[]{:S(2)}, u32[]{:S(2)}) collective-permute-start(bf16[448,256]{1,0:T(8,128)(2,1)S(1)} %collective-permute-done.6.refs_4_), channel_id=1, source_target_pairs={{0,2},{1,3},{2,6},{3,7},{4,0},{5,1},{6,4},{7,5},{8,10},{9,11},{10,... | collective-permute-start | bytes 688136 | tf_op jit(solution)/shard_map/ppermute | solution.py:191
  28.7 6.0 %collective-permute-start.13 = (bf16[448,256]{1,0:T(8,128)(2,1)S(1)}, bf16[448,256]{1,0:T(8,128)(2,1)S(1)}, u32[]{:S(2)}, u32[]{:S(2)}) collective-permute-start(bf16[448,256]{1,0:T(8,128)(2,1)S(1)} %collective-permute-done.5.refs_3_), channel_id=1, source_target_pairs={{0,16},{1,17},{2,18},{3,19},{4,20},{5,21},{6,22},{7,23},{8,24},{9,... | collective-permute-start | bytes 688136 | tf_op jit(solution)/shard_map/ppermute | solution.py:191
  29.2 12.0 %collective-permute-start.12 = (bf16[448,256]{1,0:T(8,128)(2,1)S(1)}, bf16[448,256]{1,0:T(8,128)(2,1)S(1)}, u32[]{:S(2)}, u32[]{:S(2)}) collective-permute-start(bf16[448,256]{1,0:T(8,128)(2,1)S(1)} %collective-permute-done.4.refs_2_), channel_id=1, source_target_pairs={{0,16},{1,17},{2,18},{3,19},{4,20},{5,21},{6,22},{7,23},{8,24},{9,... | collective-permute-start | bytes 688136 | tf_op jit(solution)/shard_map/ppermute | solution.py:191
  31.8 9.9 %collective-permute-start.15 = (bf16[448,256]{1,0:T(8,128)(2,1)S(1)}, bf16[448,256]{1,0:T(8,128)(2,1)S(1)}, u32[]{:S(2)}, u32[]{:S(2)}) collective-permute-start(bf16[448,256]{1,0:T(8,128)(2,1)S(1)} %collective-permute-done.14.refs_5_), channel_id=1, source_target_pairs={{0,2},{1,3},{2,6},{3,7},{4,0},{5,1},{6,4},{7,5},{8,10},{9,11},{10,... | collective-permute-start | bytes 688136 | tf_op jit(solution)/shard_map/ppermute | solution.py:191
  34.7 8.5 %collective-permute-start.16 = (bf16[448,256]{1,0:T(8,128)(2,1)S(1)}, bf16[448,256]{1,0:T(8,128)(2,1)S(1)}, u32[]{:S(2)}, u32[]{:S(2)}) collective-permute-start(bf16[448,256]{1,0:T(8,128)(2,1)S(1)} %collective-permute-done.13.refs_3_), channel_id=1, source_target_pairs={{0,1},{1,0},{2,3},{3,2},{4,5},{5,4},{6,7},{7,6},{8,9},{9,8},{10,11... | collective-permute-start | bytes 688136 | tf_op jit(solution)/shard_map/ppermute | solution.py:191
  35.2 3.8 %collective-permute-start = (bf16[1,256]{1,0:T(2,128)(2,1)}, bf16[1,256]{1,0:T(2,128)(2,1)S(1)}, u32[]{:S(2)}, u32[]{:S(2)}) collective-permute-start(bf16[1,256]{1,0:T(2,128)(2,1)} %param.7), channel_id=1, source_target_pairs={{0,16},{1,17},{2,18},{3,19},{4,20},{5,21},{6,22},{7,23},{8,24},{9,... | collective-permute-start | bytes 1544 | tf_op jit(solution)/shard_map/ppermute | solution.py:191
  39.7 7.3 %collective-permute-start.8 = (bf16[448,256]{1,0:T(8,128)(2,1)S(1)}, bf16[448,256]{1,0:T(8,128)(2,1)S(1)}, u32[]{:S(2)}, u32[]{:S(2)}) collective-permute-start(bf16[448,256]{1,0:T(8,128)(2,1)S(1)} %collective-permute-done.4.refs_2_), channel_id=1, source_target_pairs={{0,1},{1,0},{2,3},{3,2},{4,5},{5,4},{6,7},{7,6},{8,9},{9,8},{10,11... | collective-permute-start | bytes 688136 | tf_op jit(solution)/shard_map/ppermute | solution.py:191
  41.2 8.2 %collective-permute-start.9 = (bf16[448,256]{1,0:T(8,128)(2,1)S(1)}, bf16[448,256]{1,0:T(8,128)(2,1)S(1)}, u32[]{:S(2)}, u32[]{:S(2)}) collective-permute-start(bf16[448,256]{1,0:T(8,128)(2,1)S(1)} %collective-permute-done.5.refs_3_), channel_id=1, source_target_pairs={{0,1},{1,0},{2,3},{3,2},{4,5},{5,4},{6,7},{7,6},{8,9},{9,8},{10,11... | collective-permute-start | bytes 688136 | tf_op jit(solution)/shard_map/ppermute | solution.py:191
  44.9 6.3 %collective-permute-start.19 = (bf16[128,3584]{1,0:T(8,128)(2,1)S(1)}, bf16[128,3584]{1,0:T(8,128)(2,1)S(1)}, u32[]{:S(2)}, u32[]{:S(2)}) collective-permute-start(bf16[128,3584]{1,0:T(8,128)(2,1)S(1)} %get-tuple-element.58), channel_id=1, source_target_pairs={{0,8},{1,9},{2,10},{3,11},{4,12},{5,13},{6,14},{7,15},{8,0},{9,1},... | collective-permute-start | bytes 2752520 | tf_op jit(solution)/shard_map/ppermute | solution.py:191
  51.1 3.7 %collective-permute-start.10 = (bf16[128,3584]{1,0:T(8,128)(2,1)S(1)}, bf16[128,3584]{1,0:T(8,128)(2,1)S(1)}, u32[]{:S(2)}, u32[]{:S(2)}) collective-permute-start(bf16[128,3584]{1,0:T(8,128)(2,1)S(1)} %get-tuple-element.51), channel_id=1, source_target_pairs={{0,8},{1,9},{2,10},{3,11},{4,12},{5,13},{6,14},{7,15},{8,0},{9,1},... | collective-permute-start | bytes 2752520 | tf_op jit(solution)/shard_map/ppermute | solution.py:191
  54.3 3.7 %collective-permute-start.20 = (bf16[128,3584]{1,0:T(8,128)(2,1)S(1)}, bf16[128,3584]{1,0:T(8,128)(2,1)S(1)}, u32[]{:S(2)}, u32[]{:S(2)}) collective-permute-start(bf16[128,3584]{1,0:T(8,128)(2,1)S(1)} %get-tuple-element.64), channel_id=1, source_target_pairs={{0,8},{1,9},{2,10},{3,11},{4,12},{5,13},{6,14},{7,15},{8,0},{9,1},... | collective-permute-start | bytes 2752520 | tf_op jit(solution)/shard_map/ppermute | solution.py:191
  57.9 4.7 %collective-permute-start.18 = (bf16[128,3584]{1,0:T(8,128)(2,1)S(1)}, bf16[128,3584]{1,0:T(8,128)(2,1)S(1)}, u32[]{:S(2)}, u32[]{:S(2)}) collective-permute-start(bf16[128,3584]{1,0:T(8,128)(2,1)S(1)} %get-tuple-element.55), channel_id=1, source_target_pairs={{0,8},{1,9},{2,10},{3,11},{4,12},{5,13},{6,14},{7,15},{8,0},{9,1},... | collective-permute-start | bytes 2752520 | tf_op jit(solution)/shard_map/ppermute | solution.py:191
  59.6 9.0 %collective-permute-start.23 = (bf16[448,256]{1,0:T(8,128)(2,1)S(1)}, bf16[448,256]{1,0:T(8,128)(2,1)S(1)}, u32[]{:S(2)}, u32[]{:S(2)}) collective-permute-start(bf16[448,256]{1,0:T(8,128)(2,1)S(1)} %get-tuple-element.73), channel_id=1, source_target_pairs={{0,2},{1,3},{2,6},{3,7},{4,0},{5,1},{6,4},{7,5},{8,10},{9,11},{10,... | collective-permute-start | bytes 688136 | tf_op jit(solution)/shard_map/ppermute | solution.py:191
  64.4 7.8 %collective-permute-start.22 = (bf16[448,256]{1,0:T(8,128)(2,1)S(1)}, bf16[448,256]{1,0:T(8,128)(2,1)S(1)}, u32[]{:S(2)}, u32[]{:S(2)}) collective-permute-start(bf16[448,256]{1,0:T(8,128)(2,1)S(1)} %get-tuple-element.71), channel_id=1, source_target_pairs={{0,1},{1,0},{2,3},{3,2},{4,5},{5,4},{6,7},{7,6},{8,9},{9,8},{10,11... | collective-permute-start | bytes 688136 | tf_op jit(solution)/shard_map/ppermute | solution.py:191
  66.0 26.0 %collective-permute-start.29 = (bf16[448,256]{1,0:T(8,128)(2,1)S(1)}, bf16[448,256]{1,0:T(8,128)(2,1)S(1)}, u32[]{:S(2)}, u32[]{:S(2)}) collective-permute-start(bf16[448,256]{1,0:T(8,128)(2,1)S(1)} %get-tuple-element.82), channel_id=1, source_target_pairs={{0,16},{1,17},{2,18},{3,19},{4,20},{5,21},{6,22},{7,23},{8,24},{9,... | collective-permute-start | bytes 688136 | tf_op jit(solution)/shard_map/ppermute | solution.py:191
  72.3 20.3 %collective-permute-start.24 = (bf16[448,256]{1,0:T(8,128)(2,1)S(1)}, bf16[448,256]{1,0:T(8,128)(2,1)S(1)}, u32[]{:S(2)}, u32[]{:S(2)}) collective-permute-start(bf16[448,256]{1,0:T(8,128)(2,1)S(1)} %add_convert_fusion.6), channel_id=1, source_target_pairs={{0,16},{1,17},{2,18},{3,19},{4,20},{5,21},{6,22},{7,23},{8,24},{9,... | collective-permute-start | bytes 688136 | tf_op jit(solution)/shard_map/ppermute | solution.py:191
  72.9 21.2 %collective-permute-start.31 = (bf16[448,256]{1,0:T(8,128)(2,1)S(1)}, bf16[448,256]{1,0:T(8,128)(2,1)S(1)}, u32[]{:S(2)}, u32[]{:S(2)}) collective-permute-start(bf16[448,256]{1,0:T(8,128)(2,1)S(1)} %get-tuple-element.85), channel_id=1, source_target_pairs={{0,1},{1,0},{2,3},{3,2},{4,5},{5,4},{6,7},{7,6},{8,9},{9,8},{10,11... | collective-permute-start | bytes 688136 | tf_op jit(solution)/shard_map/ppermute | solution.py:191
  74.4 4.9 %collective-permute-start.36 = (f32[1,256]{1,0:T(1,128)S(1)}, f32[1,256]{1,0:T(1,128)S(1)}, u32[]{:S(2)}, u32[]{:S(2)}) collective-permute-start(f32[1,256]{1,0:T(1,128)S(1)} %get-tuple-element.92), channel_id=1, source_target_pairs={{0,16},{1,17},{2,18},{3,19},{4,20},{5,21},{6,22},{7,23},{8,24},{9,... | collective-permute-start | bytes 3080 | tf_op jit(solution)/shard_map/ppermute | solution.py:191
  79.3 3.6 %collective-permute-start.37 = (f32[1,256]{1,0:T(1,128)S(1)}, f32[1,256]{1,0:T(1,128)S(1)}, u32[]{:S(2)}, u32[]{:S(2)}) collective-permute-start(f32[1,256]{1,0:T(1,128)S(1)} %add.71), channel_id=1, source_target_pairs={{0,1},{1,0},{2,3},{3,2},{4,5},{5,4},{6,7},{7,6},{8,9},{9,8},{10,11... | collective-permute-start | bytes 3080 | tf_op jit(solution)/shard_map/ppermute | solution.py:191
  82.8 3.6 %collective-permute-start.38 = (f32[1,256]{1,0:T(1,128)S(1)}, f32[1,256]{1,0:T(1,128)S(1)}, u32[]{:S(2)}, u32[]{:S(2)}) collective-permute-start(f32[1,256]{1,0:T(1,128)S(1)} %add.72), channel_id=1, source_target_pairs={{0,2},{1,3},{2,0},{3,1},{4,6},{5,7},{6,4},{7,5},{8,10},{9,11},{10,... | collective-permute-start | bytes 3080 | tf_op jit(solution)/shard_map/ppermute | solution.py:191
  86.4 4.5 %collective-permute-start.39 = (f32[1,256]{1,0:T(1,128)S(1)}, f32[1,256]{1,0:T(1,128)S(1)}, u32[]{:S(2)}, u32[]{:S(2)}) collective-permute-start(f32[1,256]{1,0:T(1,128)S(1)} %add.73), channel_id=1, source_target_pairs={{0,4},{1,5},{2,6},{3,7},{4,0},{5,1},{6,2},{7,3},{8,12},{9,13},{10,... | collective-permute-start | bytes 3080 | tf_op jit(solution)/shard_map/ppermute | solution.py:191
  87.5 29.9 %collective-permute-start.21 = (bf16[128,3584]{1,0:T(8,128)(2,1)S(1)}, bf16[128,3584]{1,0:T(8,128)(2,1)S(1)}, u32[]{:S(2)}, u32[]{:S(2)}) collective-permute-start(bf16[128,3584]{1,0:T(8,128)(2,1)S(1)} %shard_map.82), channel_id=1, source_target_pairs={{0,8},{1,9},{2,10},{3,11},{4,12},{5,13},{6,14},{7,15},{8,0},{9,1},... | collective-permute-start | bytes 2752520 | tf_op jit(solution)/shard_map/ppermute | solution.py:191
  91.5 6.9 %collective-permute-start.26 = (bf16[448,256]{1,0:T(8,128)(2,1)S(1)}, bf16[448,256]{1,0:T(8,128)(2,1)S(1)}, u32[]{:S(2)}, u32[]{:S(2)}) collective-permute-start(bf16[448,256]{1,0:T(8,128)(2,1)S(1)} %add_convert_fusion.5), channel_id=1, source_target_pairs={{0,2},{1,3},{2,6},{3,7},{4,0},{5,1},{6,4},{7,5},{8,10},{9,11},{10,... | collective-permute-start | bytes 688136 | tf_op jit(solution)/shard_map/ppermute | solution.py:191
  92.0 17.2 %collective-permute-start.30 = (bf16[448,256]{1,0:T(8,128)(2,1)S(1)}, bf16[448,256]{1,0:T(8,128)(2,1)S(1)}, u32[]{:S(2)}, u32[]{:S(2)}) collective-permute-start(bf16[448,256]{1,0:T(8,128)(2,1)S(1)} %get-tuple-element.83), channel_id=1, source_target_pairs={{0,16},{1,17},{2,18},{3,19},{4,20},{5,21},{6,22},{7,23},{8,24},{9,... | collective-permute-start | bytes 688136 | tf_op jit(solution)/shard_map/ppermute | solution.py:191
  92.6 6.0 %collective-permute-start.33 = (bf16[448,256]{1,0:T(8,128)(2,1)S(1)}, bf16[448,256]{1,0:T(8,128)(2,1)S(1)}, u32[]{:S(2)}, u32[]{:S(2)}) collective-permute-start(bf16[448,256]{1,0:T(8,128)(2,1)S(1)} %get-tuple-element.89), channel_id=1, source_target_pairs={{0,1},{1,0},{2,3},{3,2},{4,5},{5,4},{6,7},{7,6},{8,9},{9,8},{10,11... | collective-permute-start | bytes 688136 | tf_op jit(solution)/shard_map/ppermute | solution.py:191
  94.1 23.3 %collective-permute-start.25 = (bf16[448,256]{1,0:T(8,128)(2,1)S(1)}, bf16[448,256]{1,0:T(8,128)(2,1)S(1)}, u32[]{:S(2)}, u32[]{:S(2)}) collective-permute-start(bf16[448,256]{1,0:T(8,128)(2,1)S(1)} %get-tuple-element.76), channel_id=1, source_target_pairs={{0,16},{1,17},{2,18},{3,19},{4,20},{5,21},{6,22},{7,23},{8,24},{9,... | collective-permute-start | bytes 688136 | tf_op jit(solution)/shard_map/ppermute | solution.py:191
  98.4 6.9 %collective-permute-start.34 = (bf16[448,256]{1,0:T(8,128)(2,1)S(1)}, bf16[448,256]{1,0:T(8,128)(2,1)S(1)}, u32[]{:S(2)}, u32[]{:S(2)}) collective-permute-start(bf16[448,256]{1,0:T(8,128)(2,1)S(1)} %add_convert_fusion.2), channel_id=1, source_target_pairs={{0,2},{1,3},{2,6},{3,7},{4,0},{5,1},{6,4},{7,5},{8,10},{9,11},{10,... | collective-permute-start | bytes 688136 | tf_op jit(solution)/shard_map/ppermute | solution.py:191
  98.6 8.4 %collective-permute-start.27 = (bf16[448,256]{1,0:T(8,128)(2,1)S(1)}, bf16[448,256]{1,0:T(8,128)(2,1)S(1)}, u32[]{:S(2)}, u32[]{:S(2)}) collective-permute-start(bf16[448,256]{1,0:T(8,128)(2,1)S(1)} %add_convert_fusion.4), channel_id=1, source_target_pairs={{0,16},{1,17},{2,18},{3,19},{4,20},{5,21},{6,22},{7,23},{8,24},{9,... | collective-permute-start | bytes 688136 | tf_op jit(solution)/shard_map/ppermute | solution.py:191
  105.3 7.6 %collective-permute-start.32 = (bf16[448,256]{1,0:T(8,128)(2,1)S(1)}, bf16[448,256]{1,0:T(8,128)(2,1)S(1)}, u32[]{:S(2)}, u32[]{:S(2)}) collective-permute-start(bf16[448,256]{1,0:T(8,128)(2,1)S(1)} %get-tuple-element.86), channel_id=1, source_target_pairs={{0,1},{1,0},{2,3},{3,2},{4,5},{5,4},{6,7},{7,6},{8,9},{9,8},{10,11... | collective-permute-start | bytes 688136 | tf_op jit(solution)/shard_map/ppermute | solution.py:191
  107.1 6.9 %collective-permute-start.35 = (bf16[448,256]{1,0:T(8,128)(2,1)S(1)}, bf16[448,256]{1,0:T(8,128)(2,1)S(1)}, u32[]{:S(2)}, u32[]{:S(2)}) collective-permute-start(bf16[448,256]{1,0:T(8,128)(2,1)S(1)} %add_convert_fusion.1), channel_id=1, source_target_pairs={{0,2},{1,3},{2,6},{3,7},{4,0},{5,1},{6,4},{7,5},{8,10},{9,11},{10,... | collective-permute-start | bytes 688136 | tf_op jit(solution)/shard_map/ppermute | solution.py:191
  109.3 8.1 %collective-permute-start.28 = (bf16[448,256]{1,0:T(8,128)(2,1)S(1)}, bf16[448,256]{1,0:T(8,128)(2,1)S(1)}, u32[]{:S(2)}, u32[]{:S(2)}) collective-permute-start(bf16[448,256]{1,0:T(8,128)(2,1)S(1)} %add_convert_fusion.3), channel_id=1, source_target_pairs={{0,1},{1,0},{2,3},{3,2},{4,5},{5,4},{6,7},{7,6},{8,9},{9,8},{10,11... | collective-permute-start | bytes 688136 | tf_op jit(solution)/shard_map/ppermute | solution.py:191
  114.1 7.0 %collective-permute-start.40 = (bf16[448,256]{1,0:T(8,128)(2,1)S(1)}, bf16[448,256]{1,0:T(8,128)(2,1)S(1)}, u32[]{:S(2)}, u32[]{:S(2)}) collective-permute-start(bf16[448,256]{1,0:T(8,128)(2,1)S(1)} %add_convert_fusion), channel_id=1, source_target_pairs={{0,2},{1,3},{2,6},{3,7},{4,0},{5,1},{6,4},{7,5},{8,10},{9,11},{10,... | collective-permute-start | bytes 688136 | tf_op jit(solution)/shard_map/ppermute | solution.py:191

commit v3 on v2

--- a/solution.py
+++ b/solution.py
@@ -12,6 +12,7 @@
 BF16 = jnp.bfloat16
 F32 = jnp.float32
 CHUNK = 512
+TAIL = 16
 VMEM_LIMIT = 40 * 1024 * 1024
 
 
@@ -130,9 +131,8 @@
 
 def first_weight_grad(slot, *refs):
     gain_ref, x_ref, c_ref, p_ref, cot_ref, x2a_ref, x2b_ref, dc2a_ref, dc2b_ref, dg2a_ref, dg2b_ref = refs[:11]
-    dc_ref, dg_ref = refs[11:13]
-    pieces, (dw_ref, dcs_ref) = refs[13:21], refs[21:]
-    tokens, rows = x_ref.shape[0], pieces[0].shape[0]
+    dc_ref, pieces, (dw_ref, dcs_ref, dg_ref) = refs[11], refs[12:20], refs[20:]
+    tokens, rows = x_ref.shape[0], pieces[0].shape[0] - TAIL
     g = gain_ref[slot : slot + 1, :]
     c, probs = c_ref[...], p_ref[...]
     inv, normed = latent_norm(c, g)
@@ -149,25 +149,100 @@
                 x = jnp.concatenate([x_ref[:, cols], x2_ref[:, cols]], axis=0)
                 dw_ref[cols, :] = matmul_tn(x, dcs_ref[...]).astype(BF16)
 
+    tail = split_tail(dg_ref[...])
     for at, piece in enumerate(pieces):
-        piece[...] = dw_ref[pl.ds(shard_row(at // 4, at % 4, rows), rows), :]
+        piece[:rows, :] = dw_ref[pl.ds(shard_row(at // 4, 4 - at % 4, rows), rows), :]
+        piece[rows:, :] = tail
+
+
+def split_tail(dgain):
+    high = dgain.astype(BF16).astype(F32)
+    at = lax.broadcasted_iota(jnp.int32, (TAIL, dgain.shape[-1]), 0)
+    return jnp.where(at == 0, high, jnp.where(at == 1, dgain - high, 0.0)).astype(BF16)
+
+
+def sum_rows(refs):
+    return sum(ref[:-TAIL, :].astype(F32) for ref in refs)
+
+
+def sum_tail(refs):
+    tail = sum(ref[-TAIL:, :].astype(F32) for ref in refs)
+    return tail[0:1, :] + tail[1:2, :]
+
+
+def partial_sum(*refs):
+    *ins, out_ref = refs
+    out_ref[:-TAIL, :] = sum_rows(ins).astype(BF16)
+    out_ref[-TAIL:, :] = split_tail(sum_tail(ins))
+
+
+def final_sum(*refs):
+    *ins, out_ref, dg_ref = refs
+    out_ref[...] = sum_rows(ins)
+    dg_ref[...] = sum_tail(ins)
 
 
 def first_input_grad(cot_ref, p_ref, dc_ref, w_ref, out_ref):
     input_grad(out_ref, cot_ref, p_ref[...].astype(BF16), dc_ref[...], w_ref)
 
 
-def kernel_call(body, args, outs, scratch=(), flops=0):
+def store(value_ref, out_ref):
+    pltpu.sync_copy(value_ref, out_ref)
+
+
+def kernel_call(body, args, outs, scratch=(), flops=0, out_space=pltpu.VMEM):
     local = pl.BlockSpec(memory_space=pltpu.VMEM)
     return pl.pallas_call(
         body,
         out_shape=outs,
         in_specs=[local] * len(args),
-        out_specs=[local] * len(outs),
+        out_specs=[pl.BlockSpec(memory_space=out_space)] * len(outs),
         scratch_shapes=scratch,
         compiler_params=pltpu.CompilerParams(vmem_limit_bytes=VMEM_LIMIT),
+        name=getattr(body, "func", body).__name__,
         cost_estimate=pl.CostEstimate(flops=flops, bytes_accessed=4 << 20, transcendentals=0),
     )(*args)
+
+
+GATHER = (
+    ("Y0", "y", "O0", ()),
+    ("O3", "r", "O0", ()),
+    ("X0", "x", "O0", ()),
+    ("O1", "z", "O0", ()),
+    ("D0", "x", "Y0", ("G", "H")),
+    ("Y3", "y", "O3", ()),
+    ("O2", "r", "O3", ("Y0",)),
+    ("X3", "x", "O3", ("Y0",)),
+    ("Y1", "y", "O1", ("X0", "O3", "Y0")),
+    ("D1", "z", "D0", ("X0", "O3", "Y0")),
+    ("X1", "x", "O1", ("X0", "O3", "Y0")),
+    ("Y2", "y", "O2", ("D0", "O1", "X0")),
+    ("D3", "r", "D0", ("Y3", "O1", "X0")),
+    ("X2", "x", "O2", ("Y3", "D0", "O1")),
+    ("D2", "z", "D1", ("Y1", "X3", "O2")),
+)
+SCATTER = (
+    ("D2", "z", "D1", ()),
+    ("Y2", "y", "O2", ()),
+    ("D3", "x", "Y3", ()),
+    ("R", "", "", ()),
+    ("Y1", "y", "O1", ()),
+    ("X2", "x", "O2", ()),
+    ("D1", "z", "D0", ()),
+    ("Y3", "y", "O3", ("D2",)),
+    ("X3", "x", "O3", ("D3", "Y2", "D2")),
+    ("O2", "z", "O1", ("R", "D3", "D2")),
+    ("D0", "y", "X0", ("Y1", "R", "D3")),
+    ("X1", "x", "O1", ("X2", "Y1", "R")),
+    ("F", "", "", ("D1", "X2", "Y1")),
+    ("O3", "r", "O0", ("D1", "X2", "Y1")),
+    ("Y0", "y", "O0", ("Y3", "D1", "X2")),
+    ("X0", "x", "O0", ("F", "X3", "Y3")),
+    ("O1", "z", "O0", ("F", "X3", "Y3")),
+)
+FIRST_AFTER = ("D3", "Y2")
+PLACES = tuple(tuple(column + str(k) for column in columns for k in range(4)) for columns in ("OY", "XD"))
+BACK = {"x": "x", "y": "y", "z": "r", "r": "z"}
 
 
 def moves_between():
@@ -180,64 +255,55 @@
         return found
 
     following = {0: 1, 1: 3, 3: 2, 2: 0}
-    changes = (
-        lambda s, d: (s ^ 1, d),
-        lambda s, d: (s ^ 2, d),
-        lambda s, d: (s, d ^ 1),
-        lambda s, d: (s, following[d >> 1] * 2 + (d & 1)),
-        lambda s, d: (s, d ^ 2),
-        lambda s, d: (s, d ^ 4),
-    )
-    return [functools.partial(lambda v, p: lax.ppermute(v, AXES, p), p=pairs(c)) for c in changes]
-
-
-def after(value, *others):
-    return lax.optimization_barrier((value, *others))[0]
-
-
-def gather(shard, over_x, over_y, along_z):
-    own, x, y, xy = [shard] + [None] * 3, [None] * 4, [None] * 4, [None] * 4
-    x[0], y[0], own[1] = over_x(own[0]), over_y(own[0]), along_z(own[0])
-    own[1] = after(own[1], x[0], y[0])
-    xy[0], y[1], own[2] = over_x(y[0]), over_y(own[1]), along_z(own[1])
-    x[1], y[2], own[3] = over_x(own[1]), over_y(own[2]), along_z(own[2])
-    own[3] = after(own[3], xy[0], y[1])
-    x[3], y[3], xy[1] = over_x(own[3]), over_y(own[3]), along_z(xy[0])
-    x[2] = over_x(after(own[2], x[1]))
-    xy[3], xy[2] = over_y(x[3]), along_z(xy[1])
-    return own + y, x + xy
-
-
-def add(*values):
-    return sum(v.astype(F32) for v in values)
-
-
-def scatter(slot0, slot1, dgain, over_x, over_y, along_z):
-    own, y, x, xy = slot0[:4], slot0[4:], slot1[:4], slot1[4:]
-
-    def total(*values):
-        return add(*values).astype(BF16)
-
-    xy2, xy3, x2 = along_z(xy[2]), over_y(xy[3]), over_x(x[2])
-    c3, e1 = total(x[3], xy3), total(xy[1], xy2)
-    c3, e1, y3 = lax.optimization_barrier((c3, e1, y[3]))
-    y3, c3, e1 = over_y(y3), over_x(c3), along_z(e1)
-    s3, e0 = total(own[3], c3, y3), total(xy[0], e1)
-    y2, s3, x1 = over_y(after(y[2], xy3, x2)), along_z(s3), over_x(after(x[1], x2))
-    s2 = total(own[2], x2, y2, s3)
-    e0, y1, s2 = over_x(e0), over_y(after(y[1], y3)), along_z(s2)
-    s1, b0 = total(own[1], x1, y1, s2), total(y[0], e0)
-    s1 = after(s1, dgain)
-    return add(own[0], over_x(after(x[0], c3)), over_y(b0), along_z(s1))
+    last = {after: before for before, after in following.items()}
+    changes = {
+        "core": lambda s, d: (s ^ 1, d),
+        "x": lambda s, d: (s ^ 2, d),
+        "y": lambda s, d: (s, d ^ 1),
+        "z": lambda s, d: (s, following[d >> 1] * 2 + (d & 1)),
+        "r": lambda s, d: (s, last[d >> 1] * 2 + (d & 1)),
+    }
+    return {name: functools.partial(lambda v, p: lax.ppermute(v, AXES, p), p=pairs(c)) for name, c in changes.items()}
+
+
+def after(value, others):
+    return lax.optimization_barrier((value, *others))[0] if others else value
+
+
+def gather(held, moves):
+    for place, way, source, earlier in GATHER:
+        held[place] = moves[way](after(held[source], [held[name] for name in earlier]))
+
+
+def scatter(parts, beside, moves):
+    rows, latent = parts["O0"].shape
+    piece = jax.ShapeDtypeStruct((rows, latent), BF16)
+    sums = [jax.ShapeDtypeStruct((rows - TAIL, latent), F32), jax.ShapeDtypeStruct((1, latent), F32)]
+    into, held = {}, {}
+    for place, _, source, _ in SCATTER:
+        into.setdefault(source, []).append(place)
+    for place, way, _, earlier in SCATTER:
+        earlier = [held[name] for name in earlier]
+        if place in beside:
+            held[place] = beside[place](earlier)
+            continue
+        value = parts[place]
+        if place in into:
+            value = kernel_call(partial_sum, (value, *[held[name] for name in into[place]]), [piece])[0]
+        held[place] = moves[BACK[way]](after(value, earlier))
+    sums = kernel_call(final_sum, (parts["O0"], *[held[name] for name in into["O0"]]), sums)
+    return sums, held
 
 
 def on_chip_relay(h_forward, h_reverse, weights, gains):
-    other_core, over_x, over_y, along_z, z_near, z_far = moves_between()
+    moves = moves_between()
+    other_core = moves["core"]
     tokens, width = h_forward.shape[2:]
     rows, latent = weights.shape[1:]
     x_fwd, x_rev = h_forward[0, 0], other_core(h_reverse[0, 0])
-    both_gains = jnp.concatenate([gains, over_x(gains)], axis=0)
-    shards = gather(weights[0], over_x, over_y, along_z)
+    both_gains = jnp.concatenate([gains, moves["x"](gains)], axis=0)
+    held = {"O0": weights[0], "G": both_gains, "H": x_rev}
+    gather(held, moves)
 
     one = jax.ShapeDtypeStruct((tokens, width), BF16)
     matrix = jax.ShapeDtypeStruct((width, latent), BF16)
@@ -245,39 +311,43 @@
     saved_p = jax.ShapeDtypeStruct((tokens, tokens), F32)
     dgains = jax.ShapeDtypeStruct((1, latent), F32)
     dcs = jax.ShapeDtypeStruct((tokens, latent), BF16)
-    piece = jax.ShapeDtypeStruct((rows, latent), BF16)
+    piece = jax.ShapeDtypeStruct((rows + TAIL, latent), BF16)
     product = 2 * tokens * width * latent
 
     x1, x2, w, c1, p1 = (x_fwd, x_rev), [None] * 2, [None] * 2, [None] * 2, [None] * 2
     for slot in range(2):
+        gain = after(both_gains, [c1[0]] if slot else [held[name] for name in FIRST_AFTER])
         u, w[slot], c1[slot], p1[slot] = kernel_call(
-            functools.partial(first_block, slot), (*shards[slot], both_gains, x1[slot]),
+            functools.partial(first_block, slot), (*[held[name] for name in PLACES[slot]], gain, x1[slot]),
             [one, matrix, saved_c, saved_p], flops=2 * product,
         )
         x2[slot] = other_core(u)
     cot, dc2, dg2 = [None] * 2, [None] * 2, [None] * 2
     for chain in range(2):
+        gain = after(both_gains, [dc2[0]] if chain else [])
         e, dc2[chain], dg2[chain] = kernel_call(
-            functools.partial(second_block, chain), (both_gains, x2[chain], *w), [one, dcs, dgains],
+            functools.partial(second_block, chain), (gain, x2[chain], *w), [one, dcs, dgains],
             [pltpu.VMEM((tokens, width), BF16), pltpu.VMEM((tokens, latent), F32)], 4 * product,
         )
         cot[chain] = other_core(e)
-    parts, dgain, grads = [None] * 2, [None] * 2, [None] * 2
-    dc1 = [None] * 2
+    parts, dc1 = [None] * 2, [None] * 2
     for slot in range(2):
-        dc1[slot], dgain[slot], *parts[slot] = kernel_call(
+        dc1[slot], *parts[slot] = kernel_call(
             functools.partial(first_weight_grad, slot),
-            (both_gains, x1[slot], c1[slot], p1[slot], cot[slot], *x2, *dc2, *dg2), [dcs, dgains] + [piece] * 8,
-            [pltpu.VMEM((width, latent), BF16), pltpu.VMEM((2 * tokens, latent), BF16)], 4 * product,
+            (both_gains, x1[slot], c1[slot], p1[slot], cot[slot], *x2, *dc2, *dg2), [dcs] + [piece] * 8,
+            [pltpu.VMEM((width, latent), BF16), pltpu.VMEM((2 * tokens, latent), BF16), pltpu.VMEM((1, latent), F32)],
+            4 * product,
         )
-    for slot in range(2):
-        (grads[slot],) = kernel_call(first_input_grad, (cot[slot], p1[slot], dc1[slot], w[slot]), [one], flops=2 * product)
-    dgain = dgain[0] + over_x(dgain[1])
-    dgain = dgain + over_y(dgain)
-    dgain = dgain + z_near(dgain)
-    dgain = dgain + z_far(dgain)
-    grad_weights = scatter(*parts, dgain, over_x, over_y, along_z)
-    return grads[0][None, None], other_core(grads[1])[None, None], grad_weights[None], dgain
+
+    def input_grads(slot, earlier):
+        args = (after(cot[slot], earlier), p1[slot], dc1[slot], w[slot])
+        (grad,) = kernel_call(first_input_grad, args, [one], flops=2 * product)
+        return kernel_call(store, (other_core(grad),), [one], out_space=pl.ANY)[0] if slot else grad
+
+    beside = {"F": functools.partial(input_grads, 0), "R": functools.partial(input_grads, 1)}
+    parts = {name: part for slot in range(2) for name, part in zip(PLACES[slot], parts[slot])}
+    (grad_weights, dgain), held = scatter(parts, beside, moves)
+    return held["F"][None, None], held["R"][None, None], grad_weights[None], dgain
 
 
 def from_partner(value, axis, apart):

time: 123 us -> 93.2 us (0.76)
  waiting for transfers between devices: 59.9 us -> 23.6 us
  starting transfers between devices: 42.5 us -> 47.5 us
  Pallas kernels: 16 us -> 18.3 us
  other arithmetic: 2.73 us -> 0.69 us
    ppermute x41 -> x37, waiting for transfers between devices: 59.9 us -> 23.6 us  [moves_between(): lax.ppermute(v, AXES, p)]
    ppermute x41 -> x37, starting transfers between devices: 42.5 us -> 47.5 us  [moves_between(): lax.ppermute(v, AXES, p)]
    pallas_call x8 -> x17, Pallas kernels: 16 us -> 18.3 us  [kernel_call(): pl.pallas_call(body, out_shape=outs, in_specs=[local] * len(args), out_sp...]
  transfers between devices with their start and end apart: 41 -> 37, of which waited for: 25 -> 15; matrix products, arithmetic and copies ran while one was open for 1% -> 1% of each run, Pallas kernels for 13% -> 15%
where the time goes in v3:
time: 93.2 us; the launch traced here: 93 us
  starting transfers between devices  47.5 us (51%)
  waiting for transfers between devices  23.6 us (25%)
  Pallas kernels  18.3 us (20%)
  local copies, waits for them, and re-layouts  2.12 us (2%)
    ppermute x37, starting transfers between devices, moves_between(): lax.ppermute(v, AXES, p)  47.5 us
    ppermute x37, waiting for transfers between devices, moves_between(): lax.ppermute(v, AXES, p)  23.6 us
    pallas_call x17, Pallas kernels, kernel_call(): pl.pallas_call(body, out_shape=outs, in_specs=[local] * len(args), out_sp...  18.3 us
    unnamed x6, local copies, waits for them, and re-layouts  2.12 us
  transfers between devices with their start and end apart: 37, of which 15 were waited for; matrix products, arithmetic and copies ran while one was open for 1% of the time, Pallas kernels for 15%

profile of v3, /device:TPU:0, one launch (start us, length us, event | category | flops | bytes accessed | tf_op | source)
XLA Modules:
  0.0 93.0 jit_solution(14956758301054472284)
XLA Ops:
  1.1 2.6 %collective-permute-start.3 = (bf16[448,256]{1,0:T(8,128)(2,1)}, bf16[448,256]{1,0:T(8,128)(2,1)S(1)}, u32[]{:S(2)}, u32[]{:S(2)}) collective-permute-start(bf16[448,256]{1,0:T(8,128)(2,1)} %bitcast.8), channel_id=1, source_target_pairs={{0,1},{1,0},{2,3},{3,2},{4,5},{5,4},{6,7},{7,6},{8,9},{9,8},{10,11... | collective-permute-start | bytes 688136 | tf_op jit(solution)/shard_map/ppermute | solution.py:266
  3.7 1.5 %collective-permute-start = (bf16[1,256]{1,0:T(2,128)(2,1)}, bf16[1,256]{1,0:T(2,128)(2,1)S(1)}, u32[]{:S(2)}, u32[]{:S(2)}) collective-permute-start(bf16[1,256]{1,0:T(2,128)(2,1)} %param.7), channel_id=1, source_target_pairs={{0,16},{1,17},{2,18},{3,19},{4,20},{5,21},{6,22},{7,23},{8,24},{9,... | collective-permute-start | bytes 1544 | tf_op jit(solution)/shard_map/ppermute | solution.py:266
  5.2 2.6 %collective-permute-start.2 = (bf16[448,256]{1,0:T(8,128)(2,1)}, bf16[448,256]{1,0:T(8,128)(2,1)S(1)}, u32[]{:S(2)}, u32[]{:S(2)}) collective-permute-start(bf16[448,256]{1,0:T(8,128)(2,1)} %bitcast.9), channel_id=1, source_target_pairs={{0,4},{1,5},{2,0},{3,1},{4,6},{5,7},{6,2},{7,3},{8,12},{9,13},{10,... | collective-permute-start | bytes 688136 | tf_op jit(solution)/shard_map/ppermute | solution.py:266
  7.8 1.2 %collective-permute-start.5 = (bf16[448,256]{1,0:T(8,128)(2,1)}, bf16[448,256]{1,0:T(8,128)(2,1)S(1)}, u32[]{:S(2)}, u32[]{:S(2)}) collective-permute-start(bf16[448,256]{1,0:T(8,128)(2,1)} %bitcast.11), channel_id=1, source_target_pairs={{0,16},{1,17},{2,18},{3,19},{4,20},{5,21},{6,22},{7,23},{8,24},{9,... | collective-permute-start | bytes 688136 | tf_op jit(solution)/shard_map/ppermute | solution.py:266
  9.0 0.7 pad_maximum_fusion.refs_8_.gain_ref.refs_0_
  10.2 1.7 %collective-permute-start.8 = (bf16[448,256]{1,0:T(8,128)(2,1)S(1)}, bf16[448,256]{1,0:T(8,128)(2,1)S(1)}, u32[]{:S(2)}, u32[]{:S(2)}) collective-permute-start(bf16[448,256]{1,0:T(8,128)(2,1)S(1)} %collective-permute-done.3.refs_4_), channel_id=1, source_target_pairs={{0,16},{1,17},{2,18},{3,19},{4,20},{5,21},{6,22},{7,23},{8,24},{9,... | collective-permute-start | bytes 688136 | tf_op jit(solution)/shard_map/ppermute | solution.py:266
  11.9 2.3 %collective-permute-done.2.refs_3_ = bf16[448,256]{1,0:T(8,128)(2,1)S(1)} collective-permute-done((bf16[448,256]{1,0:T(8,128)(2,1)}, bf16[448,256]{1,0:T(8,128)(2,1)S(1)}, u32[]{:S(2)}, u32[]{:S(2)}) %collective-permute-start.2) | collective-permute-done | bytes 229408 | tf_op jit(solution)/shard_map/ppermute | solution.py:266
  14.2 3.3 %collective-permute-start.4 = (bf16[448,256]{1,0:T(8,128)(2,1)S(1)}, bf16[448,256]{1,0:T(8,128)(2,1)S(1)}, u32[]{:S(2)}, u32[]{:S(2)}) collective-permute-start(bf16[448,256]{1,0:T(8,128)(2,1)S(1)} %collective-permute-done.2.refs_3_), channel_id=1, source_target_pairs={{0,4},{1,5},{2,0},{3,1},{4,6},{5,7},{6,2},{7,3},{8,12},{9,13},{10,... | collective-permute-start | bytes 688136 | tf_op jit(solution)/shard_map/ppermute | solution.py:266
  18.0 2.8 %collective-permute-done.1.refs_1_ = bf16[448,256]{1,0:T(8,128)(2,1)S(1)} collective-permute-done((bf16[448,256]{1,0:T(8,128)(2,1)}, bf16[448,256]{1,0:T(8,128)(2,1)S(1)}, u32[]{:S(2)}, u32[]{:S(2)}) %collective-permute-start.1) | collective-permute-done | bytes 229408 | tf_op jit(solution)/shard_map/ppermute | solution.py:266
  21.9 0.7 collective-permute-start.16
  22.5 1.7 %collective-permute-done.4.refs_2_ = bf16[448,256]{1,0:T(8,128)(2,1)S(1)} collective-permute-done((bf16[448,256]{1,0:T(8,128)(2,1)S(1)}, bf16[448,256]{1,0:T(8,128)(2,1)S(1)}, u32[]{:S(2)}, u32[]{:S(2)}) %collective-permute-start.4) | collective-permute-done | bytes 229408 | tf_op jit(solution)/shard_map/ppermute | solution.py:266
  24.8 2.5 %collective-permute-start.11 = (bf16[448,256]{1,0:T(8,128)(2,1)S(1)}, bf16[448,256]{1,0:T(8,128)(2,1)S(1)}, u32[]{:S(2)}, u32[]{:S(2)}) collective-permute-start(bf16[448,256]{1,0:T(8,128)(2,1)S(1)} %collective-permute-done.8.refs_4_), channel_id=1, source_target_pairs={{0,4},{1,5},{2,0},{3,1},{4,6},{5,7},{6,2},{7,3},{8,12},{9,13},{10,... | collective-permute-start | bytes 688136 | tf_op jit(solution)/shard_map/ppermute | solution.py:266
  27.3 2.6 %collective-permute-done.6.refs_5_ = bf16[448,256]{1,0:T(8,128)(2,1)S(1)} collective-permute-done((bf16[448,256]{1,0:T(8,128)(2,1)S(1)}, bf16[448,256]{1,0:T(8,128)(2,1)S(1)}, u32[]{:S(2)}, u32[]{:S(2)}) %collective-permute-start.6) | collective-permute-done | bytes 229408 | tf_op jit(solution)/shard_map/ppermute | solution.py:266
  29.9 1.5 %collective-permute-start.13 = (bf16[448,256]{1,0:T(8,128)(2,1)S(1)}, bf16[448,256]{1,0:T(8,128)(2,1)S(1)}, u32[]{:S(2)}, u32[]{:S(2)}) collective-permute-start(bf16[448,256]{1,0:T(8,128)(2,1)S(1)} %collective-permute-done.1.refs_1_), channel_id=1, source_target_pairs={{0,16},{1,17},{2,18},{3,19},{4,20},{5,21},{6,22},{7,23},{8,24},{9,... | collective-permute-start | bytes 688136 | tf_op jit(solution)/shard_map/ppermute | solution.py:266
  31.9 2.6 %collective-permute-start.17 = (bf16[448,256]{1,0:T(8,128)(2,1)S(1)}, bf16[448,256]{1,0:T(8,128)(2,1)S(1)}, u32[]{:S(2)}, u32[]{:S(2)}) collective-permute-start(bf16[448,256]{1,0:T(8,128)(2,1)S(1)} %collective-permute-done.16.refs_5_), channel_id=1, source_target_pairs={{0,2},{1,3},{2,6},{3,7},{4,0},{5,1},{6,4},{7,5},{8,10},{9,11},{10,... | collective-permute-start | bytes 688136 | tf_op jit(solution)/shard_map/ppermute | solution.py:266
  34.5 1.3 %collective-permute-done.11.refs_7_ = bf16[448,256]{1,0:T(8,128)(2,1)S(1)} collective-permute-done((bf16[448,256]{1,0:T(8,128)(2,1)S(1)}, bf16[448,256]{1,0:T(8,128)(2,1)S(1)}, u32[]{:S(2)}, u32[]{:S(2)}) %collective-permute-start.11) | collective-permute-done | bytes 229408 | tf_op jit(solution)/shard_map/ppermute | solution.py:266
  35.8 1.2 %copy-done = bf16[1,1,128,3584]{3,2,1,0:T(8,128)(2,1)S(1)} copy-done((bf16[1,1,128,3584]{3,2,1,0:T(8,128)(2,1)S(1)}, bf16[1,1,128,3584]{3,2,1,0:T(8,128)(2,1)}, u32[]{:S(2)}) %copy-start) | copy-done | bytes 917528
  37.0 0.9 %copy-done.2 = bf16[1,448,256]{2,1,0:T(8,128)(2,1)S(1)} copy-done((bf16[1,448,256]{2,1,0:T(8,128)(2,1)S(1)}, bf16[1,448,256]{2,1,0:T(8,128)(2,1)}, u32[]{:S(2)}) %copy-start.2) | copy-done | bytes 229400
  37.9 1.7 %first_block.2 = (bf16[128,3584]{1,0:T(8,128)(2,1)S(1)}, bf16[3584,256]{1,0:T(8,128)(2,1)S(1)}, f32[128,256]{1,0:T(8,128)S(1)}, f32[128,128]{1,0:T(8,128)S(1)}) custom-call(bf16[448,256]{1,0:T(8,128)(2,1)S(1)} %bitcast.12, bf16[448,256]{1,0:T(8,128)(2,1)S(1)} %collective-permute-done.1.refs_1_, bf16[448,256]{1,0:T(8,128)(2,1)S(1)} %collective-permute-done.4.refs_2_, ...), custom_call_target="tpu_custom_call" | custom-call | flops 469762048 | bytes 4194304 | tf_op jit(solution)/shard_map/first_block/pallas_call | solution.py:195
  39.7 1.7 %first_block.3 = (bf16[128,3584]{1,0:T(8,128)(2,1)S(1)}, bf16[3584,256]{1,0:T(8,128)(2,1)S(1)}, f32[128,256]{1,0:T(8,128)S(1)}, f32[128,128]{1,0:T(8,128)S(1)}) custom-call(bf16[448,256]{1,0:T(8,128)(2,1)S(1)} %collective-permute-done.5.refs_0_, bf16[448,256]{1,0:T(8,128)(2,1)S(1)} %collective-permute-done.13.refs_1_, ...), custom_call_target="tpu_custom_call" | custom-call | flops 469762048 | bytes 4194304 | tf_op jit(solution)/shard_map/first_block/pallas_call | solution.py:195
  42.2 3.1 %second_block.2 = (bf16[128,3584]{1,0:T(8,128)(2,1)S(1)}, bf16[128,256]{1,0:T(8,128)(2,1)S(1)}, f32[1,256]{1,0:T(1,128)S(1)}) custom-call(bf16[2,256]{1,0:T(2,128)(2,1)S(1)} %pad_maximum_fusion.refs_8_.gain_ref.refs_0_, bf16[128,3584]{1,0:T(8,128)(2,1)S(1)} %collective-permute-done.12.x_ref.refs_5_, bf16[3584,256]{1,0:T(8,128)(2,1)S(1)} %get-tuple-element.66.w0_ref.w_ref, ...), custom_call_target="tpu_custom_call" | custom-call | flops 939524096 | bytes 4194304 | tf_op jit(solution)/shard_map/second_block/pallas_call | solution.py:195
  45.2 3.1 %second_block.3 = (bf16[128,3584]{1,0:T(8,128)(2,1)S(1)}, bf16[128,256]{1,0:T(8,128)(2,1)S(1)}, f32[1,256]{1,0:T(1,128)S(1)}) custom-call(bf16[2,256]{1,0:T(2,128)(2,1)S(1)} %pad_maximum_fusion.refs_8_.gain_ref.refs_0_, bf16[128,3584]{1,0:T(8,128)(2,1)S(1)} %collective-permute-done.19.x_ref.refs_6_, bf16[3584,256]{1,0:T(8,128)(2,1)S(1)} %get-tuple-element.66.w0_ref.w_ref, ...), custom_call_target="tpu_custom_call" | custom-call | flops 939524096 | bytes 4194304 | tf_op jit(solution)/shard_map/second_block/pallas_call | solution.py:195
  48.9 2.0 %collective-permute-done.20.refs_4_.cot_ref = bf16[128,3584]{1,0:T(8,128)(2,1)S(1)} collective-permute-done((bf16[128,3584]{1,0:T(8,128)(2,1)S(1)}, bf16[128,3584]{1,0:T(8,128)(2,1)S(1)}, u32[]{:S(2)}, u32[]{:S(2)}) %collective-permute-start.20) | collective-permute-done | bytes 917536 | tf_op jit(solution)/shard_map/ppermute | solution.py:266
  50.8 1.6 %first_weight_grad.2 = (bf16[128,256]{1,0:T(8,128)(2,1)S(1)}, bf16[464,256]{1,0:T(8,128)(2,1)S(1)}, bf16[464,256]{1,0:T(8,128)(2,1)S(1)}, bf16[464,256]{1,0:T(8,...) custom-call(bf16[2,256]{1,0:T(2,128)(2,1)S(1)} %pad_maximum_fusion.r, ...), custom_call_target="tpu_custom_call" | custom-call | flops 939524096 | bytes 4194304 | tf_op jit(solution)/shard_map/first_weight_grad/pallas_call | solution.py:195
  52.5 1.0 %first_input_grad.3 = bf16[128,3584]{1,0:T(8,128)(2,1)S(1)} custom-call(bf16[128,3584]{1,0:T(8,128)(2,1)S(1)} %collective-permute-done.20.refs_4_.cot_ref, f32[128,128]{1,0:T(8,128)S(1)} %get-tuple-element.75.refs_3_.p_ref, bf16[128,256]{1,0:T(8,128)(2,1)S(1)} %get-tuple-element.90.dc_ref, bf16[3584,256]{1,0:T(8,128)(2,1)S(1)} %get-tuple-element.72.w1_ref.w_ref), custom_call_target="tpu_custom_call" | custom-call | flops 469762048 | bytes 4194304 | tf_op jit(solution)/shard_map/first_input_grad/pallas_call | solution.py:195
  53.8 2.4 %collective-permute-start.21 = (bf16[464,256]{1,0:T(8,128)(2,1)S(1)}, bf16[464,256]{1,0:T(8,128)(2,1)S(1)}, u32[]{:S(2)}, u32[]{:S(2)}) collective-permute-start(bf16[464,256]{1,0:T(8,128)(2,1)S(1)} %get-tuple-element.84), channel_id=1, source_target_pairs={{0,4},{1,5},{2,0},{3,1},{4,6},{5,7},{6,2},{7,3},{8,12},{9,13},{10,... | collective-permute-start | bytes 712712 | tf_op jit(solution)/shard_map/ppermute | solution.py:266
  56.1 1.5 %collective-permute-start.26 = (bf16[464,256]{1,0:T(8,128)(2,1)S(1)}, bf16[464,256]{1,0:T(8,128)(2,1)S(1)}, u32[]{:S(2)}, u32[]{:S(2)}) collective-permute-start(bf16[464,256]{1,0:T(8,128)(2,1)S(1)} %get-tuple-element.94), channel_id=1, source_target_pairs={{0,16},{1,17},{2,18},{3,19},{4,20},{5,21},{6,22},{7,23},{8,24},{9,... | collective-permute-start | bytes 712712 | tf_op jit(solution)/shard_map/ppermute | solution.py:266
  57.6 1.6 %first_weight_grad.3 = (bf16[128,256]{1,0:T(8,128)(2,1)S(1)}, bf16[464,256]{1,0:T(8,128)(2,1)S(1)}, bf16[464,256]{1,0:T(8,128)(2,1)S(1)}, bf16[464,256]{1,0:T(8,...) custom-call(bf16[2,256]{1,0:T(2,128)(2,1)S(1)} %pad_maximum_fusion.r, ...), custom_call_target="tpu_custom_call" | custom-call | flops 939524096 | bytes 4194304 | tf_op jit(solution)/shard_map/first_weight_grad/pallas_call | solution.py:195
  59.2 0.9 collective-permute-start.28
  60.1 0.5 collective-permute-start.23
  60.7 2.0 %collective-permute-done.21.refs_1_ = bf16[464,256]{1,0:T(8,128)(2,1)S(1)} collective-permute-done((bf16[464,256]{1,0:T(8,128)(2,1)S(1)}, bf16[464,256]{1,0:T(8,128)(2,1)S(1)}, u32[]{:S(2)}, u32[]{:S(2)}) %collective-permute-start.21) | collective-permute-done | bytes 237600 | tf_op jit(solution)/shard_map/ppermute | solution.py:266
  62.7 0.8 collective-permute-start.24
  63.5 1.2 %collective-permute-done.26.refs_1_ = bf16[464,256]{1,0:T(8,128)(2,1)S(1)} collective-permute-done((bf16[464,256]{1,0:T(8,128)(2,1)S(1)}, bf16[464,256]{1,0:T(8,128)(2,1)S(1)}, u32[]{:S(2)}, u32[]{:S(2)}) %collective-permute-start.26) | collective-permute-done | bytes 237600 | tf_op jit(solution)/shard_map/ppermute | solution.py:266
  64.8 2.9 %collective-permute-start.22 = (bf16[464,256]{1,0:T(8,128)(2,1)S(1)}, bf16[464,256]{1,0:T(8,128)(2,1)S(1)}, u32[]{:S(2)}, u32[]{:S(2)}) collective-permute-start(bf16[464,256]{1,0:T(8,128)(2,1)S(1)} %partial_sum.7), channel_id=1, source_target_pairs={{0,4},{1,5},{2,0},{3,1},{4,6},{5,7},{6,2},{7,3},{8,12},{9,13},{10,... | collective-permute-start | bytes 712712 | tf_op jit(solution)/shard_map/ppermute | solution.py:266
  68.0 0.8 collective-permute-start.27
  68.9 1.5 %collective-permute-start.29 = (bf16[464,256]{1,0:T(8,128)(2,1)S(1)}, bf16[464,256]{1,0:T(8,128)(2,1)S(1)}, u32[]{:S(2)}, u32[]{:S(2)}) collective-permute-start(bf16[464,256]{1,0:T(8,128)(2,1)S(1)} %get-tuple-element.98), channel_id=1, source_target_pairs={{0,16},{1,17},{2,18},{3,19},{4,20},{5,21},{6,22},{7,23},{8,24},{9,... | collective-permute-start | bytes 712712 | tf_op jit(solution)/shard_map/ppermute | solution.py:266
  70.4 0.9 store.1
  71.4 1.7 %collective-permute-done.24.refs_1_ = bf16[464,256]{1,0:T(8,128)(2,1)S(1)} collective-permute-done((bf16[464,256]{1,0:T(8,128)(2,1)S(1)}, bf16[464,256]{1,0:T(8,128)(2,1)S(1)}, u32[]{:S(2)}, u32[]{:S(2)}) %collective-permute-start.24) | collective-permute-done | bytes 237600 | tf_op jit(solution)/shard_map/ppermute | solution.py:266
  73.1 3.5 %collective-permute-start.34 = (bf16[464,256]{1,0:T(8,128)(2,1)S(1)}, bf16[464,256]{1,0:T(8,128)(2,1)S(1)}, u32[]{:S(2)}, u32[]{:S(2)}) collective-permute-start(bf16[464,256]{1,0:T(8,128)(2,1)S(1)} %partial_sum.12), channel_id=1, source_target_pairs={{0,4},{1,5},{2,0},{3,1},{4,6},{5,7},{6,2},{7,3},{8,12},{9,13},{10,... | collective-permute-start | bytes 712712 | tf_op jit(solution)/shard_map/ppermute | solution.py:266
  76.6 0.9 collective-permute-start.32
  77.5 1.2 %collective-permute-start.31 = (bf16[464,256]{1,0:T(8,128)(2,1)S(1)}, bf16[464,256]{1,0:T(8,128)(2,1)S(1)}, u32[]{:S(2)}, u32[]{:S(2)}) collective-permute-start(bf16[464,256]{1,0:T(8,128)(2,1)S(1)} %get-tuple-element.101), channel_id=1, source_target_pairs={{0,1},{1,0},{2,3},{3,2},{4,5},{5,4},{6,7},{7,6},{8,9},{9,8},{10,11... | collective-permute-start | bytes 712712 | tf_op jit(solution)/shard_map/ppermute | solution.py:266
  78.8 1.2 %collective-permute-start.30 = (bf16[464,256]{1,0:T(8,128)(2,1)S(1)}, bf16[464,256]{1,0:T(8,128)(2,1)S(1)}, u32[]{:S(2)}, u32[]{:S(2)}) collective-permute-start(bf16[464,256]{1,0:T(8,128)(2,1)S(1)} %partial_sum.9), channel_id=1, source_target_pairs={{0,2},{1,3},{2,6},{3,7},{4,0},{5,1},{6,4},{7,5},{8,10},{9,11},{10,... | collective-permute-start | bytes 712712 | tf_op jit(solution)/shard_map/ppermute | solution.py:266
  80.1 2.0 %first_input_grad.2 = bf16[128,3584]{1,0:T(8,128)(2,1)} custom-call(bf16[128,3584]{1,0:T(8,128)(2,1)S(1)} %collective-permute-done.18.refs_4_.cot_ref, f32[128,128]{1,0:T(8,128)S(1)} %get-tuple-element.86.refs_3_.p_ref, bf16[128,256]{1,0:T(8,128)(2,1)S(1)} %get-tuple-element.89.dc_ref, bf16[3584,256]{1,0:T(8,128)(2,1)S(1)} %get-tuple-element.66.w0_ref.w_ref), custom_call_target="tpu_custom_call" | custom-call | flops 469762048 | bytes 4194304 | tf_op jit(solution)/shard_map/first_input_grad/pallas_call | solution.py:195
  82.3 3.5 %collective-permute-start.36 = (bf16[464,256]{1,0:T(8,128)(2,1)S(1)}, bf16[464,256]{1,0:T(8,128)(2,1)S(1)}, u32[]{:S(2)}, u32[]{:S(2)}) collective-permute-start(bf16[464,256]{1,0:T(8,128)(2,1)S(1)} %partial_sum.13), channel_id=1, source_target_pairs={{0,4},{1,5},{2,0},{3,1},{4,6},{5,7},{6,2},{7,3},{8,12},{9,13},{10,... | collective-permute-start | bytes 712712 | tf_op jit(solution)/shard_map/ppermute | solution.py:266
  85.9 1.2 %collective-permute-start.33 = (bf16[464,256]{1,0:T(8,128)(2,1)S(1)}, bf16[464,256]{1,0:T(8,128)(2,1)S(1)}, u32[]{:S(2)}, u32[]{:S(2)}) collective-permute-start(bf16[464,256]{1,0:T(8,128)(2,1)S(1)} %partial_sum.11), channel_id=1, source_target_pairs={{0,16},{1,17},{2,18},{3,19},{4,20},{5,21},{6,22},{7,23},{8,24},{9,... | collective-permute-start | bytes 712712 | tf_op jit(solution)/shard_map/ppermute | solution.py:266
  87.1 2.3 %collective-permute-done.30.refs_1_ = bf16[464,256]{1,0:T(8,128)(2,1)S(1)} collective-permute-done((bf16[464,256]{1,0:T(8,128)(2,1)S(1)}, bf16[464,256]{1,0:T(8,128)(2,1)S(1)}, u32[]{:S(2)}, u32[]{:S(2)}) %collective-permute-start.30) | collective-permute-done | bytes 237600 | tf_op jit(solution)/shard_map/ppermute | solution.py:266
  89.5 2.6 %collective-permute-done.36.refs_4_ = bf16[464,256]{1,0:T(8,128)(2,1)S(1)} collective-permute-done((bf16[464,256]{1,0:T(8,128)(2,1)S(1)}, bf16[464,256]{1,0:T(8,128)(2,1)S(1)}, u32[]{:S(2)}, u32[]{:S(2)}) %collective-permute-start.36) | collective-permute-done | bytes 237600 | tf_op jit(solution)/shard_map/ppermute | solution.py:266
  92.1 0.9 final_sum.1
  (50 shorter events, 6.1 us)
Async XLA Ops:
  0.6 9.5 %collective-permute-start.7 = (bf16[128,3584]{1,0:T(8,128)(2,1)}, bf16[128,3584]{1,0:T(8,128)(2,1)S(1)}, u32[]{:S(2)}, u32[]{:S(2)}) collective-permute-start(bf16[128,3584]{1,0:T(8,128)(2,1)} %bitcast.15), channel_id=1, source_target_pairs={{0,8},{1,9},{2,10},{3,11},{4,12},{5,13},{6,14},{7,15},{8,0},{9,1},... | collective-permute-start | bytes 2752520 | tf_op jit(solution)/shard_map/ppermute | solution.py:266
  1.1 9.0 %collective-permute-start.3 = (bf16[448,256]{1,0:T(8,128)(2,1)}, bf16[448,256]{1,0:T(8,128)(2,1)S(1)}, u32[]{:S(2)}, u32[]{:S(2)}) collective-permute-start(bf16[448,256]{1,0:T(8,128)(2,1)} %bitcast.8), channel_id=1, source_target_pairs={{0,1},{1,0},{2,3},{3,2},{4,5},{5,4},{6,7},{7,6},{8,9},{9,8},{10,11... | collective-permute-start | bytes 688136 | tf_op jit(solution)/shard_map/ppermute | solution.py:266
  3.7 4.1 %collective-permute-start = (bf16[1,256]{1,0:T(2,128)(2,1)}, bf16[1,256]{1,0:T(2,128)(2,1)S(1)}, u32[]{:S(2)}, u32[]{:S(2)}) collective-permute-start(bf16[1,256]{1,0:T(2,128)(2,1)} %param.7), channel_id=1, source_target_pairs={{0,16},{1,17},{2,18},{3,19},{4,20},{5,21},{6,22},{7,23},{8,24},{9,... | collective-permute-start | bytes 1544 | tf_op jit(solution)/shard_map/ppermute | solution.py:266
  5.2 9.0 %collective-permute-start.2 = (bf16[448,256]{1,0:T(8,128)(2,1)}, bf16[448,256]{1,0:T(8,128)(2,1)S(1)}, u32[]{:S(2)}, u32[]{:S(2)}) collective-permute-start(bf16[448,256]{1,0:T(8,128)(2,1)} %bitcast.9), channel_id=1, source_target_pairs={{0,4},{1,5},{2,0},{3,1},{4,6},{5,7},{6,2},{7,3},{8,12},{9,13},{10,... | collective-permute-start | bytes 688136 | tf_op jit(solution)/shard_map/ppermute | solution.py:266
  7.8 13.0 %collective-permute-start.1 = (bf16[448,256]{1,0:T(8,128)(2,1)}, bf16[448,256]{1,0:T(8,128)(2,1)S(1)}, u32[]{:S(2)}, u32[]{:S(2)}) collective-permute-start(bf16[448,256]{1,0:T(8,128)(2,1)} %bitcast.10), channel_id=1, source_target_pairs={{0,2},{1,3},{2,6},{3,7},{4,0},{5,1},{6,4},{7,5},{8,10},{9,11},{10,... | collective-permute-start | bytes 688136 | tf_op jit(solution)/shard_map/ppermute | solution.py:266
  7.8 13.5 %collective-permute-start.5 = (bf16[448,256]{1,0:T(8,128)(2,1)}, bf16[448,256]{1,0:T(8,128)(2,1)S(1)}, u32[]{:S(2)}, u32[]{:S(2)}) collective-permute-start(bf16[448,256]{1,0:T(8,128)(2,1)} %bitcast.11), channel_id=1, source_target_pairs={{0,16},{1,17},{2,18},{3,19},{4,20},{5,21},{6,22},{7,23},{8,24},{9,... | collective-permute-start | bytes 688136 | tf_op jit(solution)/shard_map/ppermute | solution.py:266
  10.2 11.7 %collective-permute-start.8 = (bf16[448,256]{1,0:T(8,128)(2,1)S(1)}, bf16[448,256]{1,0:T(8,128)(2,1)S(1)}, u32[]{:S(2)}, u32[]{:S(2)}) collective-permute-start(bf16[448,256]{1,0:T(8,128)(2,1)S(1)} %collective-permute-done.3.refs_4_), channel_id=1, source_target_pairs={{0,16},{1,17},{2,18},{3,19},{4,20},{5,21},{6,22},{7,23},{8,24},{9,... | collective-permute-start | bytes 688136 | tf_op jit(solution)/shard_map/ppermute | solution.py:266
  14.2 10.1 %collective-permute-start.4 = (bf16[448,256]{1,0:T(8,128)(2,1)S(1)}, bf16[448,256]{1,0:T(8,128)(2,1)S(1)}, u32[]{:S(2)}, u32[]{:S(2)}) collective-permute-start(bf16[448,256]{1,0:T(8,128)(2,1)S(1)} %collective-permute-done.2.refs_3_), channel_id=1, source_target_pairs={{0,4},{1,5},{2,0},{3,1},{4,6},{5,7},{6,2},{7,3},{8,12},{9,13},{10,... | collective-permute-start | bytes 688136 | tf_op jit(solution)/shard_map/ppermute | solution.py:266
  17.5 7.3 %collective-permute-start.10 = (bf16[448,256]{1,0:T(8,128)(2,1)S(1)}, bf16[448,256]{1,0:T(8,128)(2,1)S(1)}, u32[]{:S(2)}, u32[]{:S(2)}) collective-permute-start(bf16[448,256]{1,0:T(8,128)(2,1)S(1)} %collective-permute-done.2.refs_3_), channel_id=1, source_target_pairs={{0,1},{1,0},{2,3},{3,2},{4,5},{5,4},{6,7},{7,6},{8,9},{9,8},{10,11... | collective-permute-start | bytes 688136 | tf_op jit(solution)/shard_map/ppermute | solution.py:266
  20.8 10.6 %collective-permute-start.15 = (bf16[448,256]{1,0:T(8,128)(2,1)S(1)}, bf16[448,256]{1,0:T(8,128)(2,1)S(1)}, u32[]{:S(2)}, u32[]{:S(2)}) collective-permute-start(bf16[448,256]{1,0:T(8,128)(2,1)S(1)} %collective-permute-done.2.refs_3_), channel_id=1, source_target_pairs={{0,16},{1,17},{2,18},{3,19},{4,20},{5,21},{6,22},{7,23},{8,24},{9,... | collective-permute-start | bytes 688136 | tf_op jit(solution)/shard_map/ppermute | solution.py:266
  21.3 8.5 %collective-permute-start.6 = (bf16[448,256]{1,0:T(8,128)(2,1)S(1)}, bf16[448,256]{1,0:T(8,128)(2,1)S(1)}, u32[]{:S(2)}, u32[]{:S(2)}) collective-permute-start(bf16[448,256]{1,0:T(8,128)(2,1)S(1)} %collective-permute-done.1.refs_1_), channel_id=1, source_target_pairs={{0,1},{1,0},{2,3},{3,2},{4,5},{5,4},{6,7},{7,6},{8,9},{9,8},{10,11... | collective-permute-start | bytes 688136 | tf_op jit(solution)/shard_map/ppermute | solution.py:266
  21.9 10.0 %collective-permute-start.16 = (bf16[448,256]{1,0:T(8,128)(2,1)S(1)}, bf16[448,256]{1,0:T(8,128)(2,1)S(1)}, u32[]{:S(2)}, u32[]{:S(2)}) collective-permute-start(bf16[448,256]{1,0:T(8,128)(2,1)S(1)} %collective-permute-done.8.refs_4_), channel_id=1, source_target_pairs={{0,2},{1,3},{2,6},{3,7},{4,0},{5,1},{6,4},{7,5},{8,10},{9,11},{10,... | collective-permute-start | bytes 688136 | tf_op jit(solution)/shard_map/ppermute | solution.py:266
  24.3 10.2 %collective-permute-start.9 = (bf16[448,256]{1,0:T(8,128)(2,1)S(1)}, bf16[448,256]{1,0:T(8,128)(2,1)S(1)}, u32[]{:S(2)}, u32[]{:S(2)}) collective-permute-start(bf16[448,256]{1,0:T(8,128)(2,1)S(1)} %collective-permute-done.4.refs_2_), channel_id=1, source_target_pairs={{0,1},{1,0},{2,3},{3,2},{4,5},{5,4},{6,7},{7,6},{8,9},{9,8},{10,11... | collective-permute-start | bytes 688136 | tf_op jit(solution)/shard_map/ppermute | solution.py:266
  24.8 11.0 %collective-permute-start.11 = (bf16[448,256]{1,0:T(8,128)(2,1)S(1)}, bf16[448,256]{1,0:T(8,128)(2,1)S(1)}, u32[]{:S(2)}, u32[]{:S(2)}) collective-permute-start(bf16[448,256]{1,0:T(8,128)(2,1)S(1)} %collective-permute-done.8.refs_4_), channel_id=1, source_target_pairs={{0,4},{1,5},{2,0},{3,1},{4,6},{5,7},{6,2},{7,3},{8,12},{9,13},{10,... | collective-permute-start | bytes 688136 | tf_op jit(solution)/shard_map/ppermute | solution.py:266
  29.9 9.8 %collective-permute-start.13 = (bf16[448,256]{1,0:T(8,128)(2,1)S(1)}, bf16[448,256]{1,0:T(8,128)(2,1)S(1)}, u32[]{:S(2)}, u32[]{:S(2)}) collective-permute-start(bf16[448,256]{1,0:T(8,128)(2,1)S(1)} %collective-permute-done.1.refs_1_), channel_id=1, source_target_pairs={{0,16},{1,17},{2,18},{3,19},{4,20},{5,21},{6,22},{7,23},{8,24},{9,... | collective-permute-start | bytes 688136 | tf_op jit(solution)/shard_map/ppermute | solution.py:266
  31.4 8.3 %collective-permute-start.14 = (bf16[448,256]{1,0:T(8,128)(2,1)S(1)}, bf16[448,256]{1,0:T(8,128)(2,1)S(1)}, u32[]{:S(2)}, u32[]{:S(2)}) collective-permute-start(bf16[448,256]{1,0:T(8,128)(2,1)S(1)} %collective-permute-done.4.refs_2_), channel_id=1, source_target_pairs={{0,16},{1,17},{2,18},{3,19},{4,20},{5,21},{6,22},{7,23},{8,24},{9,... | collective-permute-start | bytes 688136 | tf_op jit(solution)/shard_map/ppermute | solution.py:266
  31.9 7.8 %collective-permute-start.17 = (bf16[448,256]{1,0:T(8,128)(2,1)S(1)}, bf16[448,256]{1,0:T(8,128)(2,1)S(1)}, u32[]{:S(2)}, u32[]{:S(2)}) collective-permute-start(bf16[448,256]{1,0:T(8,128)(2,1)S(1)} %collective-permute-done.16.refs_5_), channel_id=1, source_target_pairs={{0,2},{1,3},{2,6},{3,7},{4,0},{5,1},{6,4},{7,5},{8,10},{9,11},{10,... | collective-permute-start | bytes 688136 | tf_op jit(solution)/shard_map/ppermute | solution.py:266
  35.8 1.2 %copy-start = (bf16[1,1,128,3584]{3,2,1,0:T(8,128)(2,1)S(1)}, bf16[1,1,128,3584]{3,2,1,0:T(8,128)(2,1)}, u32[]{:S(2)}) copy-start(bf16[1,1,128,3584]{3,2,1,0:T(8,128)(2,1)} %param.4) | copy-start | bytes 2752516
  37.0 0.9 %copy-start.2 = (bf16[1,448,256]{2,1,0:T(8,128)(2,1)S(1)}, bf16[1,448,256]{2,1,0:T(8,128)(2,1)}, u32[]{:S(2)}) copy-start(bf16[1,448,256]{2,1,0:T(8,128)(2,1)} %param.6) | copy-start | bytes 688132
  39.6 2.5 %collective-permute-start.12 = (bf16[128,3584]{1,0:T(8,128)(2,1)S(1)}, bf16[128,3584]{1,0:T(8,128)(2,1)S(1)}, u32[]{:S(2)}, u32[]{:S(2)}) collective-permute-start(bf16[128,3584]{1,0:T(8,128)(2,1)S(1)} %get-tuple-element.65), channel_id=1, source_target_pairs={{0,8},{1,9},{2,10},{3,11},{4,12},{5,13},{6,14},{7,15},{8,0},{9,1},... | collective-permute-start | bytes 2752520 | tf_op jit(solution)/shard_map/ppermute | solution.py:266
  41.4 3.8 %collective-permute-start.19 = (bf16[128,3584]{1,0:T(8,128)(2,1)S(1)}, bf16[128,3584]{1,0:T(8,128)(2,1)S(1)}, u32[]{:S(2)}, u32[]{:S(2)}) collective-permute-start(bf16[128,3584]{1,0:T(8,128)(2,1)S(1)} %get-tuple-element.78), channel_id=1, source_target_pairs={{0,8},{1,9},{2,10},{3,11},{4,12},{5,13},{6,14},{7,15},{8,0},{9,1},... | collective-permute-start | bytes 2752520 | tf_op jit(solution)/shard_map/ppermute | solution.py:266
  48.3 2.5 %collective-permute-start.20 = (bf16[128,3584]{1,0:T(8,128)(2,1)S(1)}, bf16[128,3584]{1,0:T(8,128)(2,1)S(1)}, u32[]{:S(2)}, u32[]{:S(2)}) collective-permute-start(bf16[128,3584]{1,0:T(8,128)(2,1)S(1)} %get-tuple-element.79), channel_id=1, source_target_pairs={{0,8},{1,9},{2,10},{3,11},{4,12},{5,13},{6,14},{7,15},{8,0},{9,1},... | collective-permute-start | bytes 2752520 | tf_op jit(solution)/shard_map/ppermute | solution.py:266
  48.5 9.1 %collective-permute-start.18 = (bf16[128,3584]{1,0:T(8,128)(2,1)S(1)}, bf16[128,3584]{1,0:T(8,128)(2,1)S(1)}, u32[]{:S(2)}, u32[]{:S(2)}) collective-permute-start(bf16[128,3584]{1,0:T(8,128)(2,1)S(1)} %get-tuple-element.73), channel_id=1, source_target_pairs={{0,8},{1,9},{2,10},{3,11},{4,12},{5,13},{6,14},{7,15},{8,0},{9,1},... | collective-permute-start | bytes 2752520 | tf_op jit(solution)/shard_map/ppermute | solution.py:266
  52.5 5.1 %copy-start.1 = (bf16[1,1,128,3584]{3,2,1,0:T(8,128)(2,1)S(1)}, bf16[1,1,128,3584]{3,2,1,0:T(8,128)(2,1)}, u32[]{:S(2)}) copy-start(bf16[1,1,128,3584]{3,2,1,0:T(8,128)(2,1)} %param.4) | copy-start | bytes 2752516
  53.5 16.9 %collective-permute-start.25 = (bf16[128,3584]{1,0:T(8,128)(2,1)S(1)}, bf16[128,3584]{1,0:T(8,128)(2,1)S(1)}, u32[]{:S(2)}, u32[]{:S(2)}) collective-permute-start(bf16[128,3584]{1,0:T(8,128)(2,1)S(1)} %first_input_grad.3), channel_id=1, source_target_pairs={{0,8},{1,9},{2,10},{3,11},{4,12},{5,13},{6,14},{7,15},{8,0},{9,1},... | collective-permute-start | bytes 2752520 | tf_op jit(solution)/shard_map/ppermute | solution.py:266
  53.8 8.9 %collective-permute-start.21 = (bf16[464,256]{1,0:T(8,128)(2,1)S(1)}, bf16[464,256]{1,0:T(8,128)(2,1)S(1)}, u32[]{:S(2)}, u32[]{:S(2)}) collective-permute-start(bf16[464,256]{1,0:T(8,128)(2,1)S(1)} %get-tuple-element.84), channel_id=1, source_target_pairs={{0,4},{1,5},{2,0},{3,1},{4,6},{5,7},{6,2},{7,3},{8,12},{9,13},{10,... | collective-permute-start | bytes 712712 | tf_op jit(solution)/shard_map/ppermute | solution.py:266
  56.1 8.7 %collective-permute-start.26 = (bf16[464,256]{1,0:T(8,128)(2,1)S(1)}, bf16[464,256]{1,0:T(8,128)(2,1)S(1)}, u32[]{:S(2)}, u32[]{:S(2)}) collective-permute-start(bf16[464,256]{1,0:T(8,128)(2,1)S(1)} %get-tuple-element.94), channel_id=1, source_target_pairs={{0,16},{1,17},{2,18},{3,19},{4,20},{5,21},{6,22},{7,23},{8,24},{9,... | collective-permute-start | bytes 712712 | tf_op jit(solution)/shard_map/ppermute | solution.py:266
  59.2 8.8 %collective-permute-start.28 = (bf16[464,256]{1,0:T(8,128)(2,1)S(1)}, bf16[464,256]{1,0:T(8,128)(2,1)S(1)}, u32[]{:S(2)}, u32[]{:S(2)}) collective-permute-start(bf16[464,256]{1,0:T(8,128)(2,1)S(1)} %get-tuple-element.97), channel_id=1, source_target_pairs={{0,1},{1,0},{2,3},{3,2},{4,5},{5,4},{6,7},{7,6},{8,9},{9,8},{10,11... | collective-permute-start | bytes 712712 | tf_op jit(solution)/shard_map/ppermute | solution.py:266
  60.1 8.7 %collective-permute-start.23 = (bf16[464,256]{1,0:T(8,128)(2,1)S(1)}, bf16[464,256]{1,0:T(8,128)(2,1)S(1)}, u32[]{:S(2)}, u32[]{:S(2)}) collective-permute-start(bf16[464,256]{1,0:T(8,128)(2,1)S(1)} %get-tuple-element.85), channel_id=1, source_target_pairs={{0,16},{1,17},{2,18},{3,19},{4,20},{5,21},{6,22},{7,23},{8,24},{9,... | collective-permute-start | bytes 712712 | tf_op jit(solution)/shard_map/ppermute | solution.py:266
  62.7 10.4 %collective-permute-start.24 = (bf16[464,256]{1,0:T(8,128)(2,1)S(1)}, bf16[464,256]{1,0:T(8,128)(2,1)S(1)}, u32[]{:S(2)}, u32[]{:S(2)}) collective-permute-start(bf16[464,256]{1,0:T(8,128)(2,1)S(1)} %get-tuple-element.87), channel_id=1, source_target_pairs={{0,1},{1,0},{2,3},{3,2},{4,5},{5,4},{6,7},{7,6},{8,9},{9,8},{10,11... | collective-permute-start | bytes 712712 | tf_op jit(solution)/shard_map/ppermute | solution.py:266
  64.8 11.8 %collective-permute-start.22 = (bf16[464,256]{1,0:T(8,128)(2,1)S(1)}, bf16[464,256]{1,0:T(8,128)(2,1)S(1)}, u32[]{:S(2)}, u32[]{:S(2)}) collective-permute-start(bf16[464,256]{1,0:T(8,128)(2,1)S(1)} %partial_sum.7), channel_id=1, source_target_pairs={{0,4},{1,5},{2,0},{3,1},{4,6},{5,7},{6,2},{7,3},{8,12},{9,13},{10,... | collective-permute-start | bytes 712712 | tf_op jit(solution)/shard_map/ppermute | solution.py:266
  68.0 9.5 %collective-permute-start.27 = (bf16[464,256]{1,0:T(8,128)(2,1)S(1)}, bf16[464,256]{1,0:T(8,128)(2,1)S(1)}, u32[]{:S(2)}, u32[]{:S(2)}) collective-permute-start(bf16[464,256]{1,0:T(8,128)(2,1)S(1)} %partial_sum.8), channel_id=1, source_target_pairs={{0,1},{1,0},{2,3},{3,2},{4,5},{5,4},{6,7},{7,6},{8,9},{9,8},{10,11... | collective-permute-start | bytes 712712 | tf_op jit(solution)/shard_map/ppermute | solution.py:266
  68.9 9.9 %collective-permute-start.29 = (bf16[464,256]{1,0:T(8,128)(2,1)S(1)}, bf16[464,256]{1,0:T(8,128)(2,1)S(1)}, u32[]{:S(2)}, u32[]{:S(2)}) collective-permute-start(bf16[464,256]{1,0:T(8,128)(2,1)S(1)} %get-tuple-element.98), channel_id=1, source_target_pairs={{0,16},{1,17},{2,18},{3,19},{4,20},{5,21},{6,22},{7,23},{8,24},{9,... | collective-permute-start | bytes 712712 | tf_op jit(solution)/shard_map/ppermute | solution.py:266
  73.1 9.0 %collective-permute-start.35 = (bf16[464,256]{1,0:T(8,128)(2,1)S(1)}, bf16[464,256]{1,0:T(8,128)(2,1)S(1)}, u32[]{:S(2)}, u32[]{:S(2)}) collective-permute-start(bf16[464,256]{1,0:T(8,128)(2,1)S(1)} %get-tuple-element.110), channel_id=1, source_target_pairs={{0,16},{1,17},{2,18},{3,19},{4,20},{5,21},{6,22},{7,23},{8,24},{9,... | collective-permute-start | bytes 712712 | tf_op jit(solution)/shard_map/ppermute | solution.py:266
  73.1 9.1 %collective-permute-start.34 = (bf16[464,256]{1,0:T(8,128)(2,1)S(1)}, bf16[464,256]{1,0:T(8,128)(2,1)S(1)}, u32[]{:S(2)}, u32[]{:S(2)}) collective-permute-start(bf16[464,256]{1,0:T(8,128)(2,1)S(1)} %partial_sum.12), channel_id=1, source_target_pairs={{0,4},{1,5},{2,0},{3,1},{4,6},{5,7},{6,2},{7,3},{8,12},{9,13},{10,... | collective-permute-start | bytes 712712 | tf_op jit(solution)/shard_map/ppermute | solution.py:266
  76.6 9.2 %collective-permute-start.32 = (bf16[464,256]{1,0:T(8,128)(2,1)S(1)}, bf16[464,256]{1,0:T(8,128)(2,1)S(1)}, u32[]{:S(2)}, u32[]{:S(2)}) collective-permute-start(bf16[464,256]{1,0:T(8,128)(2,1)S(1)} %partial_sum.10), channel_id=1, source_target_pairs={{0,1},{1,0},{2,3},{3,2},{4,5},{5,4},{6,7},{7,6},{8,9},{9,8},{10,11... | collective-permute-start | bytes 712712 | tf_op jit(solution)/shard_map/ppermute | solution.py:266
  77.5 9.6 %collective-permute-start.31 = (bf16[464,256]{1,0:T(8,128)(2,1)S(1)}, bf16[464,256]{1,0:T(8,128)(2,1)S(1)}, u32[]{:S(2)}, u32[]{:S(2)}) collective-permute-start(bf16[464,256]{1,0:T(8,128)(2,1)S(1)} %get-tuple-element.101), channel_id=1, source_target_pairs={{0,1},{1,0},{2,3},{3,2},{4,5},{5,4},{6,7},{7,6},{8,9},{9,8},{10,11... | collective-permute-start | bytes 712712 | tf_op jit(solution)/shard_map/ppermute | solution.py:266
  78.8 10.6 %collective-permute-start.30 = (bf16[464,256]{1,0:T(8,128)(2,1)S(1)}, bf16[464,256]{1,0:T(8,128)(2,1)S(1)}, u32[]{:S(2)}, u32[]{:S(2)}) collective-permute-start(bf16[464,256]{1,0:T(8,128)(2,1)S(1)} %partial_sum.9), channel_id=1, source_target_pairs={{0,2},{1,3},{2,6},{3,7},{4,0},{5,1},{6,4},{7,5},{8,10},{9,11},{10,... | collective-permute-start | bytes 712712 | tf_op jit(solution)/shard_map/ppermute | solution.py:266
  82.3 9.8 %collective-permute-start.36 = (bf16[464,256]{1,0:T(8,128)(2,1)S(1)}, bf16[464,256]{1,0:T(8,128)(2,1)S(1)}, u32[]{:S(2)}, u32[]{:S(2)}) collective-permute-start(bf16[464,256]{1,0:T(8,128)(2,1)S(1)} %partial_sum.13), channel_id=1, source_target_pairs={{0,4},{1,5},{2,0},{3,1},{4,6},{5,7},{6,2},{7,3},{8,12},{9,13},{10,... | collective-permute-start | bytes 712712 | tf_op jit(solution)/shard_map/ppermute | solution.py:266
  85.9 6.2 %collective-permute-start.33 = (bf16[464,256]{1,0:T(8,128)(2,1)S(1)}, bf16[464,256]{1,0:T(8,128)(2,1)S(1)}, u32[]{:S(2)}, u32[]{:S(2)}) collective-permute-start(bf16[464,256]{1,0:T(8,128)(2,1)S(1)} %partial_sum.11), channel_id=1, source_target_pairs={{0,16},{1,17},{2,18},{3,19},{4,20},{5,21},{6,22},{7,23},{8,24},{9,... | collective-permute-start | bytes 712712 | tf_op jit(solution)/shard_map/ppermute | solution.py:266

commit v4 on v3

--- a/solution.py
+++ b/solution.py
@@ -71,11 +71,14 @@
     return dc.astype(BF16), dgain
 
 
-def input_grad(out_ref, dy_ref, probs_b, dc_b, w_ref):
-    for cols in column_chunks(dy_ref.shape[-1]):
+def input_grad(out_ref, dy_ref, probs_b, dc_b, w_ref, after_chunk=None):
+    left = jnp.concatenate([probs_b.astype(F32).T.astype(BF16), dc_b], axis=1)
+    for at, cols in enumerate(column_chunks(dy_ref.shape[-1])):
         dy = dy_ref[:, cols]
-        dx = dy.astype(F32) + matmul_tn(probs_b, dy) + matmul_nt(dc_b, w_ref[cols, :])
+        dx = dy.astype(F32) + matmul(left, jnp.concatenate([dy, w_ref[cols, :].T], axis=0))
         out_ref[:, cols] = dx.astype(BF16)
+        if after_chunk is not None:
+            after_chunk(at, cols)
 
 
 def ring_place(value):
@@ -92,17 +95,42 @@
     return chain ^ 1 ^ (lax.axis_index("section") & 1)
 
 
-def first_block(slot, *refs):
-    pieces, (gain_ref, x_ref, u_ref, w_ref, c_ref, p_ref) = refs[:8], refs[8:]
-    rows = pieces[0].shape[0]
+def place_shards(w_ref, pieces):
+    rows = pieces[-1].shape[0]
     for at, piece in enumerate(pieces):
-        w_ref[pl.ds(shard_row(at // 4, 4 - at % 4, rows), rows), :] = piece[...]
-    c = matmul(x_ref[...], w_ref[...])
+        if piece is not None:
+            w_ref[pl.ds(shard_row(at // 4, 4 - at % 4, rows), rows), :] = piece[...]
+
+
+def first_output(slot, c, gain_ref, x_ref, u_ref, c_ref, p_ref):
     _, normed = latent_norm(c, gain_ref[slot : slot + 1, :])
     probs = attention(normed, c.shape[-1])
     c_ref[...] = c
     p_ref[...] = probs
     mix_into(u_ref, x_ref, probs.astype(BF16))
+
+
+def first_block_own(own_ref, x_hbm_ref, *refs):
+    pieces, (gain_ref, u_ref, w_ref, c_ref, p_ref, x_ref, sems) = refs[:7], refs[7:]
+    rows = own_ref.shape[0]
+    own = pltpu.make_async_copy(own_ref, w_ref.at[pl.ds(shard_row(0, 0, rows), rows), :], sems.at[0])
+    chunks = column_chunks(x_ref.shape[-1])
+    loads = [pltpu.make_async_copy(x_hbm_ref.at[:, cols], x_ref.at[:, cols], sems.at[1 + i]) for i, cols in enumerate(chunks)]
+    for load in (own, *loads):
+        load.start()
+    place_shards(w_ref, (None, *pieces))
+    own.wait()
+    c = 0.0
+    for load, cols in zip(loads, chunks):
+        load.wait()
+        c = c + matmul(x_ref[:, cols], w_ref[cols, :])
+    first_output(0, c, gain_ref, x_ref, u_ref, c_ref, p_ref)
+
+
+def first_block_other(*refs):
+    pieces, (gain_ref, x_ref, u_ref, w_ref, c_ref, p_ref) = refs[:8], refs[8:]
+    place_shards(w_ref, pieces)
+    first_output(1, matmul(x_ref[...], w_ref[...]), gain_ref, x_ref, u_ref, c_ref, p_ref)
 
 
 def second_block(chain, gain_ref, x_ref, w0_ref, w1_ref, e_ref, dc_ref, dg_ref, v_ref, c_ref):
@@ -186,40 +214,52 @@
     input_grad(out_ref, cot_ref, p_ref[...].astype(BF16), dc_ref[...], w_ref)
 
 
+def first_input_grad_out(cot_ref, p_ref, dc_ref, w_ref, out_ref, grad_ref, sems):
+    stores = []
+
+    def send(at, cols):
+        stores.append(pltpu.make_async_copy(grad_ref.at[:, cols], out_ref.at[:, cols], sems.at[at]))
+        stores[-1].start()
+
+    input_grad(grad_ref, cot_ref, p_ref[...].astype(BF16), dc_ref[...], w_ref, send)
+    for moved in stores:
+        moved.wait()
+
+
 def store(value_ref, out_ref):
     pltpu.sync_copy(value_ref, out_ref)
 
 
-def kernel_call(body, args, outs, scratch=(), flops=0, out_space=pltpu.VMEM):
-    local = pl.BlockSpec(memory_space=pltpu.VMEM)
+def kernel_call(body, args, outs, scratch=(), flops=0, from_hbm=0, out_space=pltpu.VMEM):
+    local, far = pl.BlockSpec(memory_space=pltpu.VMEM), pl.BlockSpec(memory_space=pltpu.HBM)
     return pl.pallas_call(
         body,
         out_shape=outs,
-        in_specs=[local] * len(args),
+        in_specs=[far] * from_hbm + [local] * (len(args) - from_hbm),
         out_specs=[pl.BlockSpec(memory_space=out_space)] * len(outs),
         scratch_shapes=scratch,
         compiler_params=pltpu.CompilerParams(vmem_limit_bytes=VMEM_LIMIT),
         name=getattr(body, "func", body).__name__,
         cost_estimate=pl.CostEstimate(flops=flops, bytes_accessed=4 << 20, transcendentals=0),
-    )(*args)
+    )(*[pltpu.with_memory_space_constraint(v, pltpu.HBM) if i < from_hbm else v for i, v in enumerate(args)])
 
 
 GATHER = (
     ("Y0", "y", "O0", ()),
+    ("O1", "z", "O0", ()),
     ("O3", "r", "O0", ()),
     ("X0", "x", "O0", ()),
-    ("O1", "z", "O0", ()),
     ("D0", "x", "Y0", ("G", "H")),
-    ("Y3", "y", "O3", ()),
-    ("O2", "r", "O3", ("Y0",)),
-    ("X3", "x", "O3", ("Y0",)),
-    ("Y1", "y", "O1", ("X0", "O3", "Y0")),
-    ("D1", "z", "D0", ("X0", "O3", "Y0")),
-    ("X1", "x", "O1", ("X0", "O3", "Y0")),
-    ("Y2", "y", "O2", ("D0", "O1", "X0")),
-    ("D3", "r", "D0", ("Y3", "O1", "X0")),
-    ("X2", "x", "O2", ("Y3", "D0", "O1")),
-    ("D2", "z", "D1", ("Y1", "X3", "O2")),
+    ("Y1", "y", "O1", ("Y0",)),
+    ("X1", "x", "O1", ("Y0",)),
+    ("O2", "r", "O3", ("X0", "O1", "Y0")),
+    ("Y3", "y", "O3", ("X0", "O1", "Y0")),
+    ("D3", "r", "D0", ("Y1", "O3", "X0")),
+    ("X3", "x", "O3", ("D0", "Y1", "X0")),
+    ("Y2", "y", "O2", ("D0", "Y1", "O3")),
+    ("D1", "y", "X1", ("Y3", "O2", "D0")),
+    ("X2", "x", "O2", ("Y3", "X1", "D0")),
+    ("D2", "r", "D3", ("Y3", "X1", "O2")),
 )
 SCATTER = (
     ("D2", "z", "D1", ()),
@@ -240,7 +280,7 @@
     ("X0", "x", "O0", ("F", "X3", "Y3")),
     ("O1", "z", "O0", ("F", "X3", "Y3")),
 )
-FIRST_AFTER = ("D3", "Y2")
+FIRST_AFTER = ("Y2", "X3")
 PLACES = tuple(tuple(column + str(k) for column in columns for k in range(4)) for columns in ("OY", "XD"))
 BACK = {"x": "x", "y": "y", "z": "r", "r": "z"}
 
@@ -315,13 +355,17 @@
     product = 2 * tokens * width * latent
 
     x1, x2, w, c1, p1 = (x_fwd, x_rev), [None] * 2, [None] * 2, [None] * 2, [None] * 2
-    for slot in range(2):
-        gain = after(both_gains, [c1[0]] if slot else [held[name] for name in FIRST_AFTER])
-        u, w[slot], c1[slot], p1[slot] = kernel_call(
-            functools.partial(first_block, slot), (*[held[name] for name in PLACES[slot]], gain, x1[slot]),
-            [one, matrix, saved_c, saved_p], flops=2 * product,
-        )
-        x2[slot] = other_core(u)
+    first = [one, matrix, saved_c, saved_p]
+    chunks = pltpu.SemaphoreType.DMA((width // CHUNK + 1,))
+    gain = after(both_gains, [held[name] for name in FIRST_AFTER])
+    own, *others = [held[name] for name in PLACES[0]]
+    u, w[0], c1[0], p1[0] = kernel_call(
+        first_block_own, (own, x_fwd, *others, gain), first, [pltpu.VMEM((tokens, width), BF16), chunks], 2 * product, from_hbm=2
+    )
+    x2[0] = other_core(u)
+    gain = after(both_gains, [c1[0]])
+    u, w[1], c1[1], p1[1] = kernel_call(first_block_other, (*[held[name] for name in PLACES[1]], gain, x_rev), first, flops=2 * product)
+    x2[1] = other_core(u)
     cot, dc2, dg2 = [None] * 2, [None] * 2, [None] * 2
     for chain in range(2):
         gain = after(both_gains, [dc2[0]] if chain else [])
@@ -341,8 +385,11 @@
 
     def input_grads(slot, earlier):
         args = (after(cot[slot], earlier), p1[slot], dc1[slot], w[slot])
+        if slot == 0:
+            scratch = [pltpu.VMEM((tokens, width), BF16), chunks]
+            return kernel_call(first_input_grad_out, args, [one], scratch, 2 * product, out_space=pltpu.HBM)[0]
         (grad,) = kernel_call(first_input_grad, args, [one], flops=2 * product)
-        return kernel_call(store, (other_core(grad),), [one], out_space=pl.ANY)[0] if slot else grad
+        return kernel_call(store, (other_core(grad),), [one], out_space=pltpu.HBM)[0]
 
     beside = {"F": functools.partial(input_grads, 0), "R": functools.partial(input_grads, 1)}
     parts = {name: part for slot in range(2) for name, part in zip(PLACES[slot], parts[slot])}

time: 93.2 us -> 92 us (0.987)
  starting transfers between devices: 47.5 us -> 52 us
  waiting for transfers between devices: 23.6 us -> 20 us
  local copies, waits for them, and re-layouts: 2.12 us -> 0.01 us
    ppermute x37, starting transfers between devices: 47.5 us -> 52 us  [moves_between(): lax.ppermute(v, AXES, p)]
    ppermute x37, waiting for transfers between devices: 23.6 us -> 20 us  [moves_between(): lax.ppermute(v, AXES, p)]
    unnamed x6 -> x2, local copies, waits for them, and re-layouts: 2.12 us -> 0.01 us
  transfers between devices with their start and end apart: 37 -> 37, of which waited for: 15 -> 13; matrix products, arithmetic and copies ran while one was open for 1% -> 1% of each run, Pallas kernels for 15% -> 16%
where the time goes in v4:
time: 92 us; the launch traced here: 91.9 us
  starting transfers between devices  52 us (57%)
  waiting for transfers between devices  20 us (22%)
  Pallas kernels  18.4 us (20%)
    ppermute x37, starting transfers between devices, moves_between(): lax.ppermute(v, AXES, p)  52 us
    ppermute x37, waiting for transfers between devices, moves_between(): lax.ppermute(v, AXES, p)  20 us
    pallas_call x17, Pallas kernels, kernel_call(): pl.pallas_call(body, out_shape=outs, in_specs=[far] * from_hbm + [local]...  18.4 us
  transfers between devices with their start and end apart: 37, of which 13 were waited for; matrix products, arithmetic and copies ran while one was open for 1% of the time, Pallas kernels for 16%

profile of v4, /device:TPU:0, one launch (start us, length us, event | category | flops | bytes accessed | tf_op | source)
XLA Modules:
  0.0 91.9 jit_solution(14611628454629161545)
XLA Ops:
  1.1 2.6 %collective-permute-start.4 = (bf16[448,256]{1,0:T(8,128)(2,1)}, bf16[448,256]{1,0:T(8,128)(2,1)S(1)}, u32[]{:S(2)}, u32[]{:S(2)}) collective-permute-start(bf16[448,256]{1,0:T(8,128)(2,1)} %bitcast.10), channel_id=1, source_target_pairs={{0,1},{1,0},{2,3},{3,2},{4,5},{5,4},{6,7},{7,6},{8,9},{9,8},{10,11... | collective-permute-start | bytes 688136 | tf_op jit(solution)/shard_map/ppermute | solution.py:306
  3.7 1.6 %collective-permute-start.1 = (bf16[448,256]{1,0:T(8,128)(2,1)}, bf16[448,256]{1,0:T(8,128)(2,1)S(1)}, u32[]{:S(2)}, u32[]{:S(2)}) collective-permute-start(bf16[448,256]{1,0:T(8,128)(2,1)} %bitcast.11), channel_id=1, source_target_pairs={{0,2},{1,3},{2,6},{3,7},{4,0},{5,1},{6,4},{7,5},{8,10},{9,11},{10,... | collective-permute-start | bytes 688136 | tf_op jit(solution)/shard_map/ppermute | solution.py:306
  5.3 1.5 %collective-permute-start = (bf16[1,256]{1,0:T(2,128)(2,1)}, bf16[1,256]{1,0:T(2,128)(2,1)S(1)}, u32[]{:S(2)}, u32[]{:S(2)}) collective-permute-start(bf16[1,256]{1,0:T(2,128)(2,1)} %param.7), channel_id=1, source_target_pairs={{0,16},{1,17},{2,18},{3,19},{4,20},{5,21},{6,22},{7,23},{8,24},{9,... | collective-permute-start | bytes 1544 | tf_op jit(solution)/shard_map/ppermute | solution.py:306
  6.8 1.3 %collective-permute-start.2 = (bf16[448,256]{1,0:T(8,128)(2,1)}, bf16[448,256]{1,0:T(8,128)(2,1)S(1)}, u32[]{:S(2)}, u32[]{:S(2)}) collective-permute-start(bf16[448,256]{1,0:T(8,128)(2,1)} %bitcast.12), channel_id=1, source_target_pairs={{0,4},{1,5},{2,0},{3,1},{4,6},{5,7},{6,2},{7,3},{8,12},{9,13},{10,... | collective-permute-start | bytes 688136 | tf_op jit(solution)/shard_map/ppermute | solution.py:306
  8.2 0.9 %collective-permute-done = bf16[1,256]{1,0:T(2,128)(2,1)S(1)} collective-permute-done((bf16[1,256]{1,0:T(2,128)(2,1)}, bf16[1,256]{1,0:T(2,128)(2,1)S(1)}, u32[]{:S(2)}, u32[]{:S(2)}) %collective-permute-start) | collective-permute-done | bytes 544 | tf_op jit(solution)/shard_map/ppermute | solution.py:306
  9.1 1.5 %collective-permute-start.3 = (bf16[448,256]{1,0:T(8,128)(2,1)}, bf16[448,256]{1,0:T(8,128)(2,1)S(1)}, u32[]{:S(2)}, u32[]{:S(2)}) collective-permute-start(bf16[448,256]{1,0:T(8,128)(2,1)} %bitcast.13), channel_id=1, source_target_pairs={{0,16},{1,17},{2,18},{3,19},{4,20},{5,21},{6,22},{7,23},{8,24},{9,... | collective-permute-start | bytes 688136 | tf_op jit(solution)/shard_map/ppermute | solution.py:306
  11.3 1.4 %collective-permute-done.1.refs_0_ = bf16[448,256]{1,0:T(8,128)(2,1)S(1)} collective-permute-done((bf16[448,256]{1,0:T(8,128)(2,1)}, bf16[448,256]{1,0:T(8,128)(2,1)S(1)}, u32[]{:S(2)}, u32[]{:S(2)}) %collective-permute-start.1) | collective-permute-done | bytes 229408 | tf_op jit(solution)/shard_map/ppermute | solution.py:306
  13.1 1.5 %collective-permute-start.8 = (bf16[448,256]{1,0:T(8,128)(2,1)S(1)}, bf16[448,256]{1,0:T(8,128)(2,1)S(1)}, u32[]{:S(2)}, u32[]{:S(2)}) collective-permute-start(bf16[448,256]{1,0:T(8,128)(2,1)S(1)} %collective-permute-done.4.refs_3_), channel_id=1, source_target_pairs={{0,16},{1,17},{2,18},{3,19},{4,20},{5,21},{6,22},{7,23},{8,24},{9,... | collective-permute-start | bytes 688136 | tf_op jit(solution)/shard_map/ppermute | solution.py:306
  14.7 2.8 %collective-permute-done.2.refs_2_ = bf16[448,256]{1,0:T(8,128)(2,1)S(1)} collective-permute-done((bf16[448,256]{1,0:T(8,128)(2,1)}, bf16[448,256]{1,0:T(8,128)(2,1)S(1)}, u32[]{:S(2)}, u32[]{:S(2)}) %collective-permute-start.2) | collective-permute-done | bytes 229408 | tf_op jit(solution)/shard_map/ppermute | solution.py:306
  17.5 1.7 %collective-permute-start.5 = (bf16[448,256]{1,0:T(8,128)(2,1)S(1)}, bf16[448,256]{1,0:T(8,128)(2,1)S(1)}, u32[]{:S(2)}, u32[]{:S(2)}) collective-permute-start(bf16[448,256]{1,0:T(8,128)(2,1)S(1)} %collective-permute-done.2.refs_2_), channel_id=1, source_target_pairs={{0,4},{1,5},{2,0},{3,1},{4,6},{5,7},{6,2},{7,3},{8,12},{9,13},{10,... | collective-permute-start | bytes 688136 | tf_op jit(solution)/shard_map/ppermute | solution.py:306
  19.6 1.5 %collective-permute-start.13 = (bf16[448,256]{1,0:T(8,128)(2,1)S(1)}, bf16[448,256]{1,0:T(8,128)(2,1)S(1)}, u32[]{:S(2)}, u32[]{:S(2)}) collective-permute-start(bf16[448,256]{1,0:T(8,128)(2,1)S(1)} %collective-permute-done.1.refs_0_), channel_id=1, source_target_pairs={{0,16},{1,17},{2,18},{3,19},{4,20},{5,21},{6,22},{7,23},{8,24},{9,... | collective-permute-start | bytes 688136 | tf_op jit(solution)/shard_map/ppermute | solution.py:306
  21.1 4.6 %collective-permute-start.16 = (bf16[448,256]{1,0:T(8,128)(2,1)S(1)}, bf16[448,256]{1,0:T(8,128)(2,1)S(1)}, u32[]{:S(2)}, u32[]{:S(2)}) collective-permute-start(bf16[448,256]{1,0:T(8,128)(2,1)S(1)} %collective-permute-done.8.refs_4_), channel_id=1, source_target_pairs={{0,4},{1,5},{2,0},{3,1},{4,6},{5,7},{6,2},{7,3},{8,12},{9,13},{10,... | collective-permute-start | bytes 688136 | tf_op jit(solution)/shard_map/ppermute | solution.py:306
  25.7 1.2 %collective-permute-done.5.refs_1_ = bf16[448,256]{1,0:T(8,128)(2,1)S(1)} collective-permute-done((bf16[448,256]{1,0:T(8,128)(2,1)S(1)}, bf16[448,256]{1,0:T(8,128)(2,1)S(1)}, u32[]{:S(2)}, u32[]{:S(2)}) %collective-permute-start.5) | collective-permute-done | bytes 229408 | tf_op jit(solution)/shard_map/ppermute | solution.py:306
  27.0 1.2 %collective-permute-start.9 = (bf16[448,256]{1,0:T(8,128)(2,1)S(1)}, bf16[448,256]{1,0:T(8,128)(2,1)S(1)}, u32[]{:S(2)}, u32[]{:S(2)}) collective-permute-start(bf16[448,256]{1,0:T(8,128)(2,1)S(1)} %collective-permute-done.5.refs_1_), channel_id=1, source_target_pairs={{0,1},{1,0},{2,3},{3,2},{4,5},{5,4},{6,7},{7,6},{8,9},{9,8},{10,11... | collective-permute-start | bytes 688136 | tf_op jit(solution)/shard_map/ppermute | solution.py:306
  28.1 0.8 collective-permute-start.11
  29.0 1.2 %collective-permute-start.14 = (bf16[448,256]{1,0:T(8,128)(2,1)S(1)}, bf16[448,256]{1,0:T(8,128)(2,1)S(1)}, u32[]{:S(2)}, u32[]{:S(2)}) collective-permute-start(bf16[448,256]{1,0:T(8,128)(2,1)S(1)} %collective-permute-done.5.refs_1_), channel_id=1, source_target_pairs={{0,16},{1,17},{2,18},{3,19},{4,20},{5,21},{6,22},{7,23},{8,24},{9,... | collective-permute-start | bytes 688136 | tf_op jit(solution)/shard_map/ppermute | solution.py:306
  30.2 0.9 collective-permute-start.15
  31.0 3.7 %collective-permute-start.17 = (bf16[448,256]{1,0:T(8,128)(2,1)S(1)}, bf16[448,256]{1,0:T(8,128)(2,1)S(1)}, u32[]{:S(2)}, u32[]{:S(2)}) collective-permute-start(bf16[448,256]{1,0:T(8,128)(2,1)S(1)} %collective-permute-done.16.refs_7_), channel_id=1, source_target_pairs={{0,4},{1,5},{2,0},{3,1},{4,6},{5,7},{6,2},{7,3},{8,12},{9,13},{10,... | collective-permute-start | bytes 688136 | tf_op jit(solution)/shard_map/ppermute | solution.py:306
  34.8 2.9 %first_block_own.1 = (bf16[128,3584]{1,0:T(8,128)(2,1)S(1)}, bf16[3584,256]{1,0:T(8,128)(2,1)S(1)}, f32[128,256]{1,0:T(8,128)S(1)}, f32[128,128]{1,0:T(8,128)S(1)}) custom-call(bf16[448,256]{1,0:T(8,128)(2,1)} %bitcast.14, bf16[128,3584]{1,0:T(8,128)(2,1)} %bitcast.6, bf16[448,256]{1,0:T(8,128)(2,1)S(1)} %collective-permute-done.1.refs_0_, ...), custom_call_target="tpu_custom_call" | custom-call | flops 469762048 | bytes 4194304 | tf_op jit(solution)/shard_map/first_block_own/pallas_call | solution.py:235
  37.8 0.9 collective-permute-done.17.refs_6_
  38.7 1.7 %first_block_other.1 = (bf16[128,3584]{1,0:T(8,128)(2,1)S(1)}, bf16[3584,256]{1,0:T(8,128)(2,1)S(1)}, f32[128,256]{1,0:T(8,128)S(1)}, f32[128,128]{1,0:T(8,128)S(1)}) custom-call(bf16[448,256]{1,0:T(8,128)(2,1)S(1)} %collective-permute-done.3.refs_0_, bf16[448,256]{1,0:T(8,128)(2,1)S(1)} %collective-permute-done.13.refs_1_, ...), custom_call_target="tpu_custom_call" | custom-call | flops 469762048 | bytes 4194304 | tf_op jit(solution)/shard_map/first_block_other/pallas_call | solution.py:235
  40.5 2.8 %second_block.2 = (bf16[128,3584]{1,0:T(8,128)(2,1)S(1)}, bf16[128,256]{1,0:T(8,128)(2,1)S(1)}, f32[1,256]{1,0:T(1,128)S(1)}) custom-call(bf16[2,256]{1,0:T(2,128)(2,1)S(1)} %pad_maximum_fusion.refs_7_.refs_8_.gain_ref.refs_0_, bf16[128,3584]{1,0:T(8,128)(2,1)S(1)} %collective-permute-done.12.x_ref.refs_5_, ...), custom_call_target="tpu_custom_call" | custom-call | flops 939524096 | bytes 4194304 | tf_op jit(solution)/shard_map/second_block/pallas_call | solution.py:235
  43.3 2.8 %second_block.3 = (bf16[128,3584]{1,0:T(8,128)(2,1)S(1)}, bf16[128,256]{1,0:T(8,128)(2,1)S(1)}, f32[1,256]{1,0:T(1,128)S(1)}) custom-call(bf16[2,256]{1,0:T(2,128)(2,1)S(1)} %pad_maximum_fusion.refs_7_.refs_8_.gain_ref.refs_0_, bf16[128,3584]{1,0:T(8,128)(2,1)S(1)} %collective-permute-done.19.x_ref.refs_6_, ...), custom_call_target="tpu_custom_call" | custom-call | flops 939524096 | bytes 4194304 | tf_op jit(solution)/shard_map/second_block/pallas_call | solution.py:235
  46.7 2.0 %collective-permute-done.20.refs_4_.cot_ref = bf16[128,3584]{1,0:T(8,128)(2,1)S(1)} collective-permute-done((bf16[128,3584]{1,0:T(8,128)(2,1)S(1)}, bf16[128,3584]{1,0:T(8,128)(2,1)S(1)}, u32[]{:S(2)}, u32[]{:S(2)}) %collective-permute-start.20) | collective-permute-done | bytes 917536 | tf_op jit(solution)/shard_map/ppermute | solution.py:306
  48.8 1.8 %first_weight_grad.2 = (bf16[128,256]{1,0:T(8,128)(2,1)S(1)}, bf16[464,256]{1,0:T(8,128)(2,1)S(1)}, bf16[464,256]{1,0:T(8,128)(2,1)S(1)}, bf16[464,256]{1,0:T(8,...) custom-call(bf16[2,256]{1,0:T(2,128)(2,1)S(1)} %pad_maximum_fusion.r, ...), custom_call_target="tpu_custom_call" | custom-call | flops 939524096 | bytes 4194304 | tf_op jit(solution)/shard_map/first_weight_grad/pallas_call | solution.py:235
  50.6 0.8 first_input_grad.1
  51.8 3.5 %collective-permute-start.21 = (bf16[464,256]{1,0:T(8,128)(2,1)S(1)}, bf16[464,256]{1,0:T(8,128)(2,1)S(1)}, u32[]{:S(2)}, u32[]{:S(2)}) collective-permute-start(bf16[464,256]{1,0:T(8,128)(2,1)S(1)} %get-tuple-element.86), channel_id=1, source_target_pairs={{0,4},{1,5},{2,0},{3,1},{4,6},{5,7},{6,2},{7,3},{8,12},{9,13},{10,... | collective-permute-start | bytes 712712 | tf_op jit(solution)/shard_map/ppermute | solution.py:306
  55.3 1.3 %collective-permute-start.26 = (bf16[464,256]{1,0:T(8,128)(2,1)S(1)}, bf16[464,256]{1,0:T(8,128)(2,1)S(1)}, u32[]{:S(2)}, u32[]{:S(2)}) collective-permute-start(bf16[464,256]{1,0:T(8,128)(2,1)S(1)} %get-tuple-element.96), channel_id=1, source_target_pairs={{0,16},{1,17},{2,18},{3,19},{4,20},{5,21},{6,22},{7,23},{8,24},{9,... | collective-permute-start | bytes 712712 | tf_op jit(solution)/shard_map/ppermute | solution.py:306
  56.6 1.7 %first_weight_grad.3 = (bf16[128,256]{1,0:T(8,128)(2,1)S(1)}, bf16[464,256]{1,0:T(8,128)(2,1)S(1)}, bf16[464,256]{1,0:T(8,128)(2,1)S(1)}, bf16[464,256]{1,0:T(8,...) custom-call(bf16[2,256]{1,0:T(2,128)(2,1)S(1)} %pad_maximum_fusion.r, ...), custom_call_target="tpu_custom_call" | custom-call | flops 939524096 | bytes 4194304 | tf_op jit(solution)/shard_map/first_weight_grad/pallas_call | solution.py:235
  58.2 2.7 %collective-permute-start.28 = (bf16[464,256]{1,0:T(8,128)(2,1)S(1)}, bf16[464,256]{1,0:T(8,128)(2,1)S(1)}, u32[]{:S(2)}, u32[]{:S(2)}) collective-permute-start(bf16[464,256]{1,0:T(8,128)(2,1)S(1)} %get-tuple-element.99), channel_id=1, source_target_pairs={{0,1},{1,0},{2,3},{3,2},{4,5},{5,4},{6,7},{7,6},{8,9},{9,8},{10,11... | collective-permute-start | bytes 712712 | tf_op jit(solution)/shard_map/ppermute | solution.py:306
  60.9 0.9 %collective-permute-done.21.refs_1_ = bf16[464,256]{1,0:T(8,128)(2,1)S(1)} collective-permute-done((bf16[464,256]{1,0:T(8,128)(2,1)S(1)}, bf16[464,256]{1,0:T(8,128)(2,1)S(1)}, u32[]{:S(2)}, u32[]{:S(2)}) %collective-permute-start.21) | collective-permute-done | bytes 237600 | tf_op jit(solution)/shard_map/ppermute | solution.py:306
  61.8 1.0 %collective-permute-start.24 = (bf16[464,256]{1,0:T(8,128)(2,1)S(1)}, bf16[464,256]{1,0:T(8,128)(2,1)S(1)}, u32[]{:S(2)}, u32[]{:S(2)}) collective-permute-start(bf16[464,256]{1,0:T(8,128)(2,1)S(1)} %get-tuple-element.89), channel_id=1, source_target_pairs={{0,1},{1,0},{2,3},{3,2},{4,5},{5,4},{6,7},{7,6},{8,9},{9,8},{10,11... | collective-permute-start | bytes 712712 | tf_op jit(solution)/shard_map/ppermute | solution.py:306
  62.9 3.3 %collective-permute-start.22 = (bf16[464,256]{1,0:T(8,128)(2,1)S(1)}, bf16[464,256]{1,0:T(8,128)(2,1)S(1)}, u32[]{:S(2)}, u32[]{:S(2)}) collective-permute-start(bf16[464,256]{1,0:T(8,128)(2,1)S(1)} %partial_sum.7), channel_id=1, source_target_pairs={{0,4},{1,5},{2,0},{3,1},{4,6},{5,7},{6,2},{7,3},{8,12},{9,13},{10,... | collective-permute-start | bytes 712712 | tf_op jit(solution)/shard_map/ppermute | solution.py:306
  66.2 1.3 %collective-permute-done.28.refs_1_ = bf16[464,256]{1,0:T(8,128)(2,1)S(1)} collective-permute-done((bf16[464,256]{1,0:T(8,128)(2,1)S(1)}, bf16[464,256]{1,0:T(8,128)(2,1)S(1)}, u32[]{:S(2)}, u32[]{:S(2)}) %collective-permute-start.28) | collective-permute-done | bytes 237600 | tf_op jit(solution)/shard_map/ppermute | solution.py:306
  67.5 2.1 %collective-permute-start.27 = (bf16[464,256]{1,0:T(8,128)(2,1)S(1)}, bf16[464,256]{1,0:T(8,128)(2,1)S(1)}, u32[]{:S(2)}, u32[]{:S(2)}) collective-permute-start(bf16[464,256]{1,0:T(8,128)(2,1)S(1)} %partial_sum.8), channel_id=1, source_target_pairs={{0,1},{1,0},{2,3},{3,2},{4,5},{5,4},{6,7},{7,6},{8,9},{9,8},{10,11... | collective-permute-start | bytes 712712 | tf_op jit(solution)/shard_map/ppermute | solution.py:306
  69.7 0.9 %store.1 = bf16[128,3584]{1,0:T(8,128)(2,1)} custom-call(bf16[128,3584]{1,0:T(8,128)(2,1)S(1)} %collective-permute-done.25.value_ref), custom_call_target="tpu_custom_call" | custom-call | bytes 4194304 | tf_op jit(solution)/shard_map/store/pallas_call | solution.py:235
  70.6 2.0 %collective-permute-done.24.refs_1_ = bf16[464,256]{1,0:T(8,128)(2,1)S(1)} collective-permute-done((bf16[464,256]{1,0:T(8,128)(2,1)S(1)}, bf16[464,256]{1,0:T(8,128)(2,1)S(1)}, u32[]{:S(2)}, u32[]{:S(2)}) %collective-permute-start.24) | collective-permute-done | bytes 237600 | tf_op jit(solution)/shard_map/ppermute | solution.py:306
  72.8 1.8 %collective-permute-start.34 = (bf16[464,256]{1,0:T(8,128)(2,1)S(1)}, bf16[464,256]{1,0:T(8,128)(2,1)S(1)}, u32[]{:S(2)}, u32[]{:S(2)}) collective-permute-start(bf16[464,256]{1,0:T(8,128)(2,1)S(1)} %partial_sum.12), channel_id=1, source_target_pairs={{0,4},{1,5},{2,0},{3,1},{4,6},{5,7},{6,2},{7,3},{8,12},{9,13},{10,... | collective-permute-start | bytes 712712 | tf_op jit(solution)/shard_map/ppermute | solution.py:306
  74.6 2.1 %collective-permute-start.32 = (bf16[464,256]{1,0:T(8,128)(2,1)S(1)}, bf16[464,256]{1,0:T(8,128)(2,1)S(1)}, u32[]{:S(2)}, u32[]{:S(2)}) collective-permute-start(bf16[464,256]{1,0:T(8,128)(2,1)S(1)} %partial_sum.10), channel_id=1, source_target_pairs={{0,1},{1,0},{2,3},{3,2},{4,5},{5,4},{6,7},{7,6},{8,9},{9,8},{10,11... | collective-permute-start | bytes 712712 | tf_op jit(solution)/shard_map/ppermute | solution.py:306
  76.7 0.9 collective-permute-done.27.refs_1_
  77.6 2.1 %collective-permute-start.31 = (bf16[464,256]{1,0:T(8,128)(2,1)S(1)}, bf16[464,256]{1,0:T(8,128)(2,1)S(1)}, u32[]{:S(2)}, u32[]{:S(2)}) collective-permute-start(bf16[464,256]{1,0:T(8,128)(2,1)S(1)} %get-tuple-element.103), channel_id=1, source_target_pairs={{0,1},{1,0},{2,3},{3,2},{4,5},{5,4},{6,7},{7,6},{8,9},{9,8},{10,11... | collective-permute-start | bytes 712712 | tf_op jit(solution)/shard_map/ppermute | solution.py:306
  79.9 1.5 %first_input_grad_out.1 = bf16[128,3584]{1,0:T(8,128)(2,1)} custom-call(bf16[128,3584]{1,0:T(8,128)(2,1)S(1)} %collective-permute-done.18.refs_4_.cot_ref, f32[128,128]{1,0:T(8,128)S(1)} %get-tuple-element.88.refs_3_.p_ref, bf16[128,256]{1,0:T(8,128)(2,1)S(1)} %get-tuple-element.91.dc_ref, bf16[3584,256]{1,0:T(8,128)(2,1)S(1)} %get-tuple-element.67.w0_ref.w_ref), custom_call_target="tpu_custom_call" | custom-call | flops 469762048 | bytes 4194304 | tf_op jit(solution)/shard_map/first_input_grad_out/pallas_call | solution.py:235
  81.6 3.0 %collective-permute-start.36 = (bf16[464,256]{1,0:T(8,128)(2,1)S(1)}, bf16[464,256]{1,0:T(8,128)(2,1)S(1)}, u32[]{:S(2)}, u32[]{:S(2)}) collective-permute-start(bf16[464,256]{1,0:T(8,128)(2,1)S(1)} %partial_sum.13), channel_id=1, source_target_pairs={{0,4},{1,5},{2,0},{3,1},{4,6},{5,7},{6,2},{7,3},{8,12},{9,13},{10,... | collective-permute-start | bytes 712712 | tf_op jit(solution)/shard_map/ppermute | solution.py:306
  84.6 0.7 collective-permute-start.33
  85.3 1.4 %collective-permute-done.31.refs_2_ = bf16[464,256]{1,0:T(8,128)(2,1)S(1)} collective-permute-done((bf16[464,256]{1,0:T(8,128)(2,1)S(1)}, bf16[464,256]{1,0:T(8,128)(2,1)S(1)}, u32[]{:S(2)}, u32[]{:S(2)}) %collective-permute-start.31) | collective-permute-done | bytes 237600 | tf_op jit(solution)/shard_map/ppermute | solution.py:306
  86.8 2.3 %collective-permute-done.30.refs_1_ = bf16[464,256]{1,0:T(8,128)(2,1)S(1)} collective-permute-done((bf16[464,256]{1,0:T(8,128)(2,1)S(1)}, bf16[464,256]{1,0:T(8,128)(2,1)S(1)}, u32[]{:S(2)}, u32[]{:S(2)}) %collective-permute-start.30) | collective-permute-done | bytes 237600 | tf_op jit(solution)/shard_map/ppermute | solution.py:306
  89.0 1.9 %collective-permute-done.36.refs_4_ = bf16[464,256]{1,0:T(8,128)(2,1)S(1)} collective-permute-done((bf16[464,256]{1,0:T(8,128)(2,1)S(1)}, bf16[464,256]{1,0:T(8,128)(2,1)S(1)}, u32[]{:S(2)}, u32[]{:S(2)}) %collective-permute-start.36) | collective-permute-done | bytes 237600 | tf_op jit(solution)/shard_map/ppermute | solution.py:306
  90.9 0.9 %final_sum.1 = (f32[448,256]{1,0:T(8,128)}, f32[1,256]{1,0:T(1,128)}) custom-call(bf16[464,256]{1,0:T(8,128)(2,1)S(1)} %get-tuple-element.93.refs_0_, bf16[464,256]{1,0:T(8,128)(2,1)S(1)} %collective-permute-done.30.refs_1_, bf16[464,256]{1,0:T(8,128)(2,1)S(1)} %collective-permute-done.31.refs_2_, bf16[464,256]{1,0:T(8,128)(2,1)S(1)} %collective-permute-done.33.refs_3_, ...), custom_call_target="tpu_custom_call" | custom-call | bytes 4194304 | tf_op jit(solution)/shard_map/final_sum/pallas_call | solution.py:235
  (46 shorter events, 4.3 us)
Async XLA Ops:
  0.6 12.5 %collective-permute-start.7 = (bf16[128,3584]{1,0:T(8,128)(2,1)}, bf16[128,3584]{1,0:T(8,128)(2,1)S(1)}, u32[]{:S(2)}, u32[]{:S(2)}) collective-permute-start(bf16[128,3584]{1,0:T(8,128)(2,1)} %bitcast.15), channel_id=1, source_target_pairs={{0,8},{1,9},{2,10},{3,11},{4,12},{5,13},{6,14},{7,15},{8,0},{9,1},... | collective-permute-start | bytes 2752520 | tf_op jit(solution)/shard_map/ppermute | solution.py:306
  1.1 10.1 %collective-permute-start.4 = (bf16[448,256]{1,0:T(8,128)(2,1)}, bf16[448,256]{1,0:T(8,128)(2,1)S(1)}, u32[]{:S(2)}, u32[]{:S(2)}) collective-permute-start(bf16[448,256]{1,0:T(8,128)(2,1)} %bitcast.10), channel_id=1, source_target_pairs={{0,1},{1,0},{2,3},{3,2},{4,5},{5,4},{6,7},{7,6},{8,9},{9,8},{10,11... | collective-permute-start | bytes 688136 | tf_op jit(solution)/shard_map/ppermute | solution.py:306
  3.7 8.9 %collective-permute-start.1 = (bf16[448,256]{1,0:T(8,128)(2,1)}, bf16[448,256]{1,0:T(8,128)(2,1)S(1)}, u32[]{:S(2)}, u32[]{:S(2)}) collective-permute-start(bf16[448,256]{1,0:T(8,128)(2,1)} %bitcast.11), channel_id=1, source_target_pairs={{0,2},{1,3},{2,6},{3,7},{4,0},{5,1},{6,4},{7,5},{8,10},{9,11},{10,... | collective-permute-start | bytes 688136 | tf_op jit(solution)/shard_map/ppermute | solution.py:306
  5.3 3.8 %collective-permute-start = (bf16[1,256]{1,0:T(2,128)(2,1)}, bf16[1,256]{1,0:T(2,128)(2,1)S(1)}, u32[]{:S(2)}, u32[]{:S(2)}) collective-permute-start(bf16[1,256]{1,0:T(2,128)(2,1)} %param.7), channel_id=1, source_target_pairs={{0,16},{1,17},{2,18},{3,19},{4,20},{5,21},{6,22},{7,23},{8,24},{9,... | collective-permute-start | bytes 1544 | tf_op jit(solution)/shard_map/ppermute | solution.py:306
  6.8 10.6 %collective-permute-start.2 = (bf16[448,256]{1,0:T(8,128)(2,1)}, bf16[448,256]{1,0:T(8,128)(2,1)S(1)}, u32[]{:S(2)}, u32[]{:S(2)}) collective-permute-start(bf16[448,256]{1,0:T(8,128)(2,1)} %bitcast.12), channel_id=1, source_target_pairs={{0,4},{1,5},{2,0},{3,1},{4,6},{5,7},{6,2},{7,3},{8,12},{9,13},{10,... | collective-permute-start | bytes 688136 | tf_op jit(solution)/shard_map/ppermute | solution.py:306
  9.1 8.4 %collective-permute-start.3 = (bf16[448,256]{1,0:T(8,128)(2,1)}, bf16[448,256]{1,0:T(8,128)(2,1)S(1)}, u32[]{:S(2)}, u32[]{:S(2)}) collective-permute-start(bf16[448,256]{1,0:T(8,128)(2,1)} %bitcast.13), channel_id=1, source_target_pairs={{0,16},{1,17},{2,18},{3,19},{4,20},{5,21},{6,22},{7,23},{8,24},{9,... | collective-permute-start | bytes 688136 | tf_op jit(solution)/shard_map/ppermute | solution.py:306
  12.6 8.5 %collective-permute-start.6 = (bf16[448,256]{1,0:T(8,128)(2,1)S(1)}, bf16[448,256]{1,0:T(8,128)(2,1)S(1)}, u32[]{:S(2)}, u32[]{:S(2)}) collective-permute-start(bf16[448,256]{1,0:T(8,128)(2,1)S(1)} %collective-permute-done.1.refs_0_), channel_id=1, source_target_pairs={{0,1},{1,0},{2,3},{3,2},{4,5},{5,4},{6,7},{7,6},{8,9},{9,8},{10,11... | collective-permute-start | bytes 688136 | tf_op jit(solution)/shard_map/ppermute | solution.py:306
  13.1 8.0 %collective-permute-start.8 = (bf16[448,256]{1,0:T(8,128)(2,1)S(1)}, bf16[448,256]{1,0:T(8,128)(2,1)S(1)}, u32[]{:S(2)}, u32[]{:S(2)}) collective-permute-start(bf16[448,256]{1,0:T(8,128)(2,1)S(1)} %collective-permute-done.4.refs_3_), channel_id=1, source_target_pairs={{0,16},{1,17},{2,18},{3,19},{4,20},{5,21},{6,22},{7,23},{8,24},{9,... | collective-permute-start | bytes 688136 | tf_op jit(solution)/shard_map/ppermute | solution.py:306
  17.5 9.5 %collective-permute-start.5 = (bf16[448,256]{1,0:T(8,128)(2,1)S(1)}, bf16[448,256]{1,0:T(8,128)(2,1)S(1)}, u32[]{:S(2)}, u32[]{:S(2)}) collective-permute-start(bf16[448,256]{1,0:T(8,128)(2,1)S(1)} %collective-permute-done.2.refs_2_), channel_id=1, source_target_pairs={{0,4},{1,5},{2,0},{3,1},{4,6},{5,7},{6,2},{7,3},{8,12},{9,13},{10,... | collective-permute-start | bytes 688136 | tf_op jit(solution)/shard_map/ppermute | solution.py:306
  19.1 9.8 %collective-permute-start.10 = (bf16[448,256]{1,0:T(8,128)(2,1)S(1)}, bf16[448,256]{1,0:T(8,128)(2,1)S(1)}, u32[]{:S(2)}, u32[]{:S(2)}) collective-permute-start(bf16[448,256]{1,0:T(8,128)(2,1)S(1)} %collective-permute-done.2.refs_2_), channel_id=1, source_target_pairs={{0,1},{1,0},{2,3},{3,2},{4,5},{5,4},{6,7},{7,6},{8,9},{9,8},{10,11... | collective-permute-start | bytes 688136 | tf_op jit(solution)/shard_map/ppermute | solution.py:306
  19.6 9.3 %collective-permute-start.13 = (bf16[448,256]{1,0:T(8,128)(2,1)S(1)}, bf16[448,256]{1,0:T(8,128)(2,1)S(1)}, u32[]{:S(2)}, u32[]{:S(2)}) collective-permute-start(bf16[448,256]{1,0:T(8,128)(2,1)S(1)} %collective-permute-done.1.refs_0_), channel_id=1, source_target_pairs={{0,16},{1,17},{2,18},{3,19},{4,20},{5,21},{6,22},{7,23},{8,24},{9,... | collective-permute-start | bytes 688136 | tf_op jit(solution)/shard_map/ppermute | solution.py:306
  21.1 9.9 %collective-permute-start.16 = (bf16[448,256]{1,0:T(8,128)(2,1)S(1)}, bf16[448,256]{1,0:T(8,128)(2,1)S(1)}, u32[]{:S(2)}, u32[]{:S(2)}) collective-permute-start(bf16[448,256]{1,0:T(8,128)(2,1)S(1)} %collective-permute-done.8.refs_4_), channel_id=1, source_target_pairs={{0,4},{1,5},{2,0},{3,1},{4,6},{5,7},{6,2},{7,3},{8,12},{9,13},{10,... | collective-permute-start | bytes 688136 | tf_op jit(solution)/shard_map/ppermute | solution.py:306
  27.0 7.8 %collective-permute-start.9 = (bf16[448,256]{1,0:T(8,128)(2,1)S(1)}, bf16[448,256]{1,0:T(8,128)(2,1)S(1)}, u32[]{:S(2)}, u32[]{:S(2)}) collective-permute-start(bf16[448,256]{1,0:T(8,128)(2,1)S(1)} %collective-permute-done.5.refs_1_), channel_id=1, source_target_pairs={{0,1},{1,0},{2,3},{3,2},{4,5},{5,4},{6,7},{7,6},{8,9},{9,8},{10,11... | collective-permute-start | bytes 688136 | tf_op jit(solution)/shard_map/ppermute | solution.py:306
  28.1 6.7 %collective-permute-start.11 = (bf16[448,256]{1,0:T(8,128)(2,1)S(1)}, bf16[448,256]{1,0:T(8,128)(2,1)S(1)}, u32[]{:S(2)}, u32[]{:S(2)}) collective-permute-start(bf16[448,256]{1,0:T(8,128)(2,1)S(1)} %collective-permute-done.2.refs_2_), channel_id=1, source_target_pairs={{0,16},{1,17},{2,18},{3,19},{4,20},{5,21},{6,22},{7,23},{8,24},{9,... | collective-permute-start | bytes 688136 | tf_op jit(solution)/shard_map/ppermute | solution.py:306
  29.0 8.8 %collective-permute-start.14 = (bf16[448,256]{1,0:T(8,128)(2,1)S(1)}, bf16[448,256]{1,0:T(8,128)(2,1)S(1)}, u32[]{:S(2)}, u32[]{:S(2)}) collective-permute-start(bf16[448,256]{1,0:T(8,128)(2,1)S(1)} %collective-permute-done.5.refs_1_), channel_id=1, source_target_pairs={{0,16},{1,17},{2,18},{3,19},{4,20},{5,21},{6,22},{7,23},{8,24},{9,... | collective-permute-start | bytes 688136 | tf_op jit(solution)/shard_map/ppermute | solution.py:306
  30.2 7.6 %collective-permute-start.15 = (bf16[448,256]{1,0:T(8,128)(2,1)S(1)}, bf16[448,256]{1,0:T(8,128)(2,1)S(1)}, u32[]{:S(2)}, u32[]{:S(2)}) collective-permute-start(bf16[448,256]{1,0:T(8,128)(2,1)S(1)} %collective-permute-done.13.refs_1_), channel_id=1, source_target_pairs={{0,1},{1,0},{2,3},{3,2},{4,5},{5,4},{6,7},{7,6},{8,9},{9,8},{10,11... | collective-permute-start | bytes 688136 | tf_op jit(solution)/shard_map/ppermute | solution.py:306
  31.0 7.7 %collective-permute-start.17 = (bf16[448,256]{1,0:T(8,128)(2,1)S(1)}, bf16[448,256]{1,0:T(8,128)(2,1)S(1)}, u32[]{:S(2)}, u32[]{:S(2)}) collective-permute-start(bf16[448,256]{1,0:T(8,128)(2,1)S(1)} %collective-permute-done.16.refs_7_), channel_id=1, source_target_pairs={{0,4},{1,5},{2,0},{3,1},{4,6},{5,7},{6,2},{7,3},{8,12},{9,13},{10,... | collective-permute-start | bytes 688136 | tf_op jit(solution)/shard_map/ppermute | solution.py:306
  37.7 2.8 %collective-permute-start.12 = (bf16[128,3584]{1,0:T(8,128)(2,1)S(1)}, bf16[128,3584]{1,0:T(8,128)(2,1)S(1)}, u32[]{:S(2)}, u32[]{:S(2)}) collective-permute-start(bf16[128,3584]{1,0:T(8,128)(2,1)S(1)} %get-tuple-element.66), channel_id=1, source_target_pairs={{0,8},{1,9},{2,10},{3,11},{4,12},{5,13},{6,14},{7,15},{8,0},{9,1},... | collective-permute-start | bytes 2752520 | tf_op jit(solution)/shard_map/ppermute | solution.py:306
  40.4 2.9 %collective-permute-start.19 = (bf16[128,3584]{1,0:T(8,128)(2,1)S(1)}, bf16[128,3584]{1,0:T(8,128)(2,1)S(1)}, u32[]{:S(2)}, u32[]{:S(2)}) collective-permute-start(bf16[128,3584]{1,0:T(8,128)(2,1)S(1)} %get-tuple-element.80), channel_id=1, source_target_pairs={{0,8},{1,9},{2,10},{3,11},{4,12},{5,13},{6,14},{7,15},{8,0},{9,1},... | collective-permute-start | bytes 2752520 | tf_op jit(solution)/shard_map/ppermute | solution.py:306
  46.1 2.6 %collective-permute-start.20 = (bf16[128,3584]{1,0:T(8,128)(2,1)S(1)}, bf16[128,3584]{1,0:T(8,128)(2,1)S(1)}, u32[]{:S(2)}, u32[]{:S(2)}) collective-permute-start(bf16[128,3584]{1,0:T(8,128)(2,1)S(1)} %get-tuple-element.81), channel_id=1, source_target_pairs={{0,8},{1,9},{2,10},{3,11},{4,12},{5,13},{6,14},{7,15},{8,0},{9,1},... | collective-permute-start | bytes 2752520 | tf_op jit(solution)/shard_map/ppermute | solution.py:306
  46.7 9.9 %collective-permute-start.18 = (bf16[128,3584]{1,0:T(8,128)(2,1)S(1)}, bf16[128,3584]{1,0:T(8,128)(2,1)S(1)}, u32[]{:S(2)}, u32[]{:S(2)}) collective-permute-start(bf16[128,3584]{1,0:T(8,128)(2,1)S(1)} %get-tuple-element.75), channel_id=1, source_target_pairs={{0,8},{1,9},{2,10},{3,11},{4,12},{5,13},{6,14},{7,15},{8,0},{9,1},... | collective-permute-start | bytes 2752520 | tf_op jit(solution)/shard_map/ppermute | solution.py:306
  50.6 6.0 %copy-start = (bf16[1,1,128,3584]{3,2,1,0:T(8,128)(2,1)S(1)}, bf16[1,1,128,3584]{3,2,1,0:T(8,128)(2,1)}, u32[]{:S(2)}) copy-start(bf16[1,1,128,3584]{3,2,1,0:T(8,128)(2,1)} %param.4) | copy-start | bytes 2752516
  51.4 18.3 %collective-permute-start.25 = (bf16[128,3584]{1,0:T(8,128)(2,1)S(1)}, bf16[128,3584]{1,0:T(8,128)(2,1)S(1)}, u32[]{:S(2)}, u32[]{:S(2)}) collective-permute-start(bf16[128,3584]{1,0:T(8,128)(2,1)S(1)} %first_input_grad.1), channel_id=1, source_target_pairs={{0,8},{1,9},{2,10},{3,11},{4,12},{5,13},{6,14},{7,15},{8,0},{9,1},... | collective-permute-start | bytes 2752520 | tf_op jit(solution)/shard_map/ppermute | solution.py:306
  51.8 10.0 %collective-permute-start.21 = (bf16[464,256]{1,0:T(8,128)(2,1)S(1)}, bf16[464,256]{1,0:T(8,128)(2,1)S(1)}, u32[]{:S(2)}, u32[]{:S(2)}) collective-permute-start(bf16[464,256]{1,0:T(8,128)(2,1)S(1)} %get-tuple-element.86), channel_id=1, source_target_pairs={{0,4},{1,5},{2,0},{3,1},{4,6},{5,7},{6,2},{7,3},{8,12},{9,13},{10,... | collective-permute-start | bytes 712712 | tf_op jit(solution)/shard_map/ppermute | solution.py:306
  55.3 7.6 %collective-permute-start.26 = (bf16[464,256]{1,0:T(8,128)(2,1)S(1)}, bf16[464,256]{1,0:T(8,128)(2,1)S(1)}, u32[]{:S(2)}, u32[]{:S(2)}) collective-permute-start(bf16[464,256]{1,0:T(8,128)(2,1)S(1)} %get-tuple-element.96), channel_id=1, source_target_pairs={{0,16},{1,17},{2,18},{3,19},{4,20},{5,21},{6,22},{7,23},{8,24},{9,... | collective-permute-start | bytes 712712 | tf_op jit(solution)/shard_map/ppermute | solution.py:306
  58.2 9.3 %collective-permute-start.28 = (bf16[464,256]{1,0:T(8,128)(2,1)S(1)}, bf16[464,256]{1,0:T(8,128)(2,1)S(1)}, u32[]{:S(2)}, u32[]{:S(2)}) collective-permute-start(bf16[464,256]{1,0:T(8,128)(2,1)S(1)} %get-tuple-element.99), channel_id=1, source_target_pairs={{0,1},{1,0},{2,3},{3,2},{4,5},{5,4},{6,7},{7,6},{8,9},{9,8},{10,11... | collective-permute-start | bytes 712712 | tf_op jit(solution)/shard_map/ppermute | solution.py:306
  60.9 8.7 %collective-permute-start.23 = (bf16[464,256]{1,0:T(8,128)(2,1)S(1)}, bf16[464,256]{1,0:T(8,128)(2,1)S(1)}, u32[]{:S(2)}, u32[]{:S(2)}) collective-permute-start(bf16[464,256]{1,0:T(8,128)(2,1)S(1)} %get-tuple-element.87), channel_id=1, source_target_pairs={{0,16},{1,17},{2,18},{3,19},{4,20},{5,21},{6,22},{7,23},{8,24},{9,... | collective-permute-start | bytes 712712 | tf_op jit(solution)/shard_map/ppermute | solution.py:306
  61.8 10.8 %collective-permute-start.24 = (bf16[464,256]{1,0:T(8,128)(2,1)S(1)}, bf16[464,256]{1,0:T(8,128)(2,1)S(1)}, u32[]{:S(2)}, u32[]{:S(2)}) collective-permute-start(bf16[464,256]{1,0:T(8,128)(2,1)S(1)} %get-tuple-element.89), channel_id=1, source_target_pairs={{0,1},{1,0},{2,3},{3,2},{4,5},{5,4},{6,7},{7,6},{8,9},{9,8},{10,11... | collective-permute-start | bytes 712712 | tf_op jit(solution)/shard_map/ppermute | solution.py:306
  62.9 11.7 %collective-permute-start.22 = (bf16[464,256]{1,0:T(8,128)(2,1)S(1)}, bf16[464,256]{1,0:T(8,128)(2,1)S(1)}, u32[]{:S(2)}, u32[]{:S(2)}) collective-permute-start(bf16[464,256]{1,0:T(8,128)(2,1)S(1)} %partial_sum.7), channel_id=1, source_target_pairs={{0,4},{1,5},{2,0},{3,1},{4,6},{5,7},{6,2},{7,3},{8,12},{9,13},{10,... | collective-permute-start | bytes 712712 | tf_op jit(solution)/shard_map/ppermute | solution.py:306
  67.5 10.1 %collective-permute-start.27 = (bf16[464,256]{1,0:T(8,128)(2,1)S(1)}, bf16[464,256]{1,0:T(8,128)(2,1)S(1)}, u32[]{:S(2)}, u32[]{:S(2)}) collective-permute-start(bf16[464,256]{1,0:T(8,128)(2,1)S(1)} %partial_sum.8), channel_id=1, source_target_pairs={{0,1},{1,0},{2,3},{3,2},{4,5},{5,4},{6,7},{7,6},{8,9},{9,8},{10,11... | collective-permute-start | bytes 712712 | tf_op jit(solution)/shard_map/ppermute | solution.py:306
  69.6 10.2 %collective-permute-start.29 = (bf16[464,256]{1,0:T(8,128)(2,1)S(1)}, bf16[464,256]{1,0:T(8,128)(2,1)S(1)}, u32[]{:S(2)}, u32[]{:S(2)}) collective-permute-start(bf16[464,256]{1,0:T(8,128)(2,1)S(1)} %get-tuple-element.100), channel_id=1, source_target_pairs={{0,16},{1,17},{2,18},{3,19},{4,20},{5,21},{6,22},{7,23},{8,24},{9,... | collective-permute-start | bytes 712712 | tf_op jit(solution)/shard_map/ppermute | solution.py:306
  72.6 8.8 %collective-permute-start.35 = (bf16[464,256]{1,0:T(8,128)(2,1)S(1)}, bf16[464,256]{1,0:T(8,128)(2,1)S(1)}, u32[]{:S(2)}, u32[]{:S(2)}) collective-permute-start(bf16[464,256]{1,0:T(8,128)(2,1)S(1)} %get-tuple-element.112), channel_id=1, source_target_pairs={{0,16},{1,17},{2,18},{3,19},{4,20},{5,21},{6,22},{7,23},{8,24},{9,... | collective-permute-start | bytes 712712 | tf_op jit(solution)/shard_map/ppermute | solution.py:306
  72.8 8.6 %collective-permute-start.34 = (bf16[464,256]{1,0:T(8,128)(2,1)S(1)}, bf16[464,256]{1,0:T(8,128)(2,1)S(1)}, u32[]{:S(2)}, u32[]{:S(2)}) collective-permute-start(bf16[464,256]{1,0:T(8,128)(2,1)S(1)} %partial_sum.12), channel_id=1, source_target_pairs={{0,4},{1,5},{2,0},{3,1},{4,6},{5,7},{6,2},{7,3},{8,12},{9,13},{10,... | collective-permute-start | bytes 712712 | tf_op jit(solution)/shard_map/ppermute | solution.py:306
  74.6 9.9 %collective-permute-start.32 = (bf16[464,256]{1,0:T(8,128)(2,1)S(1)}, bf16[464,256]{1,0:T(8,128)(2,1)S(1)}, u32[]{:S(2)}, u32[]{:S(2)}) collective-permute-start(bf16[464,256]{1,0:T(8,128)(2,1)S(1)} %partial_sum.10), channel_id=1, source_target_pairs={{0,1},{1,0},{2,3},{3,2},{4,5},{5,4},{6,7},{7,6},{8,9},{9,8},{10,11... | collective-permute-start | bytes 712712 | tf_op jit(solution)/shard_map/ppermute | solution.py:306
  77.6 9.1 %collective-permute-start.31 = (bf16[464,256]{1,0:T(8,128)(2,1)S(1)}, bf16[464,256]{1,0:T(8,128)(2,1)S(1)}, u32[]{:S(2)}, u32[]{:S(2)}) collective-permute-start(bf16[464,256]{1,0:T(8,128)(2,1)S(1)} %get-tuple-element.103), channel_id=1, source_target_pairs={{0,1},{1,0},{2,3},{3,2},{4,5},{5,4},{6,7},{7,6},{8,9},{9,8},{10,11... | collective-permute-start | bytes 712712 | tf_op jit(solution)/shard_map/ppermute | solution.py:306
  79.9 9.1 %collective-permute-start.30 = (bf16[464,256]{1,0:T(8,128)(2,1)S(1)}, bf16[464,256]{1,0:T(8,128)(2,1)S(1)}, u32[]{:S(2)}, u32[]{:S(2)}) collective-permute-start(bf16[464,256]{1,0:T(8,128)(2,1)S(1)} %partial_sum.9), channel_id=1, source_target_pairs={{0,2},{1,3},{2,6},{3,7},{4,0},{5,1},{6,4},{7,5},{8,10},{9,11},{10,... | collective-permute-start | bytes 712712 | tf_op jit(solution)/shard_map/ppermute | solution.py:306
  81.6 9.4 %collective-permute-start.36 = (bf16[464,256]{1,0:T(8,128)(2,1)S(1)}, bf16[464,256]{1,0:T(8,128)(2,1)S(1)}, u32[]{:S(2)}, u32[]{:S(2)}) collective-permute-start(bf16[464,256]{1,0:T(8,128)(2,1)S(1)} %partial_sum.13), channel_id=1, source_target_pairs={{0,4},{1,5},{2,0},{3,1},{4,6},{5,7},{6,2},{7,3},{8,12},{9,13},{10,... | collective-permute-start | bytes 712712 | tf_op jit(solution)/shard_map/ppermute | solution.py:306
  84.6 6.3 %collective-permute-start.33 = (bf16[464,256]{1,0:T(8,128)(2,1)S(1)}, bf16[464,256]{1,0:T(8,128)(2,1)S(1)}, u32[]{:S(2)}, u32[]{:S(2)}) collective-permute-start(bf16[464,256]{1,0:T(8,128)(2,1)S(1)} %partial_sum.11), channel_id=1, source_target_pairs={{0,16},{1,17},{2,18},{3,19},{4,20},{5,21},{6,22},{7,23},{8,24},{9,... | collective-permute-start | bytes 712712 | tf_op jit(solution)/shard_map/ppermute | solution.py:306

commit v5 on v4

--- a/solution.py
+++ b/solution.py
@@ -250,14 +250,14 @@
     ("O3", "r", "O0", ()),
     ("X0", "x", "O0", ()),
     ("D0", "x", "Y0", ("G", "H")),
-    ("Y1", "y", "O1", ("Y0",)),
+    ("Y1", "y", "O1", ()),
     ("X1", "x", "O1", ("Y0",)),
     ("O2", "r", "O3", ("X0", "O1", "Y0")),
     ("Y3", "y", "O3", ("X0", "O1", "Y0")),
     ("D3", "r", "D0", ("Y1", "O3", "X0")),
-    ("X3", "x", "O3", ("D0", "Y1", "X0")),
+    ("D1", "y", "X1", ("Y3", "O2", "D0")),
+    ("X3", "x", "O3", ()),
     ("Y2", "y", "O2", ("D0", "Y1", "O3")),
-    ("D1", "y", "X1", ("Y3", "O2", "D0")),
     ("X2", "x", "O2", ("Y3", "X1", "D0")),
     ("D2", "r", "D3", ("Y3", "X1", "O2")),
 )

time: 92 us -> 91.1 us (level)
  starting transfers between devices: 52 us -> 49.2 us
  waiting for transfers between devices: 20 us -> 21.9 us
    ppermute x37, starting transfers between devices: 52 us -> 49.2 us  [moves_between(): lax.ppermute(v, AXES, p)]
    ppermute x37, waiting for transfers between devices: 20 us -> 21.9 us  [moves_between(): lax.ppermute(v, AXES, p)]
  transfers between devices with their start and end apart: 37 -> 37, of which waited for: 13 -> 16; matrix products, arithmetic and copies ran while one was open for 1% -> 1% of each run, Pallas kernels for 16% -> 16%
where the time goes in v5:
time: 91.1 us; the launch traced here: 91 us
  starting transfers between devices  49.2 us (54%)
  waiting for transfers between devices  21.9 us (24%)
  Pallas kernels  18.4 us (20%)
    ppermute x37, starting transfers between devices, moves_between(): lax.ppermute(v, AXES, p)  49.2 us
    ppermute x37, waiting for transfers between devices, moves_between(): lax.ppermute(v, AXES, p)  21.9 us
    pallas_call x17, Pallas kernels, kernel_call(): pl.pallas_call(body, out_shape=outs, in_specs=[far] * from_hbm + [local]...  18.4 us
  transfers between devices with their start and end apart: 37, of which 16 were waited for; matrix products, arithmetic and copies ran while one was open for 1% of the time, Pallas kernels for 16%

profile of v5, /device:TPU:0, one launch (start us, length us, event | category | flops | bytes accessed | tf_op | source)
XLA Modules:
  0.0 91.0 jit_solution(8364677102186995558)
XLA Ops:
  1.1 2.6 %collective-permute-start.1 = (bf16[448,256]{1,0:T(8,128)(2,1)}, bf16[448,256]{1,0:T(8,128)(2,1)S(1)}, u32[]{:S(2)}, u32[]{:S(2)}) collective-permute-start(bf16[448,256]{1,0:T(8,128)(2,1)} %bitcast.10), channel_id=1, source_target_pairs={{0,2},{1,3},{2,6},{3,7},{4,0},{5,1},{6,4},{7,5},{8,10},{9,11},{10,... | collective-permute-start | bytes 688136 | tf_op jit(solution)/shard_map/ppermute | solution.py:306
  3.8 1.5 %collective-permute-start.4 = (bf16[448,256]{1,0:T(8,128)(2,1)}, bf16[448,256]{1,0:T(8,128)(2,1)S(1)}, u32[]{:S(2)}, u32[]{:S(2)}) collective-permute-start(bf16[448,256]{1,0:T(8,128)(2,1)} %bitcast.11), channel_id=1, source_target_pairs={{0,1},{1,0},{2,3},{3,2},{4,5},{5,4},{6,7},{7,6},{8,9},{9,8},{10,11... | collective-permute-start | bytes 688136 | tf_op jit(solution)/shard_map/ppermute | solution.py:306
  5.3 1.5 %collective-permute-start = (bf16[1,256]{1,0:T(2,128)(2,1)}, bf16[1,256]{1,0:T(2,128)(2,1)S(1)}, u32[]{:S(2)}, u32[]{:S(2)}) collective-permute-start(bf16[1,256]{1,0:T(2,128)(2,1)} %param.7), channel_id=1, source_target_pairs={{0,16},{1,17},{2,18},{3,19},{4,20},{5,21},{6,22},{7,23},{8,24},{9,... | collective-permute-start | bytes 1544 | tf_op jit(solution)/shard_map/ppermute | solution.py:306
  6.8 1.3 %collective-permute-start.2 = (bf16[448,256]{1,0:T(8,128)(2,1)}, bf16[448,256]{1,0:T(8,128)(2,1)S(1)}, u32[]{:S(2)}, u32[]{:S(2)}) collective-permute-start(bf16[448,256]{1,0:T(8,128)(2,1)} %bitcast.12), channel_id=1, source_target_pairs={{0,4},{1,5},{2,0},{3,1},{4,6},{5,7},{6,2},{7,3},{8,12},{9,13},{10,... | collective-permute-start | bytes 688136 | tf_op jit(solution)/shard_map/ppermute | solution.py:306
  8.1 0.9 %collective-permute-done = bf16[1,256]{1,0:T(2,128)(2,1)S(1)} collective-permute-done((bf16[1,256]{1,0:T(2,128)(2,1)}, bf16[1,256]{1,0:T(2,128)(2,1)S(1)}, u32[]{:S(2)}, u32[]{:S(2)}) %collective-permute-start) | collective-permute-done | bytes 544 | tf_op jit(solution)/shard_map/ppermute | solution.py:306
  9.1 1.5 %collective-permute-start.3 = (bf16[448,256]{1,0:T(8,128)(2,1)}, bf16[448,256]{1,0:T(8,128)(2,1)S(1)}, u32[]{:S(2)}, u32[]{:S(2)}) collective-permute-start(bf16[448,256]{1,0:T(8,128)(2,1)} %bitcast.13), channel_id=1, source_target_pairs={{0,16},{1,17},{2,18},{3,19},{4,20},{5,21},{6,22},{7,23},{8,24},{9,... | collective-permute-start | bytes 688136 | tf_op jit(solution)/shard_map/ppermute | solution.py:306
  11.3 1.6 %collective-permute-start.6 = (bf16[448,256]{1,0:T(8,128)(2,1)S(1)}, bf16[448,256]{1,0:T(8,128)(2,1)S(1)}, u32[]{:S(2)}, u32[]{:S(2)}) collective-permute-start(bf16[448,256]{1,0:T(8,128)(2,1)S(1)} %collective-permute-done.1.refs_0_), channel_id=1, source_target_pairs={{0,1},{1,0},{2,3},{3,2},{4,5},{5,4},{6,7},{7,6},{8,9},{9,8},{10,11... | collective-permute-start | bytes 688136 | tf_op jit(solution)/shard_map/ppermute | solution.py:306
  12.9 1.5 %collective-permute-start.8 = (bf16[448,256]{1,0:T(8,128)(2,1)S(1)}, bf16[448,256]{1,0:T(8,128)(2,1)S(1)}, u32[]{:S(2)}, u32[]{:S(2)}) collective-permute-start(bf16[448,256]{1,0:T(8,128)(2,1)S(1)} %collective-permute-done.4.refs_3_), channel_id=1, source_target_pairs={{0,16},{1,17},{2,18},{3,19},{4,20},{5,21},{6,22},{7,23},{8,24},{9,... | collective-permute-start | bytes 688136 | tf_op jit(solution)/shard_map/ppermute | solution.py:306
  14.4 1.7 %collective-permute-done.2.refs_2_ = bf16[448,256]{1,0:T(8,128)(2,1)S(1)} collective-permute-done((bf16[448,256]{1,0:T(8,128)(2,1)}, bf16[448,256]{1,0:T(8,128)(2,1)S(1)}, u32[]{:S(2)}, u32[]{:S(2)}) %collective-permute-start.2) | collective-permute-done | bytes 229408 | tf_op jit(solution)/shard_map/ppermute | solution.py:306
  16.8 1.1 %collective-permute-start.5 = (bf16[448,256]{1,0:T(8,128)(2,1)S(1)}, bf16[448,256]{1,0:T(8,128)(2,1)S(1)}, u32[]{:S(2)}, u32[]{:S(2)}) collective-permute-start(bf16[448,256]{1,0:T(8,128)(2,1)S(1)} %collective-permute-done.2.refs_2_), channel_id=1, source_target_pairs={{0,4},{1,5},{2,0},{3,1},{4,6},{5,7},{6,2},{7,3},{8,12},{9,13},{10,... | collective-permute-start | bytes 688136 | tf_op jit(solution)/shard_map/ppermute | solution.py:306
  17.9 1.5 %collective-permute-start.10 = (bf16[448,256]{1,0:T(8,128)(2,1)S(1)}, bf16[448,256]{1,0:T(8,128)(2,1)S(1)}, u32[]{:S(2)}, u32[]{:S(2)}) collective-permute-start(bf16[448,256]{1,0:T(8,128)(2,1)S(1)} %collective-permute-done.2.refs_2_), channel_id=1, source_target_pairs={{0,1},{1,0},{2,3},{3,2},{4,5},{5,4},{6,7},{7,6},{8,9},{9,8},{10,11... | collective-permute-start | bytes 688136 | tf_op jit(solution)/shard_map/ppermute | solution.py:306
  19.4 1.5 %collective-permute-start.13 = (bf16[448,256]{1,0:T(8,128)(2,1)S(1)}, bf16[448,256]{1,0:T(8,128)(2,1)S(1)}, u32[]{:S(2)}, u32[]{:S(2)}) collective-permute-start(bf16[448,256]{1,0:T(8,128)(2,1)S(1)} %collective-permute-done.1.refs_0_), channel_id=1, source_target_pairs={{0,16},{1,17},{2,18},{3,19},{4,20},{5,21},{6,22},{7,23},{8,24},{9,... | collective-permute-start | bytes 688136 | tf_op jit(solution)/shard_map/ppermute | solution.py:306
  20.9 3.6 %collective-permute-start.16 = (bf16[448,256]{1,0:T(8,128)(2,1)S(1)}, bf16[448,256]{1,0:T(8,128)(2,1)S(1)}, u32[]{:S(2)}, u32[]{:S(2)}) collective-permute-start(bf16[448,256]{1,0:T(8,128)(2,1)S(1)} %collective-permute-done.8.refs_4_), channel_id=1, source_target_pairs={{0,4},{1,5},{2,0},{3,1},{4,6},{5,7},{6,2},{7,3},{8,12},{9,13},{10,... | collective-permute-start | bytes 688136 | tf_op jit(solution)/shard_map/ppermute | solution.py:306
  24.4 1.5 %collective-permute-start.11 = (bf16[448,256]{1,0:T(8,128)(2,1)S(1)}, bf16[448,256]{1,0:T(8,128)(2,1)S(1)}, u32[]{:S(2)}, u32[]{:S(2)}) collective-permute-start(bf16[448,256]{1,0:T(8,128)(2,1)S(1)} %collective-permute-done.2.refs_2_), channel_id=1, source_target_pairs={{0,16},{1,17},{2,18},{3,19},{4,20},{5,21},{6,22},{7,23},{8,24},{9,... | collective-permute-start | bytes 688136 | tf_op jit(solution)/shard_map/ppermute | solution.py:306
  26.0 1.5 %collective-permute-start.9 = (bf16[448,256]{1,0:T(8,128)(2,1)S(1)}, bf16[448,256]{1,0:T(8,128)(2,1)S(1)}, u32[]{:S(2)}, u32[]{:S(2)}) collective-permute-start(bf16[448,256]{1,0:T(8,128)(2,1)S(1)} %collective-permute-done.5.refs_1_), channel_id=1, source_target_pairs={{0,1},{1,0},{2,3},{3,2},{4,5},{5,4},{6,7},{7,6},{8,9},{9,8},{10,11... | collective-permute-start | bytes 688136 | tf_op jit(solution)/shard_map/ppermute | solution.py:306
  27.5 0.8 collective-permute-start.14
  28.5 2.7 %collective-permute-done.16.refs_7_ = bf16[448,256]{1,0:T(8,128)(2,1)S(1)} collective-permute-done((bf16[448,256]{1,0:T(8,128)(2,1)S(1)}, bf16[448,256]{1,0:T(8,128)(2,1)S(1)}, u32[]{:S(2)}, u32[]{:S(2)}) %collective-permute-start.16) | collective-permute-done | bytes 229408 | tf_op jit(solution)/shard_map/ppermute | solution.py:306
  31.2 3.3 %collective-permute-start.17 = (bf16[448,256]{1,0:T(8,128)(2,1)S(1)}, bf16[448,256]{1,0:T(8,128)(2,1)S(1)}, u32[]{:S(2)}, u32[]{:S(2)}) collective-permute-start(bf16[448,256]{1,0:T(8,128)(2,1)S(1)} %collective-permute-done.16.refs_7_), channel_id=1, source_target_pairs={{0,4},{1,5},{2,0},{3,1},{4,6},{5,7},{6,2},{7,3},{8,12},{9,13},{10,... | collective-permute-start | bytes 688136 | tf_op jit(solution)/shard_map/ppermute | solution.py:306
  34.5 2.9 %first_block_own.1 = (bf16[128,3584]{1,0:T(8,128)(2,1)S(1)}, bf16[3584,256]{1,0:T(8,128)(2,1)S(1)}, f32[128,256]{1,0:T(8,128)S(1)}, f32[128,128]{1,0:T(8,128)S(1)}) custom-call(bf16[448,256]{1,0:T(8,128)(2,1)} %bitcast.14, bf16[128,3584]{1,0:T(8,128)(2,1)} %bitcast.6, bf16[448,256]{1,0:T(8,128)(2,1)S(1)} %collective-permute-done.1.refs_0_, ...), custom_call_target="tpu_custom_call" | custom-call | flops 469762048 | bytes 4194304 | tf_op jit(solution)/shard_map/first_block_own/pallas_call | solution.py:235
  37.6 0.9 collective-permute-done.17.refs_6_
  38.5 1.7 %first_block_other.1 = (bf16[128,3584]{1,0:T(8,128)(2,1)S(1)}, bf16[3584,256]{1,0:T(8,128)(2,1)S(1)}, f32[128,256]{1,0:T(8,128)S(1)}, f32[128,128]{1,0:T(8,128)S(1)}) custom-call(bf16[448,256]{1,0:T(8,128)(2,1)S(1)} %collective-permute-done.3.refs_0_, bf16[448,256]{1,0:T(8,128)(2,1)S(1)} %collective-permute-done.13.refs_1_, ...), custom_call_target="tpu_custom_call" | custom-call | flops 469762048 | bytes 4194304 | tf_op jit(solution)/shard_map/first_block_other/pallas_call | solution.py:235
  40.3 2.8 %second_block.2 = (bf16[128,3584]{1,0:T(8,128)(2,1)S(1)}, bf16[128,256]{1,0:T(8,128)(2,1)S(1)}, f32[1,256]{1,0:T(1,128)S(1)}) custom-call(bf16[2,256]{1,0:T(2,128)(2,1)S(1)} %pad_maximum_fusion.refs_7_.refs_8_.gain_ref.refs_0_, bf16[128,3584]{1,0:T(8,128)(2,1)S(1)} %collective-permute-done.12.x_ref.refs_5_, ...), custom_call_target="tpu_custom_call" | custom-call | flops 939524096 | bytes 4194304 | tf_op jit(solution)/shard_map/second_block/pallas_call | solution.py:235
  43.1 2.8 %second_block.3 = (bf16[128,3584]{1,0:T(8,128)(2,1)S(1)}, bf16[128,256]{1,0:T(8,128)(2,1)S(1)}, f32[1,256]{1,0:T(1,128)S(1)}) custom-call(bf16[2,256]{1,0:T(2,128)(2,1)S(1)} %pad_maximum_fusion.refs_7_.refs_8_.gain_ref.refs_0_, bf16[128,3584]{1,0:T(8,128)(2,1)S(1)} %collective-permute-done.19.x_ref.refs_6_, ...), custom_call_target="tpu_custom_call" | custom-call | flops 939524096 | bytes 4194304 | tf_op jit(solution)/shard_map/second_block/pallas_call | solution.py:235
  46.5 2.0 %collective-permute-done.20.refs_4_.cot_ref = bf16[128,3584]{1,0:T(8,128)(2,1)S(1)} collective-permute-done((bf16[128,3584]{1,0:T(8,128)(2,1)S(1)}, bf16[128,3584]{1,0:T(8,128)(2,1)S(1)}, u32[]{:S(2)}, u32[]{:S(2)}) %collective-permute-start.20) | collective-permute-done | bytes 917536 | tf_op jit(solution)/shard_map/ppermute | solution.py:306
  48.5 1.8 %first_weight_grad.2 = (bf16[128,256]{1,0:T(8,128)(2,1)S(1)}, bf16[464,256]{1,0:T(8,128)(2,1)S(1)}, bf16[464,256]{1,0:T(8,128)(2,1)S(1)}, bf16[464,256]{1,0:T(8,...) custom-call(bf16[2,256]{1,0:T(2,128)(2,1)S(1)} %pad_maximum_fusion.r, ...), custom_call_target="tpu_custom_call" | custom-call | flops 939524096 | bytes 4194304 | tf_op jit(solution)/shard_map/first_weight_grad/pallas_call | solution.py:235
  51.6 3.0 %collective-permute-start.21 = (bf16[464,256]{1,0:T(8,128)(2,1)S(1)}, bf16[464,256]{1,0:T(8,128)(2,1)S(1)}, u32[]{:S(2)}, u32[]{:S(2)}) collective-permute-start(bf16[464,256]{1,0:T(8,128)(2,1)S(1)} %get-tuple-element.84), channel_id=1, source_target_pairs={{0,4},{1,5},{2,0},{3,1},{4,6},{5,7},{6,2},{7,3},{8,12},{9,13},{10,... | collective-permute-start | bytes 712712 | tf_op jit(solution)/shard_map/ppermute | solution.py:306
  54.6 2.0 %collective-permute-start.26 = (bf16[464,256]{1,0:T(8,128)(2,1)S(1)}, bf16[464,256]{1,0:T(8,128)(2,1)S(1)}, u32[]{:S(2)}, u32[]{:S(2)}) collective-permute-start(bf16[464,256]{1,0:T(8,128)(2,1)S(1)} %get-tuple-element.94), channel_id=1, source_target_pairs={{0,16},{1,17},{2,18},{3,19},{4,20},{5,21},{6,22},{7,23},{8,24},{9,... | collective-permute-start | bytes 712712 | tf_op jit(solution)/shard_map/ppermute | solution.py:306
  56.6 1.7 %first_weight_grad.3 = (bf16[128,256]{1,0:T(8,128)(2,1)S(1)}, bf16[464,256]{1,0:T(8,128)(2,1)S(1)}, bf16[464,256]{1,0:T(8,128)(2,1)S(1)}, bf16[464,256]{1,0:T(8,...) custom-call(bf16[2,256]{1,0:T(2,128)(2,1)S(1)} %pad_maximum_fusion.r, ...), custom_call_target="tpu_custom_call" | custom-call | flops 939524096 | bytes 4194304 | tf_op jit(solution)/shard_map/first_weight_grad/pallas_call | solution.py:235
  58.4 0.9 %collective-permute-start.23 = (bf16[464,256]{1,0:T(8,128)(2,1)S(1)}, bf16[464,256]{1,0:T(8,128)(2,1)S(1)}, u32[]{:S(2)}, u32[]{:S(2)}) collective-permute-start(bf16[464,256]{1,0:T(8,128)(2,1)S(1)} %get-tuple-element.85), channel_id=1, source_target_pairs={{0,16},{1,17},{2,18},{3,19},{4,20},{5,21},{6,22},{7,23},{8,24},{9,... | collective-permute-start | bytes 712712 | tf_op jit(solution)/shard_map/ppermute | solution.py:306
  59.3 1.3 %collective-permute-done.21.refs_1_ = bf16[464,256]{1,0:T(8,128)(2,1)S(1)} collective-permute-done((bf16[464,256]{1,0:T(8,128)(2,1)S(1)}, bf16[464,256]{1,0:T(8,128)(2,1)S(1)}, u32[]{:S(2)}, u32[]{:S(2)}) %collective-permute-start.21) | collective-permute-done | bytes 237600 | tf_op jit(solution)/shard_map/ppermute | solution.py:306
  60.6 1.5 %collective-permute-start.24 = (bf16[464,256]{1,0:T(8,128)(2,1)S(1)}, bf16[464,256]{1,0:T(8,128)(2,1)S(1)}, u32[]{:S(2)}, u32[]{:S(2)}) collective-permute-start(bf16[464,256]{1,0:T(8,128)(2,1)S(1)} %get-tuple-element.87), channel_id=1, source_target_pairs={{0,1},{1,0},{2,3},{3,2},{4,5},{5,4},{6,7},{7,6},{8,9},{9,8},{10,11... | collective-permute-start | bytes 712712 | tf_op jit(solution)/shard_map/ppermute | solution.py:306
  62.2 1.1 %collective-permute-done.26.refs_1_ = bf16[464,256]{1,0:T(8,128)(2,1)S(1)} collective-permute-done((bf16[464,256]{1,0:T(8,128)(2,1)S(1)}, bf16[464,256]{1,0:T(8,128)(2,1)S(1)}, u32[]{:S(2)}, u32[]{:S(2)}) %collective-permute-start.26) | collective-permute-done | bytes 237600 | tf_op jit(solution)/shard_map/ppermute | solution.py:306
  63.2 2.1 %collective-permute-start.22 = (bf16[464,256]{1,0:T(8,128)(2,1)S(1)}, bf16[464,256]{1,0:T(8,128)(2,1)S(1)}, u32[]{:S(2)}, u32[]{:S(2)}) collective-permute-start(bf16[464,256]{1,0:T(8,128)(2,1)S(1)} %partial_sum.7), channel_id=1, source_target_pairs={{0,4},{1,5},{2,0},{3,1},{4,6},{5,7},{6,2},{7,3},{8,12},{9,13},{10,... | collective-permute-start | bytes 712712 | tf_op jit(solution)/shard_map/ppermute | solution.py:306
  65.4 1.6 %collective-permute-done.28.refs_1_ = bf16[464,256]{1,0:T(8,128)(2,1)S(1)} collective-permute-done((bf16[464,256]{1,0:T(8,128)(2,1)S(1)}, bf16[464,256]{1,0:T(8,128)(2,1)S(1)}, u32[]{:S(2)}, u32[]{:S(2)}) %collective-permute-start.28) | collective-permute-done | bytes 237600 | tf_op jit(solution)/shard_map/ppermute | solution.py:306
  67.5 1.7 %collective-permute-start.29 = (bf16[464,256]{1,0:T(8,128)(2,1)S(1)}, bf16[464,256]{1,0:T(8,128)(2,1)S(1)}, u32[]{:S(2)}, u32[]{:S(2)}) collective-permute-start(bf16[464,256]{1,0:T(8,128)(2,1)S(1)} %get-tuple-element.98), channel_id=1, source_target_pairs={{0,16},{1,17},{2,18},{3,19},{4,20},{5,21},{6,22},{7,23},{8,24},{9,... | collective-permute-start | bytes 712712 | tf_op jit(solution)/shard_map/ppermute | solution.py:306
  69.4 0.9 %store.1 = bf16[128,3584]{1,0:T(8,128)(2,1)} custom-call(bf16[128,3584]{1,0:T(8,128)(2,1)S(1)} %collective-permute-done.25.value_ref), custom_call_target="tpu_custom_call" | custom-call | bytes 4194304 | tf_op jit(solution)/shard_map/store/pallas_call | solution.py:235
  70.3 1.9 %collective-permute-done.24.refs_1_ = bf16[464,256]{1,0:T(8,128)(2,1)S(1)} collective-permute-done((bf16[464,256]{1,0:T(8,128)(2,1)S(1)}, bf16[464,256]{1,0:T(8,128)(2,1)S(1)}, u32[]{:S(2)}, u32[]{:S(2)}) %collective-permute-start.24) | collective-permute-done | bytes 237600 | tf_op jit(solution)/shard_map/ppermute | solution.py:306
  72.2 1.9 %collective-permute-start.34 = (bf16[464,256]{1,0:T(8,128)(2,1)S(1)}, bf16[464,256]{1,0:T(8,128)(2,1)S(1)}, u32[]{:S(2)}, u32[]{:S(2)}) collective-permute-start(bf16[464,256]{1,0:T(8,128)(2,1)S(1)} %partial_sum.12), channel_id=1, source_target_pairs={{0,4},{1,5},{2,0},{3,1},{4,6},{5,7},{6,2},{7,3},{8,12},{9,13},{10,... | collective-permute-start | bytes 712712 | tf_op jit(solution)/shard_map/ppermute | solution.py:306
  74.1 1.6 %collective-permute-start.32 = (bf16[464,256]{1,0:T(8,128)(2,1)S(1)}, bf16[464,256]{1,0:T(8,128)(2,1)S(1)}, u32[]{:S(2)}, u32[]{:S(2)}) collective-permute-start(bf16[464,256]{1,0:T(8,128)(2,1)S(1)} %partial_sum.10), channel_id=1, source_target_pairs={{0,1},{1,0},{2,3},{3,2},{4,5},{5,4},{6,7},{7,6},{8,9},{9,8},{10,11... | collective-permute-start | bytes 712712 | tf_op jit(solution)/shard_map/ppermute | solution.py:306
  75.7 1.5 %collective-permute-done.27.refs_1_ = bf16[464,256]{1,0:T(8,128)(2,1)S(1)} collective-permute-done((bf16[464,256]{1,0:T(8,128)(2,1)S(1)}, bf16[464,256]{1,0:T(8,128)(2,1)S(1)}, u32[]{:S(2)}, u32[]{:S(2)}) %collective-permute-start.27) | collective-permute-done | bytes 237600 | tf_op jit(solution)/shard_map/ppermute | solution.py:306
  77.4 1.3 %collective-permute-start.30 = (bf16[464,256]{1,0:T(8,128)(2,1)S(1)}, bf16[464,256]{1,0:T(8,128)(2,1)S(1)}, u32[]{:S(2)}, u32[]{:S(2)}) collective-permute-start(bf16[464,256]{1,0:T(8,128)(2,1)S(1)} %partial_sum.9), channel_id=1, source_target_pairs={{0,2},{1,3},{2,6},{3,7},{4,0},{5,1},{6,4},{7,5},{8,10},{9,11},{10,... | collective-permute-start | bytes 712712 | tf_op jit(solution)/shard_map/ppermute | solution.py:306
  78.7 1.5 %first_input_grad_out.1 = bf16[128,3584]{1,0:T(8,128)(2,1)} custom-call(bf16[128,3584]{1,0:T(8,128)(2,1)S(1)} %collective-permute-done.18.refs_4_.cot_ref, f32[128,128]{1,0:T(8,128)S(1)} %get-tuple-element.86.refs_3_.p_ref, bf16[128,256]{1,0:T(8,128)(2,1)S(1)} %get-tuple-element.89.dc_ref, bf16[3584,256]{1,0:T(8,128)(2,1)S(1)} %get-tuple-element.64.w0_ref.w_ref), custom_call_target="tpu_custom_call" | custom-call | flops 469762048 | bytes 4194304 | tf_op jit(solution)/shard_map/first_input_grad_out/pallas_call | solution.py:235
  80.3 3.3 %collective-permute-start.36 = (bf16[464,256]{1,0:T(8,128)(2,1)S(1)}, bf16[464,256]{1,0:T(8,128)(2,1)S(1)}, u32[]{:S(2)}, u32[]{:S(2)}) collective-permute-start(bf16[464,256]{1,0:T(8,128)(2,1)S(1)} %partial_sum.13), channel_id=1, source_target_pairs={{0,4},{1,5},{2,0},{3,1},{4,6},{5,7},{6,2},{7,3},{8,12},{9,13},{10,... | collective-permute-start | bytes 712712 | tf_op jit(solution)/shard_map/ppermute | solution.py:306
  83.7 1.3 %collective-permute-start.33 = (bf16[464,256]{1,0:T(8,128)(2,1)S(1)}, bf16[464,256]{1,0:T(8,128)(2,1)S(1)}, u32[]{:S(2)}, u32[]{:S(2)}) collective-permute-start(bf16[464,256]{1,0:T(8,128)(2,1)S(1)} %partial_sum.11), channel_id=1, source_target_pairs={{0,16},{1,17},{2,18},{3,19},{4,20},{5,21},{6,22},{7,23},{8,24},{9,... | collective-permute-start | bytes 712712 | tf_op jit(solution)/shard_map/ppermute | solution.py:306
  85.0 0.9 %collective-permute-done.31.refs_2_ = bf16[464,256]{1,0:T(8,128)(2,1)S(1)} collective-permute-done((bf16[464,256]{1,0:T(8,128)(2,1)S(1)}, bf16[464,256]{1,0:T(8,128)(2,1)S(1)}, u32[]{:S(2)}, u32[]{:S(2)}) %collective-permute-start.31) | collective-permute-done | bytes 237600 | tf_op jit(solution)/shard_map/ppermute | solution.py:306
  86.0 1.7 %collective-permute-done.30.refs_1_ = bf16[464,256]{1,0:T(8,128)(2,1)S(1)} collective-permute-done((bf16[464,256]{1,0:T(8,128)(2,1)S(1)}, bf16[464,256]{1,0:T(8,128)(2,1)S(1)}, u32[]{:S(2)}, u32[]{:S(2)}) %collective-permute-start.30) | collective-permute-done | bytes 237600 | tf_op jit(solution)/shard_map/ppermute | solution.py:306
  87.7 2.4 %collective-permute-done.36.refs_4_ = bf16[464,256]{1,0:T(8,128)(2,1)S(1)} collective-permute-done((bf16[464,256]{1,0:T(8,128)(2,1)S(1)}, bf16[464,256]{1,0:T(8,128)(2,1)S(1)}, u32[]{:S(2)}, u32[]{:S(2)}) %collective-permute-start.36) | collective-permute-done | bytes 237600 | tf_op jit(solution)/shard_map/ppermute | solution.py:306
  90.1 0.9 %final_sum.1 = (f32[448,256]{1,0:T(8,128)}, f32[1,256]{1,0:T(1,128)}) custom-call(bf16[464,256]{1,0:T(8,128)(2,1)S(1)} %get-tuple-element.91.refs_0_, bf16[464,256]{1,0:T(8,128)(2,1)S(1)} %collective-permute-done.30.refs_1_, bf16[464,256]{1,0:T(8,128)(2,1)S(1)} %collective-permute-done.31.refs_2_, bf16[464,256]{1,0:T(8,128)(2,1)S(1)} %collective-permute-done.33.refs_3_, ...), custom_call_target="tpu_custom_call" | custom-call | bytes 4194304 | tf_op jit(solution)/shard_map/final_sum/pallas_call | solution.py:235
  (46 shorter events, 5.3 us)
Async XLA Ops:
  0.6 12.3 %collective-permute-start.7 = (bf16[128,3584]{1,0:T(8,128)(2,1)}, bf16[128,3584]{1,0:T(8,128)(2,1)S(1)}, u32[]{:S(2)}, u32[]{:S(2)}) collective-permute-start(bf16[128,3584]{1,0:T(8,128)(2,1)} %bitcast.15), channel_id=1, source_target_pairs={{0,8},{1,9},{2,10},{3,11},{4,12},{5,13},{6,14},{7,15},{8,0},{9,1},... | collective-permute-start | bytes 2752520 | tf_op jit(solution)/shard_map/ppermute | solution.py:306
  1.1 10.2 %collective-permute-start.1 = (bf16[448,256]{1,0:T(8,128)(2,1)}, bf16[448,256]{1,0:T(8,128)(2,1)S(1)}, u32[]{:S(2)}, u32[]{:S(2)}) collective-permute-start(bf16[448,256]{1,0:T(8,128)(2,1)} %bitcast.10), channel_id=1, source_target_pairs={{0,2},{1,3},{2,6},{3,7},{4,0},{5,1},{6,4},{7,5},{8,10},{9,11},{10,... | collective-permute-start | bytes 688136 | tf_op jit(solution)/shard_map/ppermute | solution.py:306
  3.8 9.1 %collective-permute-start.4 = (bf16[448,256]{1,0:T(8,128)(2,1)}, bf16[448,256]{1,0:T(8,128)(2,1)S(1)}, u32[]{:S(2)}, u32[]{:S(2)}) collective-permute-start(bf16[448,256]{1,0:T(8,128)(2,1)} %bitcast.11), channel_id=1, source_target_pairs={{0,1},{1,0},{2,3},{3,2},{4,5},{5,4},{6,7},{7,6},{8,9},{9,8},{10,11... | collective-permute-start | bytes 688136 | tf_op jit(solution)/shard_map/ppermute | solution.py:306
  5.3 3.8 %collective-permute-start = (bf16[1,256]{1,0:T(2,128)(2,1)}, bf16[1,256]{1,0:T(2,128)(2,1)S(1)}, u32[]{:S(2)}, u32[]{:S(2)}) collective-permute-start(bf16[1,256]{1,0:T(2,128)(2,1)} %param.7), channel_id=1, source_target_pairs={{0,16},{1,17},{2,18},{3,19},{4,20},{5,21},{6,22},{7,23},{8,24},{9,... | collective-permute-start | bytes 1544 | tf_op jit(solution)/shard_map/ppermute | solution.py:306
  6.8 9.3 %collective-permute-start.2 = (bf16[448,256]{1,0:T(8,128)(2,1)}, bf16[448,256]{1,0:T(8,128)(2,1)S(1)}, u32[]{:S(2)}, u32[]{:S(2)}) collective-permute-start(bf16[448,256]{1,0:T(8,128)(2,1)} %bitcast.12), channel_id=1, source_target_pairs={{0,4},{1,5},{2,0},{3,1},{4,6},{5,7},{6,2},{7,3},{8,12},{9,13},{10,... | collective-permute-start | bytes 688136 | tf_op jit(solution)/shard_map/ppermute | solution.py:306
  9.1 7.7 %collective-permute-start.3 = (bf16[448,256]{1,0:T(8,128)(2,1)}, bf16[448,256]{1,0:T(8,128)(2,1)S(1)}, u32[]{:S(2)}, u32[]{:S(2)}) collective-permute-start(bf16[448,256]{1,0:T(8,128)(2,1)} %bitcast.13), channel_id=1, source_target_pairs={{0,16},{1,17},{2,18},{3,19},{4,20},{5,21},{6,22},{7,23},{8,24},{9,... | collective-permute-start | bytes 688136 | tf_op jit(solution)/shard_map/ppermute | solution.py:306
  11.3 9.6 %collective-permute-start.6 = (bf16[448,256]{1,0:T(8,128)(2,1)S(1)}, bf16[448,256]{1,0:T(8,128)(2,1)S(1)}, u32[]{:S(2)}, u32[]{:S(2)}) collective-permute-start(bf16[448,256]{1,0:T(8,128)(2,1)S(1)} %collective-permute-done.1.refs_0_), channel_id=1, source_target_pairs={{0,1},{1,0},{2,3},{3,2},{4,5},{5,4},{6,7},{7,6},{8,9},{9,8},{10,11... | collective-permute-start | bytes 688136 | tf_op jit(solution)/shard_map/ppermute | solution.py:306
  12.9 8.0 %collective-permute-start.8 = (bf16[448,256]{1,0:T(8,128)(2,1)S(1)}, bf16[448,256]{1,0:T(8,128)(2,1)S(1)}, u32[]{:S(2)}, u32[]{:S(2)}) collective-permute-start(bf16[448,256]{1,0:T(8,128)(2,1)S(1)} %collective-permute-done.4.refs_3_), channel_id=1, source_target_pairs={{0,16},{1,17},{2,18},{3,19},{4,20},{5,21},{6,22},{7,23},{8,24},{9,... | collective-permute-start | bytes 688136 | tf_op jit(solution)/shard_map/ppermute | solution.py:306
  16.8 9.2 %collective-permute-start.5 = (bf16[448,256]{1,0:T(8,128)(2,1)S(1)}, bf16[448,256]{1,0:T(8,128)(2,1)S(1)}, u32[]{:S(2)}, u32[]{:S(2)}) collective-permute-start(bf16[448,256]{1,0:T(8,128)(2,1)S(1)} %collective-permute-done.2.refs_2_), channel_id=1, source_target_pairs={{0,4},{1,5},{2,0},{3,1},{4,6},{5,7},{6,2},{7,3},{8,12},{9,13},{10,... | collective-permute-start | bytes 688136 | tf_op jit(solution)/shard_map/ppermute | solution.py:306
  17.9 9.6 %collective-permute-start.10 = (bf16[448,256]{1,0:T(8,128)(2,1)S(1)}, bf16[448,256]{1,0:T(8,128)(2,1)S(1)}, u32[]{:S(2)}, u32[]{:S(2)}) collective-permute-start(bf16[448,256]{1,0:T(8,128)(2,1)S(1)} %collective-permute-done.2.refs_2_), channel_id=1, source_target_pairs={{0,1},{1,0},{2,3},{3,2},{4,5},{5,4},{6,7},{7,6},{8,9},{9,8},{10,11... | collective-permute-start | bytes 688136 | tf_op jit(solution)/shard_map/ppermute | solution.py:306
  19.4 8.1 %collective-permute-start.13 = (bf16[448,256]{1,0:T(8,128)(2,1)S(1)}, bf16[448,256]{1,0:T(8,128)(2,1)S(1)}, u32[]{:S(2)}, u32[]{:S(2)}) collective-permute-start(bf16[448,256]{1,0:T(8,128)(2,1)S(1)} %collective-permute-done.1.refs_0_), channel_id=1, source_target_pairs={{0,16},{1,17},{2,18},{3,19},{4,20},{5,21},{6,22},{7,23},{8,24},{9,... | collective-permute-start | bytes 688136 | tf_op jit(solution)/shard_map/ppermute | solution.py:306
  20.9 10.3 %collective-permute-start.16 = (bf16[448,256]{1,0:T(8,128)(2,1)S(1)}, bf16[448,256]{1,0:T(8,128)(2,1)S(1)}, u32[]{:S(2)}, u32[]{:S(2)}) collective-permute-start(bf16[448,256]{1,0:T(8,128)(2,1)S(1)} %collective-permute-done.8.refs_4_), channel_id=1, source_target_pairs={{0,4},{1,5},{2,0},{3,1},{4,6},{5,7},{6,2},{7,3},{8,12},{9,13},{10,... | collective-permute-start | bytes 688136 | tf_op jit(solution)/shard_map/ppermute | solution.py:306
  24.4 10.1 %collective-permute-start.11 = (bf16[448,256]{1,0:T(8,128)(2,1)S(1)}, bf16[448,256]{1,0:T(8,128)(2,1)S(1)}, u32[]{:S(2)}, u32[]{:S(2)}) collective-permute-start(bf16[448,256]{1,0:T(8,128)(2,1)S(1)} %collective-permute-done.2.refs_2_), channel_id=1, source_target_pairs={{0,16},{1,17},{2,18},{3,19},{4,20},{5,21},{6,22},{7,23},{8,24},{9,... | collective-permute-start | bytes 688136 | tf_op jit(solution)/shard_map/ppermute | solution.py:306
  26.0 8.6 %collective-permute-start.9 = (bf16[448,256]{1,0:T(8,128)(2,1)S(1)}, bf16[448,256]{1,0:T(8,128)(2,1)S(1)}, u32[]{:S(2)}, u32[]{:S(2)}) collective-permute-start(bf16[448,256]{1,0:T(8,128)(2,1)S(1)} %collective-permute-done.5.refs_1_), channel_id=1, source_target_pairs={{0,1},{1,0},{2,3},{3,2},{4,5},{5,4},{6,7},{7,6},{8,9},{9,8},{10,11... | collective-permute-start | bytes 688136 | tf_op jit(solution)/shard_map/ppermute | solution.py:306
  27.5 10.1 %collective-permute-start.14 = (bf16[448,256]{1,0:T(8,128)(2,1)S(1)}, bf16[448,256]{1,0:T(8,128)(2,1)S(1)}, u32[]{:S(2)}, u32[]{:S(2)}) collective-permute-start(bf16[448,256]{1,0:T(8,128)(2,1)S(1)} %collective-permute-done.5.refs_1_), channel_id=1, source_target_pairs={{0,16},{1,17},{2,18},{3,19},{4,20},{5,21},{6,22},{7,23},{8,24},{9,... | collective-permute-start | bytes 688136 | tf_op jit(solution)/shard_map/ppermute | solution.py:306
  28.3 9.3 %collective-permute-start.15 = (bf16[448,256]{1,0:T(8,128)(2,1)S(1)}, bf16[448,256]{1,0:T(8,128)(2,1)S(1)}, u32[]{:S(2)}, u32[]{:S(2)}) collective-permute-start(bf16[448,256]{1,0:T(8,128)(2,1)S(1)} %collective-permute-done.13.refs_1_), channel_id=1, source_target_pairs={{0,1},{1,0},{2,3},{3,2},{4,5},{5,4},{6,7},{7,6},{8,9},{9,8},{10,11... | collective-permute-start | bytes 688136 | tf_op jit(solution)/shard_map/ppermute | solution.py:306
  31.2 7.3 %collective-permute-start.17 = (bf16[448,256]{1,0:T(8,128)(2,1)S(1)}, bf16[448,256]{1,0:T(8,128)(2,1)S(1)}, u32[]{:S(2)}, u32[]{:S(2)}) collective-permute-start(bf16[448,256]{1,0:T(8,128)(2,1)S(1)} %collective-permute-done.16.refs_7_), channel_id=1, source_target_pairs={{0,4},{1,5},{2,0},{3,1},{4,6},{5,7},{6,2},{7,3},{8,12},{9,13},{10,... | collective-permute-start | bytes 688136 | tf_op jit(solution)/shard_map/ppermute | solution.py:306
  37.5 2.8 %collective-permute-start.12 = (bf16[128,3584]{1,0:T(8,128)(2,1)S(1)}, bf16[128,3584]{1,0:T(8,128)(2,1)S(1)}, u32[]{:S(2)}, u32[]{:S(2)}) collective-permute-start(bf16[128,3584]{1,0:T(8,128)(2,1)S(1)} %get-tuple-element.63), channel_id=1, source_target_pairs={{0,8},{1,9},{2,10},{3,11},{4,12},{5,13},{6,14},{7,15},{8,0},{9,1},... | collective-permute-start | bytes 2752520 | tf_op jit(solution)/shard_map/ppermute | solution.py:306
  40.2 2.9 %collective-permute-start.19 = (bf16[128,3584]{1,0:T(8,128)(2,1)S(1)}, bf16[128,3584]{1,0:T(8,128)(2,1)S(1)}, u32[]{:S(2)}, u32[]{:S(2)}) collective-permute-start(bf16[128,3584]{1,0:T(8,128)(2,1)S(1)} %get-tuple-element.78), channel_id=1, source_target_pairs={{0,8},{1,9},{2,10},{3,11},{4,12},{5,13},{6,14},{7,15},{8,0},{9,1},... | collective-permute-start | bytes 2752520 | tf_op jit(solution)/shard_map/ppermute | solution.py:306
  45.9 2.6 %collective-permute-start.20 = (bf16[128,3584]{1,0:T(8,128)(2,1)S(1)}, bf16[128,3584]{1,0:T(8,128)(2,1)S(1)}, u32[]{:S(2)}, u32[]{:S(2)}) collective-permute-start(bf16[128,3584]{1,0:T(8,128)(2,1)S(1)} %get-tuple-element.79), channel_id=1, source_target_pairs={{0,8},{1,9},{2,10},{3,11},{4,12},{5,13},{6,14},{7,15},{8,0},{9,1},... | collective-permute-start | bytes 2752520 | tf_op jit(solution)/shard_map/ppermute | solution.py:306
  46.4 10.2 %collective-permute-start.18 = (bf16[128,3584]{1,0:T(8,128)(2,1)S(1)}, bf16[128,3584]{1,0:T(8,128)(2,1)S(1)}, u32[]{:S(2)}, u32[]{:S(2)}) collective-permute-start(bf16[128,3584]{1,0:T(8,128)(2,1)S(1)} %get-tuple-element.73), channel_id=1, source_target_pairs={{0,8},{1,9},{2,10},{3,11},{4,12},{5,13},{6,14},{7,15},{8,0},{9,1},... | collective-permute-start | bytes 2752520 | tf_op jit(solution)/shard_map/ppermute | solution.py:306
  50.4 6.3 %copy-start = (bf16[1,1,128,3584]{3,2,1,0:T(8,128)(2,1)S(1)}, bf16[1,1,128,3584]{3,2,1,0:T(8,128)(2,1)}, u32[]{:S(2)}) copy-start(bf16[1,1,128,3584]{3,2,1,0:T(8,128)(2,1)} %param.4) | copy-start | bytes 2752516
  51.1 18.2 %collective-permute-start.25 = (bf16[128,3584]{1,0:T(8,128)(2,1)S(1)}, bf16[128,3584]{1,0:T(8,128)(2,1)S(1)}, u32[]{:S(2)}, u32[]{:S(2)}) collective-permute-start(bf16[128,3584]{1,0:T(8,128)(2,1)S(1)} %first_input_grad.1), channel_id=1, source_target_pairs={{0,8},{1,9},{2,10},{3,11},{4,12},{5,13},{6,14},{7,15},{8,0},{9,1},... | collective-permute-start | bytes 2752520 | tf_op jit(solution)/shard_map/ppermute | solution.py:306
  51.6 9.0 %collective-permute-start.21 = (bf16[464,256]{1,0:T(8,128)(2,1)S(1)}, bf16[464,256]{1,0:T(8,128)(2,1)S(1)}, u32[]{:S(2)}, u32[]{:S(2)}) collective-permute-start(bf16[464,256]{1,0:T(8,128)(2,1)S(1)} %get-tuple-element.84), channel_id=1, source_target_pairs={{0,4},{1,5},{2,0},{3,1},{4,6},{5,7},{6,2},{7,3},{8,12},{9,13},{10,... | collective-permute-start | bytes 712712 | tf_op jit(solution)/shard_map/ppermute | solution.py:306
  54.6 8.6 %collective-permute-start.26 = (bf16[464,256]{1,0:T(8,128)(2,1)S(1)}, bf16[464,256]{1,0:T(8,128)(2,1)S(1)}, u32[]{:S(2)}, u32[]{:S(2)}) collective-permute-start(bf16[464,256]{1,0:T(8,128)(2,1)S(1)} %get-tuple-element.94), channel_id=1, source_target_pairs={{0,16},{1,17},{2,18},{3,19},{4,20},{5,21},{6,22},{7,23},{8,24},{9,... | collective-permute-start | bytes 712712 | tf_op jit(solution)/shard_map/ppermute | solution.py:306
  58.3 8.8 %collective-permute-start.28 = (bf16[464,256]{1,0:T(8,128)(2,1)S(1)}, bf16[464,256]{1,0:T(8,128)(2,1)S(1)}, u32[]{:S(2)}, u32[]{:S(2)}) collective-permute-start(bf16[464,256]{1,0:T(8,128)(2,1)S(1)} %get-tuple-element.97), channel_id=1, source_target_pairs={{0,1},{1,0},{2,3},{3,2},{4,5},{5,4},{6,7},{7,6},{8,9},{9,8},{10,11... | collective-permute-start | bytes 712712 | tf_op jit(solution)/shard_map/ppermute | solution.py:306
  58.4 9.1 %collective-permute-start.23 = (bf16[464,256]{1,0:T(8,128)(2,1)S(1)}, bf16[464,256]{1,0:T(8,128)(2,1)S(1)}, u32[]{:S(2)}, u32[]{:S(2)}) collective-permute-start(bf16[464,256]{1,0:T(8,128)(2,1)S(1)} %get-tuple-element.85), channel_id=1, source_target_pairs={{0,16},{1,17},{2,18},{3,19},{4,20},{5,21},{6,22},{7,23},{8,24},{9,... | collective-permute-start | bytes 712712 | tf_op jit(solution)/shard_map/ppermute | solution.py:306
  60.6 11.6 %collective-permute-start.24 = (bf16[464,256]{1,0:T(8,128)(2,1)S(1)}, bf16[464,256]{1,0:T(8,128)(2,1)S(1)}, u32[]{:S(2)}, u32[]{:S(2)}) collective-permute-start(bf16[464,256]{1,0:T(8,128)(2,1)S(1)} %get-tuple-element.87), channel_id=1, source_target_pairs={{0,1},{1,0},{2,3},{3,2},{4,5},{5,4},{6,7},{7,6},{8,9},{9,8},{10,11... | collective-permute-start | bytes 712712 | tf_op jit(solution)/shard_map/ppermute | solution.py:306
  63.2 10.8 %collective-permute-start.22 = (bf16[464,256]{1,0:T(8,128)(2,1)S(1)}, bf16[464,256]{1,0:T(8,128)(2,1)S(1)}, u32[]{:S(2)}, u32[]{:S(2)}) collective-permute-start(bf16[464,256]{1,0:T(8,128)(2,1)S(1)} %partial_sum.7), channel_id=1, source_target_pairs={{0,4},{1,5},{2,0},{3,1},{4,6},{5,7},{6,2},{7,3},{8,12},{9,13},{10,... | collective-permute-start | bytes 712712 | tf_op jit(solution)/shard_map/ppermute | solution.py:306
  67.1 10.2 %collective-permute-start.27 = (bf16[464,256]{1,0:T(8,128)(2,1)S(1)}, bf16[464,256]{1,0:T(8,128)(2,1)S(1)}, u32[]{:S(2)}, u32[]{:S(2)}) collective-permute-start(bf16[464,256]{1,0:T(8,128)(2,1)S(1)} %partial_sum.8), channel_id=1, source_target_pairs={{0,1},{1,0},{2,3},{3,2},{4,5},{5,4},{6,7},{7,6},{8,9},{9,8},{10,11... | collective-permute-start | bytes 712712 | tf_op jit(solution)/shard_map/ppermute | solution.py:306
  67.5 9.7 %collective-permute-start.29 = (bf16[464,256]{1,0:T(8,128)(2,1)S(1)}, bf16[464,256]{1,0:T(8,128)(2,1)S(1)}, u32[]{:S(2)}, u32[]{:S(2)}) collective-permute-start(bf16[464,256]{1,0:T(8,128)(2,1)S(1)} %get-tuple-element.98), channel_id=1, source_target_pairs={{0,16},{1,17},{2,18},{3,19},{4,20},{5,21},{6,22},{7,23},{8,24},{9,... | collective-permute-start | bytes 712712 | tf_op jit(solution)/shard_map/ppermute | solution.py:306
  72.2 8.0 %collective-permute-start.35 = (bf16[464,256]{1,0:T(8,128)(2,1)S(1)}, bf16[464,256]{1,0:T(8,128)(2,1)S(1)}, u32[]{:S(2)}, u32[]{:S(2)}) collective-permute-start(bf16[464,256]{1,0:T(8,128)(2,1)S(1)} %get-tuple-element.110), channel_id=1, source_target_pairs={{0,16},{1,17},{2,18},{3,19},{4,20},{5,21},{6,22},{7,23},{8,24},{9,... | collective-permute-start | bytes 712712 | tf_op jit(solution)/shard_map/ppermute | solution.py:306
  72.2 8.0 %collective-permute-start.34 = (bf16[464,256]{1,0:T(8,128)(2,1)S(1)}, bf16[464,256]{1,0:T(8,128)(2,1)S(1)}, u32[]{:S(2)}, u32[]{:S(2)}) collective-permute-start(bf16[464,256]{1,0:T(8,128)(2,1)S(1)} %partial_sum.12), channel_id=1, source_target_pairs={{0,4},{1,5},{2,0},{3,1},{4,6},{5,7},{6,2},{7,3},{8,12},{9,13},{10,... | collective-permute-start | bytes 712712 | tf_op jit(solution)/shard_map/ppermute | solution.py:306
  74.1 9.5 %collective-permute-start.32 = (bf16[464,256]{1,0:T(8,128)(2,1)S(1)}, bf16[464,256]{1,0:T(8,128)(2,1)S(1)}, u32[]{:S(2)}, u32[]{:S(2)}) collective-permute-start(bf16[464,256]{1,0:T(8,128)(2,1)S(1)} %partial_sum.10), channel_id=1, source_target_pairs={{0,1},{1,0},{2,3},{3,2},{4,5},{5,4},{6,7},{7,6},{8,9},{9,8},{10,11... | collective-permute-start | bytes 712712 | tf_op jit(solution)/shard_map/ppermute | solution.py:306
  77.3 8.7 %collective-permute-start.31 = (bf16[464,256]{1,0:T(8,128)(2,1)S(1)}, bf16[464,256]{1,0:T(8,128)(2,1)S(1)}, u32[]{:S(2)}, u32[]{:S(2)}) collective-permute-start(bf16[464,256]{1,0:T(8,128)(2,1)S(1)} %get-tuple-element.101), channel_id=1, source_target_pairs={{0,1},{1,0},{2,3},{3,2},{4,5},{5,4},{6,7},{7,6},{8,9},{9,8},{10,11... | collective-permute-start | bytes 712712 | tf_op jit(solution)/shard_map/ppermute | solution.py:306
  77.4 10.3 %collective-permute-start.30 = (bf16[464,256]{1,0:T(8,128)(2,1)S(1)}, bf16[464,256]{1,0:T(8,128)(2,1)S(1)}, u32[]{:S(2)}, u32[]{:S(2)}) collective-permute-start(bf16[464,256]{1,0:T(8,128)(2,1)S(1)} %partial_sum.9), channel_id=1, source_target_pairs={{0,2},{1,3},{2,6},{3,7},{4,0},{5,1},{6,4},{7,5},{8,10},{9,11},{10,... | collective-permute-start | bytes 712712 | tf_op jit(solution)/shard_map/ppermute | solution.py:306
  80.3 9.7 %collective-permute-start.36 = (bf16[464,256]{1,0:T(8,128)(2,1)S(1)}, bf16[464,256]{1,0:T(8,128)(2,1)S(1)}, u32[]{:S(2)}, u32[]{:S(2)}) collective-permute-start(bf16[464,256]{1,0:T(8,128)(2,1)S(1)} %partial_sum.13), channel_id=1, source_target_pairs={{0,4},{1,5},{2,0},{3,1},{4,6},{5,7},{6,2},{7,3},{8,12},{9,13},{10,... | collective-permute-start | bytes 712712 | tf_op jit(solution)/shard_map/ppermute | solution.py:306
  83.7 6.4 %collective-permute-start.33 = (bf16[464,256]{1,0:T(8,128)(2,1)S(1)}, bf16[464,256]{1,0:T(8,128)(2,1)S(1)}, u32[]{:S(2)}, u32[]{:S(2)}) collective-permute-start(bf16[464,256]{1,0:T(8,128)(2,1)S(1)} %partial_sum.11), channel_id=1, source_target_pairs={{0,16},{1,17},{2,18},{3,19},{4,20},{5,21},{6,22},{7,23},{8,24},{9,... | collective-permute-start | bytes 712712 | tf_op jit(solution)/shard_map/ppermute | solution.py:306
